TPU v7x, 32 devices: a whole 2x2x4 slice. The times are simulated.
32 devices in a mesh: section: 2 (over y), dp: 4 (over z), head: 4 (over x, core).
Axes of the slice: x: 2, y: 2, z: 4, core: 2. Of those that a mesh axis runs over, the one named last changes fastest.
Arguments:
- block_input: bfloat16 [8192, 512], P('dp'), may hold values from -6 to 6
- cotangent: float32 [8192, 512], P('dp'), may hold values from -6 to 6
- segment_start: int32 [8192], P('dp'), may hold values 0 or 1
- pad_mask: int32 [8192], P('dp'), may hold values 0 or 1
- qkv_weight: bfloat16 [2, 3, 512, 512], P('section', None, None, 'head'), may hold values from -0.25 to 0.25
- out_weight: bfloat16 [2, 512, 512], P('section', 'head'), may hold values from -1 to 1
- up_weight: bfloat16 [2, 512, 2048], P('section', None, 'head'), may hold values from -0.25 to 0.25
- down_weight: bfloat16 [2, 512, 2048], P('section', None, 'head'), may hold values from -0.125 to 0.125
- norm_gain: float32 [2, 2, 512], P('section'), may hold values from 0.5 to 1.5
- norm_bias: float32 [2, 2, 512], P('section'), may hold values from -3 to 3
Outputs:
- activations: float32 [2, 8192, 512], P('section', 'dp')
- input_grad: float32 [2, 8192, 512], P('section', 'dp')
- token_rms: float32 [2, 8192], P('section', 'dp')
- qkv_grad: float32 [2, 3, 512, 512], P('section', None, None, 'head')
- out_grad: float32 [2, 512, 512], P('section', 'head')
- up_grad: float32 [2, 512, 2048], P('section', None, 'head')
- down_grad: float32 [2, 512, 2048], P('section', None, 'head')
- gain_grad: float32 [2, 2, 512], P('section')
- bias_grad: float32 [2, 2, 512], P('section')
All inputs are finite; a program needn't handle non-finite values. No bound on the sum of `segment_start` or of `pad_mask` on one device may be relied on, other than what follows from the above.
Results may differ from a plain program's by a relative error of at most 0.019.
Values may be sent and summed in bfloat16 or wider, within the bound.
No kernel may reach another device: no remote copies, remote signals or barrier semaphores. Data moves between devices by JAX's collectives and lax.ppermute only.
A program may use at most 192 MiB of HBM per device.

v0:
```python
import jax
import jax.numpy as jnp
from jax import lax
from jax.sharding import PartitionSpec as P

E = 64
NMB = 4
SEQ = 1024
MB_LEN = 256


EPS = 1e-05
HIGHEST = lax.Precision.HIGHEST


def shifted_2(block, axis, distance):
    devices = range(lax.axis_size(axis))
    route = [(i - distance, i) for i in devices if i - distance in devices]
    return lax.ppermute(block, axis, route)


def layer_norm(values_in, gain_vec, bias_vec):
    centre = jnp.mean(values_in, axis=-1, keepdims=True)
    shifted = values_in - centre
    spread = jnp.mean(shifted * shifted, axis=-1, keepdims=True)
    return shifted * lax.rsqrt(spread + EPS) * gain_vec + bias_vec


def feature_map(values_in):
    return jax.nn.elu(values_in) + 1.0


def to_heads(flat_rows, row_count):
    return flat_rows.reshape(row_count, -1, flat_rows.shape[1] // E, E).transpose(0, 2, 1, 3)


def from_heads(head_major):
    row_count, head_count, span_len, head_size = head_major.shape
    return head_major.transpose(0, 2, 1, 3).reshape(row_count * span_len, head_count * head_size)


def block_of(source, block_index):
    return lax.dynamic_index_in_dim(source, block_index, axis=1, keepdims=False)


def write_block(buffer, block_index, new_value, is_valid, axis_num):
    old_value = lax.dynamic_index_in_dim(buffer, block_index, axis=axis_num, keepdims=False)
    return lax.dynamic_update_index_in_dim(
        buffer, jnp.where(is_valid, new_value, old_value), block_index, axis_num
    )


def core_forward(query_feat, key_feat, value_feat, segment_ids, carry_in):
    state_mat, state_sum, last_id = carry_in
    positions = jnp.arange(segment_ids.shape[1])
    causal = positions[:, None] >= positions[None, :]
    same_seg = ((segment_ids[:, :, None] == segment_ids[:, None, :]) & causal[None]).astype(
        jnp.float32
    )[:, None]
    scores = (
        jnp.einsum("bhte,bhse->bhts", query_feat, key_feat, preferred_element_type=jnp.float32)
        * same_seg
    )
    carried = (segment_ids == last_id[:, None]).astype(jnp.float32)[:, None, :, None]
    query_wide = query_feat.astype(jnp.float32)
    numerator = jnp.einsum(
        "bhts,bhse->bhte",
        scores.astype(jnp.bfloat16),
        value_feat,
        preferred_element_type=jnp.float32,
    ) + carried * jnp.einsum("bhte,bhef->bhtf", query_wide, state_mat, precision=HIGHEST)
    denominator = (
        jnp.sum(scores, axis=-1, keepdims=True)
        + carried * jnp.einsum("bhte,bhe->bht", query_wide, state_sum, precision=HIGHEST)[..., None]
        + 1.0
    )
    new_last = segment_ids[:, -1]
    keep_flag = (new_last == last_id).astype(jnp.float32)
    tail_mask = (segment_ids == new_last[:, None]).astype(jnp.float32)[:, None, :, None]
    masked_keys = key_feat * tail_mask.astype(jnp.bfloat16)
    new_mat = keep_flag[:, None, None, None] * state_mat + jnp.einsum(
        "bhse,bhsf->bhef", masked_keys, value_feat, preferred_element_type=jnp.float32
    )
    new_sum = keep_flag[:, None, None] * state_sum + jnp.sum(
        masked_keys.astype(jnp.float32), axis=2
    )
    saved_parts = (same_seg, scores, carried, numerator, denominator, tail_mask, keep_flag)
    return (numerator / denominator, (new_mat, new_sum, new_last), saved_parts)


def core_backward(query_feat, key_feat, value_feat, carry_in, saved_parts, grad_heads, grad_carry):
    state_mat, state_sum, last_id = carry_in
    same_seg, scores, carried, numerator, denominator, tail_mask, keep_flag = saved_parts
    grad_mat, grad_sum = grad_carry
    grad_numer = (grad_heads / denominator).astype(jnp.bfloat16)
    grad_denom = -jnp.sum(grad_heads * numerator, axis=-1, keepdims=True) / (
        denominator * denominator
    )
    numer_wide = grad_numer.astype(jnp.float32)
    query_wide = query_feat.astype(jnp.float32)
    grad_scores = (
        jnp.einsum("bhte,bhse->bhts", grad_numer, value_feat, preferred_element_type=jnp.float32)
        + grad_denom
    )
    grad_scores = (grad_scores * same_seg).astype(jnp.bfloat16)
    grad_values = jnp.einsum(
        "bhts,bhte->bhse",
        scores.astype(jnp.bfloat16),
        grad_numer,
        preferred_element_type=jnp.float32,
    )
    grad_query = jnp.einsum(
        "bhts,bhse->bhte", grad_scores, key_feat, preferred_element_type=jnp.float32
    ) + carried * (
        jnp.einsum("bhtf,bhef->bhte", numer_wide, state_mat, precision=HIGHEST)
        + grad_denom * state_sum[:, :, None, :]
    )
    grad_keys = jnp.einsum(
        "bhts,bhte->bhse", grad_scores, query_feat, preferred_element_type=jnp.float32
    )
    start_mat = (
        jnp.einsum("bhte,bhtf->bhef", query_wide, carried * numer_wide, precision=HIGHEST)
        + keep_flag[:, None, None, None] * grad_mat
    )
    start_sum = (
        jnp.sum(carried * grad_denom * query_wide, axis=2) + keep_flag[:, None, None] * grad_sum
    )
    values_wide = value_feat.astype(jnp.float32)
    keys_wide = (key_feat * tail_mask.astype(jnp.bfloat16)).astype(jnp.float32)
    grad_keys = grad_keys + tail_mask * (
        jnp.einsum("bhsf,bhef->bhse", values_wide, grad_mat, precision=HIGHEST)
        + grad_sum[:, :, None, :]
    )
    grad_values = grad_values + jnp.einsum(
        "bhse,bhef->bhsf", keys_wide, grad_mat, precision=HIGHEST
    )
    return (grad_query, grad_keys, grad_values, (start_mat, start_sum))


def weight_grads(deferred):
    normed, grad_proj, mixed_heads, grad_attn, ffn_normed, grad_up_proj, ffn_grad, active = deferred
    grad_qkv = jnp.einsum("td,ctj->cdj", normed, grad_proj, preferred_element_type=jnp.float32)
    grad_out_w = jnp.einsum("tj,td->jd", mixed_heads, grad_attn, preferred_element_type=jnp.float32)
    grad_up = jnp.einsum("td,tj->dj", ffn_normed, grad_up_proj, preferred_element_type=jnp.float32)
    grad_down = jnp.einsum("td,tj->dj", ffn_grad, active, preferred_element_type=jnp.float32)
    return (grad_qkv, grad_out_w, grad_up, grad_down)


def add_masked(running, addition, is_valid):
    return jax.tree.map(
        lambda left, right: jnp.where(is_valid, left + right, left), running, addition
    )


def layer_forward(hidden_in, params, segment_ids, pad_keys, carry_in):
    qkv_w, out_w, up_w, down_w, gains, biases = params
    row_count = segment_ids.shape[0]
    normed = layer_norm(hidden_in, gains[0], biases[0]).astype(jnp.bfloat16)
    projected = jnp.einsum("td,cdj->ctj", normed, qkv_w, preferred_element_type=jnp.float32)
    query_feat = feature_map(projected[0]).astype(jnp.bfloat16)
    key_feat = (feature_map(projected[1]) * pad_keys[:, None]).astype(jnp.bfloat16)
    value_feat = projected[2].astype(jnp.bfloat16)
    head_out, carry_out, saved_parts = core_forward(
        to_heads(query_feat, row_count),
        to_heads(key_feat, row_count),
        to_heads(value_feat, row_count),
        segment_ids,
        carry_in,
    )
    mixed_heads = from_heads(head_out).astype(jnp.bfloat16)
    branch = lax.psum(
        jnp.dot(mixed_heads, out_w, preferred_element_type=jnp.float32).astype(jnp.bfloat16), "head"
    ).astype(jnp.float32)
    middle = hidden_in + branch
    normed_two = layer_norm(middle, gains[1], biases[1]).astype(jnp.bfloat16)
    up_proj = jnp.dot(normed_two, up_w, preferred_element_type=jnp.float32)
    active = jax.nn.gelu(up_proj).astype(jnp.bfloat16)
    ffn_out = lax.psum(
        jnp.einsum("tj,dj->td", active, down_w, preferred_element_type=jnp.float32).astype(
            jnp.bfloat16
        ),
        "head",
    ).astype(jnp.float32)
    return (middle + ffn_out, middle, carry_out)


def layer_backward(
    grad_out, hidden_in, middle, params, segment_ids, pad_keys, carry_in, grad_carry
):
    qkv_w, out_w, up_w, down_w, gains, biases = params
    row_count = segment_ids.shape[0]
    normed_two_wide, norm_two_pull = jax.vjp(layer_norm, middle, gains[1], biases[1])
    normed_two = normed_two_wide.astype(jnp.bfloat16)
    grad_branch = grad_out.astype(jnp.bfloat16)
    up_proj = jnp.dot(normed_two, up_w, preferred_element_type=jnp.float32)
    active_wide, gelu_pull = jax.vjp(jax.nn.gelu, up_proj)
    active = active_wide.astype(jnp.bfloat16)
    grad_active = jnp.dot(grad_branch, down_w, preferred_element_type=jnp.float32)
    grad_up_proj = gelu_pull(grad_active)[0].astype(jnp.bfloat16)
    grad_normed_two = lax.psum(
        jnp.einsum("tj,dj->td", grad_up_proj, up_w, preferred_element_type=jnp.float32).astype(
            jnp.bfloat16
        ),
        "head",
    ).astype(jnp.float32)
    grad_mid_norm, gain_two, bias_two = norm_two_pull(grad_normed_two)
    grad_middle = grad_out + grad_mid_norm
    normed_wide, norm_one_pull = jax.vjp(layer_norm, hidden_in, gains[0], biases[0])
    normed = normed_wide.astype(jnp.bfloat16)
    projected = jnp.einsum("td,cdj->ctj", normed, qkv_w, preferred_element_type=jnp.float32)
    query_wide, query_pull = jax.vjp(feature_map, projected[0])
    key_wide, key_pull = jax.vjp(feature_map, projected[1])
    query_feat = query_wide.astype(jnp.bfloat16)
    key_feat = (key_wide * pad_keys[:, None]).astype(jnp.bfloat16)
    value_feat = projected[2].astype(jnp.bfloat16)
    query_heads = to_heads(query_feat, row_count)
    key_heads = to_heads(key_feat, row_count)
    value_heads = to_heads(value_feat, row_count)
    head_out, carry_unused, saved_parts = core_forward(
        query_heads, key_heads, value_heads, segment_ids, carry_in
    )
    mixed_heads = from_heads(head_out).astype(jnp.bfloat16)
    grad_attn = grad_middle.astype(jnp.bfloat16)
    grad_mixed = jnp.einsum("td,jd->tj", grad_attn, out_w, preferred_element_type=jnp.float32)
    grad_query, grad_keys, grad_values, grad_start = core_backward(
        query_heads,
        key_heads,
        value_heads,
        carry_in,
        saved_parts,
        to_heads(grad_mixed, row_count),
        grad_carry,
    )
    proj_query = query_pull(from_heads(grad_query))[0].astype(jnp.bfloat16)
    proj_keys = key_pull(from_heads(grad_keys) * pad_keys[:, None])[0].astype(jnp.bfloat16)
    proj_values = from_heads(grad_values).astype(jnp.bfloat16)
    grad_proj = jnp.stack([proj_query, proj_keys, proj_values])
    grad_normed = lax.psum(
        jnp.einsum("ctj,cdj->td", grad_proj, qkv_w, preferred_element_type=jnp.float32).astype(
            jnp.bfloat16
        ),
        "head",
    ).astype(jnp.float32)
    grad_in_norm, gain_one, bias_one = norm_one_pull(grad_normed)
    norm_parts = (jnp.stack([gain_one, gain_two]), jnp.stack([bias_one, bias_two]))
    deferred = (
        normed,
        grad_proj,
        mixed_heads,
        grad_attn,
        normed_two,
        grad_up_proj,
        grad_branch,
        active,
    )
    return (grad_middle + grad_in_norm, grad_start, norm_parts, deferred)


def local(
    block_input,
    cotangent,
    segment_start,
    pad_mask,
    qkv_weight,
    out_weight,
    up_weight,
    down_weight,
    norm_gain,
    norm_bias,
):
    section_num = lax.axis_index("section")
    row_count = block_input.shape[0] // SEQ
    block_rows = row_count * MB_LEN
    width = block_input.shape[1]
    heads_local = qkv_weight.shape[-1] // E
    params = (
        qkv_weight[0],
        out_weight[0],
        up_weight[0],
        down_weight[0],
        norm_gain[0],
        norm_bias[0],
    )
    segment_ids = jnp.cumsum(segment_start.reshape(row_count, SEQ), axis=1).reshape(
        row_count, NMB, MB_LEN
    )
    pad_rows = pad_mask.astype(jnp.float32).reshape(row_count, NMB, MB_LEN)
    input_blocks = block_input.reshape(row_count, NMB, MB_LEN, width)
    grad_blocks = cotangent.reshape(row_count, NMB, MB_LEN, width)
    carry_now = (
        jnp.zeros((row_count, heads_local, E, E), jnp.float32),
        jnp.zeros((row_count, heads_local, E), jnp.float32),
        jnp.full((row_count,), -1, jnp.int32),
    )
    stored_in = jnp.zeros((row_count, NMB, MB_LEN, width), jnp.float32)
    stored_mid = jnp.zeros((row_count, NMB, MB_LEN, width), jnp.float32)
    stored_out = jnp.zeros((row_count, NMB, MB_LEN, width), jnp.float32)
    stored_mat = jnp.zeros((NMB, row_count, heads_local, E, E), jnp.float32)
    stored_sum = jnp.zeros((NMB, row_count, heads_local, E), jnp.float32)
    stored_last = jnp.zeros((NMB, row_count), jnp.int32)
    received = jnp.zeros((block_rows, width), jnp.bfloat16)
    for step_num in range(NMB + 1):
        block_num = step_num - section_num
        is_valid = (block_num >= 0) & (block_num < NMB)
        safe_block = jnp.clip(block_num, 0, NMB - 1)
        own_block = (
            block_of(input_blocks, safe_block).reshape(block_rows, width).astype(jnp.float32)
        )
        layer_in = jnp.where(section_num == 0, own_block, received.astype(jnp.float32))
        layer_out, middle, carry_next = layer_forward(
            layer_in,
            params,
            block_of(segment_ids, safe_block),
            block_of(pad_rows, safe_block).reshape(-1),
            carry_now,
        )
        stored_in = write_block(
            stored_in, safe_block, layer_in.reshape(row_count, MB_LEN, width), is_valid, 1
        )
        stored_mid = write_block(
            stored_mid, safe_block, middle.reshape(row_count, MB_LEN, width), is_valid, 1
        )
        stored_out = write_block(
            stored_out, safe_block, layer_out.reshape(row_count, MB_LEN, width), is_valid, 1
        )
        stored_mat = write_block(stored_mat, safe_block, carry_now[0], is_valid, 0)
        stored_sum = write_block(stored_sum, safe_block, carry_now[1], is_valid, 0)
        stored_last = write_block(stored_last, safe_block, carry_now[2], is_valid, 0)
        carry_now = (
            jnp.where(is_valid, carry_next[0], carry_now[0]),
            jnp.where(is_valid, carry_next[1], carry_now[1]),
            jnp.where(is_valid, carry_next[2], carry_now[2]),
        )
        if step_num < NMB:
            received = shifted_2(layer_out.astype(jnp.bfloat16), "section", 1)
    unit_cols = up_weight.shape[-1]
    weight_totals = (
        jnp.zeros(qkv_weight.shape[1:], jnp.float32),
        jnp.zeros(out_weight.shape[1:], jnp.float32),
        jnp.zeros((width, unit_cols), jnp.float32),
        jnp.zeros((width, unit_cols), jnp.float32),
    )
    norm_totals = (
        jnp.zeros(norm_gain.shape[1:], jnp.float32),
        jnp.zeros(norm_bias.shape[1:], jnp.float32),
    )
    grad_carry = (
        jnp.zeros((row_count, heads_local, E, E), jnp.float32),
        jnp.zeros((row_count, heads_local, E), jnp.float32),
    )
    stored_grad = jnp.zeros((row_count, NMB, MB_LEN, width), jnp.float32)
    incoming = jnp.zeros((block_rows, width), jnp.bfloat16)
    for step_num in range(NMB + 1):
        block_num = NMB - step_num - section_num
        is_valid = (block_num >= 0) & (block_num < NMB)
        safe_block = jnp.clip(block_num, 0, NMB - 1)
        own_grad = block_of(grad_blocks, safe_block).reshape(block_rows, width)
        grad_y = jnp.where(section_num == 1, own_grad, incoming.astype(jnp.float32))
        hidden_in = block_of(stored_in, safe_block).reshape(block_rows, width)
        middle = block_of(stored_mid, safe_block).reshape(block_rows, width)
        carry_start = (
            lax.dynamic_index_in_dim(stored_mat, safe_block, 0, keepdims=False),
            lax.dynamic_index_in_dim(stored_sum, safe_block, 0, keepdims=False),
            lax.dynamic_index_in_dim(stored_last, safe_block, 0, keepdims=False),
        )
        grad_in, grad_start, norm_parts, deferred = layer_backward(
            grad_y,
            hidden_in,
            middle,
            params,
            block_of(segment_ids, safe_block),
            block_of(pad_rows, safe_block).reshape(-1),
            carry_start,
            grad_carry,
        )
        norm_totals = add_masked(norm_totals, norm_parts, is_valid)
        grad_carry = (
            jnp.where(is_valid, grad_start[0], grad_carry[0]),
            jnp.where(is_valid, grad_start[1], grad_carry[1]),
        )
        stored_grad = write_block(
            stored_grad, safe_block, grad_in.reshape(row_count, MB_LEN, width), is_valid, 1
        )
        if step_num < NMB:
            incoming = shifted_2(grad_in.astype(jnp.bfloat16), "section", -1)
        weight_totals = add_masked(weight_totals, weight_grads(deferred), is_valid)
    up_total, down_total = (weight_totals[2], weight_totals[3])
    summed = (
        lax.psum(weight_totals[0].astype(jnp.bfloat16), "dp").astype(jnp.float32),
        lax.psum(weight_totals[1].astype(jnp.bfloat16), "dp").astype(jnp.float32),
        lax.psum(up_total.astype(jnp.bfloat16), "dp").astype(jnp.float32),
        lax.psum(down_total.astype(jnp.bfloat16), "dp").astype(jnp.float32),
        lax.psum(norm_totals[0].astype(jnp.bfloat16), "dp").astype(jnp.float32),
        lax.psum(norm_totals[1].astype(jnp.bfloat16), "dp").astype(jnp.float32),
    )
    activations = stored_out.reshape(1, row_count * SEQ, width)
    input_grad = stored_grad.reshape(1, row_count * SEQ, width)
    token_rms = jnp.sqrt(jnp.mean(activations * activations, axis=-1) + 1e-06)
    return (
        activations,
        input_grad,
        token_rms,
        summed[0][None],
        summed[1][None],
        summed[2][None],
        summed[3][None],
        summed[4][None],
        summed[5][None],
    )


def solution(mesh):
    placed = (
        P("dp", None),
        P("dp", None),
        P("dp"),
        P("dp"),
        P("section", None, None, "head"),
        P("section", "head", None),
        P("section", None, "head"),
        P("section", None, "head"),
        P("section", None, None),
        P("section", None, None),
    )
    return jax.shard_map(
        local,
        mesh=mesh,
        in_specs=placed,
        out_specs=(
            P("section", "dp", None),
            P("section", "dp", None),
            P("section", "dp"),
            P("section", None, None, "head"),
            P("section", "head", None),
            P("section", None, "head"),
            P("section", None, "head"),
            P("section", None, None),
            P("section", None, None),
        ),
        check_vma=False,
    )
```

profile of v0, /device:TPU:0, one launch (start us, length us, event | category | flops | bytes accessed | tf_op | source)
XLA Modules:
  0.0 1364.5 jit_solution(10955508080331133668)
XLA Ops:
  23.8 2.9 constant_dynamic-slice_fusion.31
  28.9 4.6 constant_dynamic-slice_fusion.1
  39.6 20.1 %all-reduce.24.cloned.1.call-done = bf16[512,512]{1,0:T(8,128)(2,1)} async-done(((bf16[512,512]{1,0:T(8,128)(2,1)}), bf16[512,512]{1,0:T(8,128)(2,1)}) %all-reduce.24.cloned.1.call-update) | async-done | bytes 524304 | tf_op jit(solution)/shard_map/psum | solution.py:171
  59.8 2.7 broadcast_select_fusion.1
  62.9 2.8 convolution_convert_fusion.9
  71.5 27.6 %all-reduce.26.cloned.1.call-done = bf16[512,512]{1,0:T(8,128)(2,1)} async-done(((bf16[512,512]{1,0:T(8,128)(2,1)}), bf16[512,512]{1,0:T(8,128)(2,1)}) %all-reduce.26.cloned.1.call-update) | async-done | bytes 524304 | tf_op jit(solution)/shard_map/psum | solution.py:178
  100.4 3.6 collective-permute-start
  110.5 3.5 collective-permute-done
  142.2 30.4 %all-reduce.28.cloned.1.call-done = bf16[512,512]{1,0:T(8,128)(2,1)} async-done(((bf16[512,512]{1,0:T(8,128)(2,1)}), bf16[512,512]{1,0:T(8,128)(2,1)}) %all-reduce.28.cloned.1.call-update) | async-done | bytes 524304 | tf_op jit(solution)/shard_map/psum | solution.py:171
  174.1 2.8 convolution_convert_fusion.8
  179.4 30.9 %all-reduce.30.cloned.1.call-done = bf16[512,512]{1,0:T(8,128)(2,1)} async-done(((bf16[512,512]{1,0:T(8,128)(2,1)}), bf16[512,512]{1,0:T(8,128)(2,1)}) %all-reduce.30.cloned.1.call-update) | async-done | bytes 524304 | tf_op jit(solution)/shard_map/psum | solution.py:178
  211.6 3.4 collective-permute-start.1
  219.8 5.4 collective-permute-done.1
  249.7 29.1 %all-reduce.32.cloned.1.call-done = bf16[512,512]{1,0:T(8,128)(2,1)} async-done(((bf16[512,512]{1,0:T(8,128)(2,1)}), bf16[512,512]{1,0:T(8,128)(2,1)}) %all-reduce.32.cloned.1.call-update) | async-done | bytes 524304 | tf_op jit(solution)/shard_map/psum | solution.py:171
  281.5 2.8 convolution_convert_fusion.7
  286.8 30.9 %all-reduce.34.cloned.1.call-done = bf16[512,512]{1,0:T(8,128)(2,1)} async-done(((bf16[512,512]{1,0:T(8,128)(2,1)}), bf16[512,512]{1,0:T(8,128)(2,1)}) %all-reduce.34.cloned.1.call-update) | async-done | bytes 524304 | tf_op jit(solution)/shard_map/psum | solution.py:178
  318.9 3.4 collective-permute-start.2
  327.2 5.4 collective-permute-done.2
  356.5 28.8 %all-reduce.36.cloned.1.call-done = bf16[512,512]{1,0:T(8,128)(2,1)} async-done(((bf16[512,512]{1,0:T(8,128)(2,1)}), bf16[512,512]{1,0:T(8,128)(2,1)}) %all-reduce.36.cloned.1.call-update) | async-done | bytes 524304 | tf_op jit(solution)/shard_map/psum | solution.py:171
  386.8 2.8 convolution_convert_fusion.6
  392.1 30.9 %all-reduce.38.cloned.1.call-done = bf16[512,512]{1,0:T(8,128)(2,1)} async-done(((bf16[512,512]{1,0:T(8,128)(2,1)}), bf16[512,512]{1,0:T(8,128)(2,1)}) %all-reduce.38.cloned.1.call-update) | async-done | bytes 524304 | tf_op jit(solution)/shard_map/psum | solution.py:178
  424.3 3.4 collective-permute-start.3
  432.5 5.4 collective-permute-done.3
  448.8 31.7 %all-reduce.40.cloned.1.call-done = bf16[512,512]{1,0:T(8,128)(2,1)} async-done(((bf16[512,512]{1,0:T(8,128)(2,1)}), bf16[512,512]{1,0:T(8,128)(2,1)}) %all-reduce.40.cloned.1.call-update) | async-done | bytes 524304 | tf_op jit(solution)/shard_map/psum | solution.py:171
  485.6 7.5 fusion.810
  531.3 2.8 fusion.877
  574.8 2.8 fusion.878
  594.6 2.8 fusion.879
  616.8 2.8 fusion.880
  634.9 2.9 fusion.881
  643.0 3.2 convolution_convert_fusion.5
  646.5 3.2 convolution_select_fusion
  676.9 3.4 fusion.201
  715.0 27.3 %all-reduce.44.cloned.1.call-done = bf16[512,512]{1,0:T(8,128)(2,1)} async-done(((bf16[512,512]{1,0:T(8,128)(2,1)}), bf16[512,512]{1,0:T(8,128)(2,1)}) %all-reduce.44.cloned.1.call-update) | async-done | bytes 524304 | tf_op jit(solution)/shard_map/psum | solution.py:238
  752.5 9.3 collective-permute-done.4
  765.4 3.3 add_select_fusion.3
  768.8 29.5 %all-reduce.46.cloned.1.call-done = bf16[512,512]{1,0:T(8,128)(2,1)} async-done(((bf16[512,512]{1,0:T(8,128)(2,1)}), bf16[512,512]{1,0:T(8,128)(2,1)}) %all-reduce.46.cloned.1.call-update) | async-done | bytes 524304 | tf_op jit(solution)/shard_map/psum | solution.py:200
  798.3 3.4 fusion.203
  843.7 2.7 fusion.882
  846.4 27.6 %all-reduce.48.cloned.1.call-done = bf16[512,512]{1,0:T(8,128)(2,1)} async-done(((bf16[512,512]{1,0:T(8,128)(2,1)}), bf16[512,512]{1,0:T(8,128)(2,1)}) %all-reduce.48.cloned.1.call-update) | async-done | bytes 524304 | tf_op jit(solution)/shard_map/psum | solution.py:238
  877.1 2.8 fusion.204
  879.9 2.8 fusion.824
  886.4 10.5 collective-permute-done.5
  900.5 2.7 select_dynamic-update-slice_fusion.3
  903.2 30.0 %all-reduce.50.cloned.1.call-done = bf16[512,512]{1,0:T(8,128)(2,1)} async-done(((bf16[512,512]{1,0:T(8,128)(2,1)}), bf16[512,512]{1,0:T(8,128)(2,1)}) %all-reduce.50.cloned.1.call-update) | async-done | bytes 524304 | tf_op jit(solution)/shard_map/psum | solution.py:200
  933.2 3.3 fusion.205
  975.9 23.8 %all-reduce.52.cloned.1.call-done = bf16[512,512]{1,0:T(8,128)(2,1)} async-done(((bf16[512,512]{1,0:T(8,128)(2,1)}), bf16[512,512]{1,0:T(8,128)(2,1)}) %all-reduce.52.cloned.1.call-update) | async-done | bytes 524304 | tf_op jit(solution)/shard_map/psum | solution.py:238
  1012.7 9.0 collective-permute-done.6
  1025.5 3.1 fusion.231
  1028.6 29.4 %all-reduce.54.cloned.1.call-done = bf16[512,512]{1,0:T(8,128)(2,1)} async-done(((bf16[512,512]{1,0:T(8,128)(2,1)}), bf16[512,512]{1,0:T(8,128)(2,1)}) %all-reduce.54.cloned.1.call-update) | async-done | bytes 524304 | tf_op jit(solution)/shard_map/psum | solution.py:200
  1058.1 3.4 fusion.207
  1100.8 3.4 add_select_fusion.5
  1108.6 23.6 %all-reduce.56.cloned.1.call-done = bf16[512,512]{1,0:T(8,128)(2,1)} async-done(((bf16[512,512]{1,0:T(8,128)(2,1)}), bf16[512,512]{1,0:T(8,128)(2,1)}) %all-reduce.56.cloned.1.call-update) | async-done | bytes 524304 | tf_op jit(solution)/shard_map/psum | solution.py:238
  1144.6 9.0 collective-permute-done.7
  1158.0 3.9 fusion.48
  1161.8 28.9 %all-reduce.58.cloned.1.call-done = bf16[512,512]{1,0:T(8,128)(2,1)} async-done(((bf16[512,512]{1,0:T(8,128)(2,1)}), bf16[512,512]{1,0:T(8,128)(2,1)}) %all-reduce.58.cloned.1.call-update) | async-done | bytes 524304 | tf_op jit(solution)/shard_map/psum | solution.py:200
  1190.8 3.0 fusion.209
  1222.9 2.7 fusion.47
  1225.6 31.4 %all-reduce.60.cloned.1.call-done = (bf16[512,512]{1,0:T(8,128)(2,1)}, bf16[512,512]{1,0:T(8,128)(2,1)}) async-done(((bf16[512,512]{1,0:T(8,128)(2,1)}, bf16[512,512]{1,0:T(8,128)(2,1)}), (bf16[512,512]{1,0:T(8,128)(2,1)}, bf16[512,512]{1,0:T(8,128)(2,1)})) %all-reduce.60.cloned.1.call-update) | async-done | bytes 1048592 | tf_op jit(solution)/shard_map/psum | solution.py:178
  1259.1 3.0 fusion.210
  1264.3 12.4 all-reduce.1
  1285.4 2.8 copy.1453
  1290.7 4.7 copy.1305
  1298.6 51.8 %all-reduce.62.cloned.1.call-done = (bf16[1,3,512,128]{2,3,1,0:T(8,128)(2,1)}, bf16[1,128,512]{2,1,0:T(8,128)(2,1)}, bf16[1,512,512]{2,1,0:T(8,128)(2,1)}, bf16[1,512,512]{2,1,0:T(8,128)(2,1)}) async-done(((bf16[1,3,512,128]{2,3,1,0:T(8,128)(2,1)}, bf16[1,128,512]{2,1,0:T(8,128)(2,1)}, bf16[1,512,512]{2,1,0:T(8,128)(2,1)}, bf16[1,512,512]{2,1,0:T(8,128)(2,1)}), (bf16[1,3,512,128]{2,3,1,0:T(8,128)(2,1)}, ...) | async-done | bytes 1572880 | tf_op jit(solution)/shard_map/psum | solution.py:389
  (1205 shorter events, 595.3 us)
Async XLA Ops:
  7.2 55.7 %copy-start = (bf16[1,512,512]{2,1,0:T(8,128)(2,1)S(1)}, bf16[1,512,512]{2,1,0:T(8,128)(2,1)}, u32[]{:S(2)}) copy-start(bf16[1,512,512]{2,1,0:T(8,128)(2,1)} %param.16) | copy-start | bytes 1572868
  7.2 52.6 %all-reduce.24.cloned.1.call-start = ((), (), s32[]{:S(2)}) async-start(), calls=%async_computation | async-start | bytes 1048576 | tf_op jit(solution)/shard_map/psum | solution.py:171
  20.5 112.1 %copy-start.43 = (f32[2,256,256]{1,2,0:T(8,128)}, f32[2,256,256]{1,2,0:T(8,128)S(1)}, u32[]{:S(2)}) copy-start(f32[2,256,256]{1,2,0:T(8,128)S(1)} %get-tuple-element.318) | copy-start | bytes 1572868
  23.7 75.3 %all-reduce.26.cloned.1.call-start = ((), (), s32[]{:S(2)}) async-start(), calls=%async_computation.1 | async-start | bytes 1048576 | tf_op jit(solution)/shard_map/psum | solution.py:178
  65.7 106.9 %all-reduce.28.cloned.1.call-start = ((), (), s32[]{:S(2)}) async-start(), calls=%async_computation.2 | async-start | bytes 1048576 | tf_op jit(solution)/shard_map/psum | solution.py:171
  100.4 13.6 collective-permute-start
  132.6 41.3 %copy-start.145 = (f32[2,2,64]{0,2,1:T(8,128)}, f32[2,2,64]{0,2,1:T(8,128)S(1)}, u32[]{:S(2)}) copy-start(f32[2,2,64]{0,2,1:T(8,128)S(1)} %get-tuple-element.223) | copy-start | bytes 3076
  138.3 72.0 %all-reduce.30.cloned.1.call-start = ((), (), s32[]{:S(2)}) async-start(), calls=%async_computation.3 | async-start | bytes 1048576 | tf_op jit(solution)/shard_map/psum | solution.py:178
  176.9 101.9 %all-reduce.32.cloned.1.call-start = ((), (), s32[]{:S(2)}) async-start(), calls=%async_computation.4 | async-start | bytes 1048576 | tf_op jit(solution)/shard_map/psum | solution.py:171
  211.6 13.6 collective-permute-start.1
  244.4 73.2 %all-reduce.34.cloned.1.call-start = ((), (), s32[]{:S(2)}) async-start(), calls=%async_computation.5 | async-start | bytes 1048576 | tf_op jit(solution)/shard_map/psum | solution.py:178
  284.3 101.0 %all-reduce.36.cloned.1.call-start = ((), (), s32[]{:S(2)}) async-start(), calls=%async_computation.6 | async-start | bytes 1048576 | tf_op jit(solution)/shard_map/psum | solution.py:171
  318.9 13.6 collective-permute-start.2
  350.9 72.0 %all-reduce.38.cloned.1.call-start = ((), (), s32[]{:S(2)}) async-start(), calls=%async_computation.7 | async-start | bytes 1048576 | tf_op jit(solution)/shard_map/psum | solution.py:178
  389.6 90.9 %all-reduce.40.cloned.1.call-start = ((), (), s32[]{:S(2)}) async-start(), calls=%async_computation.8 | async-start | bytes 1048576 | tf_op jit(solution)/shard_map/psum | solution.py:171
  424.3 13.6 collective-permute-start.3
  446.2 227.6 %all-reduce.42.cloned.1.call-start = ((), (), s32[]{:S(2)}) async-start(), calls=%async_computation.9 | async-start | bytes 1048576 | tf_op jit(solution)/shard_map/psum | solution.py:200
  531.3 23.9 %copy-start.129 = (bf16[2,2,256,64]{2,0,3,1:T(2,128)(2,1)}, bf16[2,2,256,64]{2,0,3,1:T(2,128)(2,1)S(1)}, u32[]{:S(2)}) copy-start(bf16[2,2,256,64]{2,0,3,1:T(2,128)(2,1)S(1)} %get-tuple-element.170) | copy-start | bytes 393220
  559.8 182.5 %all-reduce.44.cloned.1.call-start = ((), (), s32[]{:S(2)}) async-start(), calls=%async_computation.10 | async-start | bytes 1048576 | tf_op jit(solution)/shard_map/psum | solution.py:238
  565.0 22.3 %copy-start.88 = (bf16[2,2,256,64]{2,0,3,1:T(2,128)(2,1)}, bf16[2,2,256,64]{2,0,3,1:T(2,128)(2,1)S(1)}, u32[]{:S(2)}) copy-start(bf16[2,2,256,64]{2,0,3,1:T(2,128)(2,1)S(1)} %fusion.566) | copy-start | bytes 393220
  607.8 46.5 %copy-start.86 = (bf16[2,2,256,64]{2,0,3,1:T(2,128)(2,1)}, bf16[2,2,256,64]{2,0,3,1:T(2,128)(2,1)S(1)}, u32[]{:S(2)}) copy-start(bf16[2,2,256,64]{2,0,3,1:T(2,128)(2,1)S(1)} %fusion.568) | copy-start | bytes 393220
  646.4 16.4 %copy-start.255 = (f32[1,2,2,128]{3,2,1,0:T(2,128)S(1)}, f32[1,2,2,128]{3,2,1,0:T(2,128)}, u32[]{:S(2)}) copy-start(f32[1,2,2,128]{3,2,1,0:T(2,128)} %get-tuple-element.376) | copy-start | bytes 6148
  646.4 17.0 %copy-start.254 = (f32[1,2,2,128]{3,2,1,0:T(2,128)S(1)}, f32[1,2,2,128]{3,2,1,0:T(2,128)}, u32[]{:S(2)}) copy-start(f32[1,2,2,128]{3,2,1,0:T(2,128)} %get-tuple-element.378) | copy-start | bytes 6148
  646.4 17.5 %copy-start.244 = (f32[1,2,2,128]{3,2,1,0:T(2,128)S(1)}, f32[1,2,2,128]{3,2,1,0:T(2,128)}, u32[]{:S(2)}) copy-start(f32[1,2,2,128]{3,2,1,0:T(2,128)} %get-tuple-element.366) | copy-start | bytes 6148
  646.4 18.1 %copy-start.245 = (f32[1,2,2,128]{3,2,1,0:T(2,128)S(1)}, f32[1,2,2,128]{3,2,1,0:T(2,128)}, u32[]{:S(2)}) copy-start(f32[1,2,2,128]{3,2,1,0:T(2,128)} %get-tuple-element.364) | copy-start | bytes 6148
  646.4 18.7 %copy-start.253 = (f32[1,2,2,128]{3,2,1,0:T(2,128)S(1)}, f32[1,2,2,128]{3,2,1,0:T(2,128)}, u32[]{:S(2)}) copy-start(f32[1,2,2,128]{3,2,1,0:T(2,128)} %get-tuple-element.358) | copy-start | bytes 6148
  646.5 19.8 %copy-start.252 = (f32[1,2,2,128]{3,2,1,0:T(2,128)S(1)}, f32[1,2,2,128]{3,2,1,0:T(2,128)}, u32[]{:S(2)}) copy-start(f32[1,2,2,128]{3,2,1,0:T(2,128)} %get-tuple-element.360) | copy-start | bytes 6148
  708.9 89.3 %all-reduce.46.cloned.1.call-start = ((), (), s32[]{:S(2)}) async-start(), calls=%async_computation.11 | async-start | bytes 1048576 | tf_op jit(solution)/shard_map/psum | solution.py:200
  747.6 14.2 %collective-permute-start.4 = (bf16[512,512]{1,0:T(8,128)(2,1)S(1)}, bf16[512,512]{1,0:T(8,128)(2,1)S(1)}, u32[]{:S(2)}, u32[]{:S(2)}) collective-permute-start(bf16[512,512]{1,0:T(8,128)(2,1)S(1)} %get-tuple-element.262), channel_id=1, source_target_pairs={{16,0},{17,1},{18,2},{19,3},{20,4},{21,5},{22,6},{23,7},{24,8},{25... | collective-permute-start | bytes 1572872 | tf_op jit(solution)/shard_map/ppermute | solution.py:19
  763.9 34.3 %copy-start.226 = (f32[512]{0:T(512)S(1)}, f32[512]{0:T(512)}, u32[]{:S(2)}) copy-start(f32[512]{0:T(512)} %rsqrt.225) | copy-start | bytes 6148
  763.9 34.3 %copy-start.227 = (f32[1,2,2,128]{3,1,2,0:T(2,128)S(1)}, f32[1,2,2,128]{3,1,2,0:T(2,128)}, u32[]{:S(2)}) copy-start(f32[1,2,2,128]{3,1,2,0:T(2,128)} %copy.1735) | copy-start | bytes 6148
  763.9 37.8 %copy-start.220 = (f32[1,2,2,128]{3,1,2,0:T(2,128)S(1)}, f32[1,2,2,128]{3,1,2,0:T(2,128)}, u32[]{:S(2)}) copy-start(f32[1,2,2,128]{3,1,2,0:T(2,128)} %copy-done.219) | copy-start | bytes 6148
  765.2 108.8 %all-reduce.48.cloned.1.call-start = ((), (), s32[]{:S(2)}) async-start(), calls=%async_computation.12 | async-start | bytes 1048576 | tf_op jit(solution)/shard_map/psum | solution.py:238
  824.6 17.6 %copy-start.101 = (f32[2,2,256,64]{2,3,1,0:T(8,128)S(1)}, f32[2,2,256,64]{2,3,1,0:T(8,128)}, u32[]{:S(2)}) copy-start(f32[2,2,256,64]{2,3,1,0:T(8,128)} %convolution_add_fusion.8) | copy-start | bytes 786436
  840.6 92.6 %all-reduce.50.cloned.1.call-start = ((), (), s32[]{:S(2)}) async-start(), calls=%async_computation.13 | async-start | bytes 1048576 | tf_op jit(solution)/shard_map/psum | solution.py:200
  879.9 17.1 %copy-start.23 = (f32[2,1,256,512]{3,2,1,0:T(8,128)S(1)}, f32[2,1,256,512]{3,2,1,0:T(8,128)}, u32[]{:S(2)}) copy-start(f32[2,1,256,512]{3,2,1,0:T(8,128)} %get-tuple-element.251) | copy-start | bytes 3145732
  882.7 14.2 %collective-permute-start.5 = (bf16[512,512]{1,0:T(8,128)(2,1)S(1)}, bf16[512,512]{1,0:T(8,128)(2,1)S(1)}, u32[]{:S(2)}, u32[]{:S(2)}) collective-permute-start(bf16[512,512]{1,0:T(8,128)(2,1)S(1)} %get-tuple-element.156), channel_id=1, source_target_pairs={{16,0},{17,1},{18,2},{19,3},{20,4},{21,5},{22,6},{23,7},{24,8},{25... | collective-permute-start | bytes 1572872 | tf_op jit(solution)/shard_map/ppermute | solution.py:19
  900.2 99.4 %all-reduce.52.cloned.1.call-start = ((), (), s32[]{:S(2)}) async-start(), calls=%async_computation.14 | async-start | bytes 1048576 | tf_op jit(solution)/shard_map/psum | solution.py:238
  903.2 37.0 %copy-start.99 = (f32[2,2,256,64]{2,3,1,0:T(8,128)S(1)}, f32[2,2,256,64]{2,3,1,0:T(8,128)}, u32[]{:S(2)}) copy-start(f32[2,2,256,64]{2,3,1,0:T(8,128)} %convolution_add_fusion.7) | copy-start | bytes 786436
  966.3 91.7 %all-reduce.54.cloned.1.call-start = ((), (), s32[]{:S(2)}) async-start(), calls=%async_computation.15 | async-start | bytes 1048576 | tf_op jit(solution)/shard_map/psum | solution.py:200
  1007.5 14.2 %collective-permute-start.6 = (bf16[512,512]{1,0:T(8,128)(2,1)S(1)}, bf16[512,512]{1,0:T(8,128)(2,1)S(1)}, u32[]{:S(2)}, u32[]{:S(2)}) collective-permute-start(bf16[512,512]{1,0:T(8,128)(2,1)S(1)} %get-tuple-element.141), channel_id=1, source_target_pairs={{16,0},{17,1},{18,2},{19,3},{20,4},{21,5},{22,6},{23,7},{24,8},{25... | collective-permute-start | bytes 1572872 | tf_op jit(solution)/shard_map/ppermute | solution.py:19
  1023.7 34.3 %copy-start.224 = (f32[512]{0:T(512)S(1)}, f32[512]{0:T(512)}, u32[]{:S(2)}) copy-start(f32[512]{0:T(512)} %rsqrt.233) | copy-start | bytes 6148
  1023.7 34.3 %copy-start.225 = (f32[1,2,2,128]{3,1,2,0:T(2,128)S(1)}, f32[1,2,2,128]{3,1,2,0:T(2,128)}, u32[]{:S(2)}) copy-start(f32[1,2,2,128]{3,1,2,0:T(2,128)} %copy.1743) | copy-start | bytes 6148
  1023.7 37.7 %copy-start.217 = (f32[1,2,2,128]{3,1,2,0:T(2,128)S(1)}, f32[1,2,2,128]{3,1,2,0:T(2,128)}, u32[]{:S(2)}) copy-start(f32[1,2,2,128]{3,1,2,0:T(2,128)} %copy-done.216) | copy-start | bytes 6148
  1025.0 107.3 %all-reduce.56.cloned.1.call-start = ((), (), s32[]{:S(2)}) async-start(), calls=%async_computation.16 | async-start | bytes 1048576 | tf_op jit(solution)/shard_map/psum | solution.py:238
  1028.6 36.5 %copy-start.97 = (f32[2,2,256,64]{2,3,1,0:T(8,128)S(1)}, f32[2,2,256,64]{2,3,1,0:T(8,128)}, u32[]{:S(2)}) copy-start(f32[2,2,256,64]{2,3,1,0:T(8,128)} %convolution_add_fusion.6) | copy-start | bytes 786436
  1073.0 17.7 %copy-start.120 = (f32[2,2,64,64]{3,2,1,0:T(8,128)S(1)}, f32[2,2,64,64]{3,2,1,0:T(8,128)}, u32[]{:S(2)}) copy-start(f32[2,2,64,64]{3,2,1,0:T(8,128)} %fusion.111) | copy-start | bytes 196612
  1099.0 91.7 %all-reduce.58.cloned.1.call-start = ((), (), s32[]{:S(2)}) async-start(), calls=%async_computation.17 | async-start | bytes 1048576 | tf_op jit(solution)/shard_map/psum | solution.py:200
  1139.4 14.2 %collective-permute-start.7 = (bf16[512,512]{1,0:T(8,128)(2,1)S(1)}, bf16[512,512]{1,0:T(8,128)(2,1)S(1)}, u32[]{:S(2)}, u32[]{:S(2)}) collective-permute-start(bf16[512,512]{1,0:T(8,128)(2,1)S(1)} %get-tuple-element.128), channel_id=1, source_target_pairs={{16,0},{17,1},{18,2},{19,3},{20,4},{21,5},{22,6},{23,7},{24,8},{25... | collective-permute-start | bytes 1572872 | tf_op jit(solution)/shard_map/ppermute | solution.py:19
  1156.4 34.3 %copy-start.13 = (f32[2,1,256,512]{3,2,0,1:T(8,128)S(1)}, f32[2,1,256,512]{3,2,0,1:T(8,128)}, u32[]{:S(2)}) copy-start(f32[2,1,256,512]{3,2,0,1:T(8,128)} %get-tuple-element.469) | copy-start | bytes 3145732
  1156.4 34.3 %copy-start.222 = (f32[512]{0:T(512)S(1)}, f32[512]{0:T(512)}, u32[]{:S(2)}) copy-start(f32[512]{0:T(512)} %rsqrt.237) | copy-start | bytes 6148
  1156.4 34.3 %copy-start.223 = (f32[1,2,2,128]{3,1,2,0:T(2,128)S(1)}, f32[1,2,2,128]{3,1,2,0:T(2,128)}, u32[]{:S(2)}) copy-start(f32[1,2,2,128]{3,1,2,0:T(2,128)} %copy.1747) | copy-start | bytes 6148
  1157.7 36.1 %copy-start.215 = (f32[1,2,2,128]{3,1,2,0:T(2,128)S(1)}, f32[1,2,2,128]{3,1,2,0:T(2,128)}, u32[]{:S(2)}) copy-start(f32[1,2,2,128]{3,1,2,0:T(2,128)} %copy-done.214) | copy-start | bytes 6148
  1157.7 99.2 %all-reduce.60.cloned.1.call-start = ((), (), s32[]{:S(2)}) async-start(), calls=%async_computation.18 | async-start | bytes 2097152 | tf_op jit(solution)/shard_map/psum | solution.py:178
  1161.8 34.0 %copy-start.96 = (f32[2,2,256,64]{2,3,1,0:T(8,128)S(1)}, f32[2,2,256,64]{2,3,1,0:T(8,128)}, u32[]{:S(2)}) copy-start(f32[2,2,256,64]{2,3,1,0:T(8,128)} %convolution_add_fusion.5) | copy-start | bytes 786436
  1198.6 18.1 %copy-start.51 = (f32[3,512,128]{2,1,0:T(8,128)S(1)}, f32[3,512,128]{2,1,0:T(8,128)}, u32[]{:S(2)}) copy-start(f32[3,512,128]{2,1,0:T(8,128)} %copy-done.50) | copy-start | bytes 2359300
  1216.6 40.3 %copy-start.201 = (f32[1,2,2,128]{3,1,2,0:T(2,128)S(1)}, f32[1,2,2,128]{3,1,2,0:T(2,128)}, u32[]{:S(2)}) copy-start(f32[1,2,2,128]{3,1,2,0:T(2,128)} %copy.1749) | copy-start | bytes 6148
  1220.8 129.6 %all-reduce.62.cloned.1.call-start = ((), (), s32[]{:S(2)}) async-start(), calls=%async_computation.19 | async-start | bytes 3145728 | tf_op jit(solution)/shard_map/psum | solution.py:389
  1220.8 59.0 %copy-start.156 = (bf16[1,512,128]{2,1,0:T(8,128)(2,1)S(1)}, bf16[1,512,128]{2,1,0:T(8,128)(2,1)}, u32[]{:S(2)}) copy-start(bf16[1,512,128]{2,1,0:T(8,128)(2,1)} %reshape.2679) | copy-start | bytes 393220
  1220.8 59.0 %copy-start.158 = (bf16[1,512,128]{2,1,0:T(8,128)(2,1)S(1)}, bf16[1,512,128]{2,1,0:T(8,128)(2,1)}, u32[]{:S(2)}) copy-start(bf16[1,512,128]{2,1,0:T(8,128)(2,1)} %copy-done.157) | copy-start | bytes 393220
  1220.9 59.0 %copy-start.160 = (bf16[1,512,128]{2,1,0:T(8,128)(2,1)S(1)}, bf16[1,512,128]{2,1,0:T(8,128)(2,1)}, u32[]{:S(2)}) copy-start(bf16[1,512,128]{2,1,0:T(8,128)(2,1)} %copy-done.159) | copy-start | bytes 393220
  1225.6 56.7 %copy-start.19 = (f32[2,1,256,512]{3,2,1,0:T(8,128)S(1)}, f32[2,1,256,512]{3,2,1,0:T(8,128)}, u32[]{:S(2)}) copy-start(f32[2,1,256,512]{3,2,1,0:T(8,128)} %get-tuple-element.249) | copy-start | bytes 3145732
  1225.6 56.7 %copy-start.207 = (f32[512]{0:T(512)S(1)}, f32[512]{0:T(512)}, u32[]{:S(2)}) copy-start(f32[512]{0:T(512)} %copy-done.206) | copy-start | bytes 6148
  1257.0 25.4 %copy-start.56 = (bf16[512,512]{1,0:T(8,128)(2,1)S(1)}, bf16[512,512]{1,0:T(8,128)(2,1)}, u32[]{:S(2)}) copy-start(bf16[512,512]{1,0:T(8,128)(2,1)} %get-tuple-element.106) | copy-start | bytes 1572868
  (254 other events, 1599.8 us)
Sparse Core Ops, SparseCore 0:
  23.8 35.8 all-reduce.23
  65.8 33.1 all-reduce.25
  138.4 34.1 all-reduce.27
  177.1 33.1 all-reduce.29
  244.6 34.1 all-reduce.31
  284.4 33.1 all-reduce.33
  351.1 34.1 all-reduce.35
  389.7 33.1 all-reduce.37
  446.3 34.1 all-reduce.39
  559.9 33.1 all-reduce.41
  709.0 33.1 all-reduce.43
  765.3 32.8 all-reduce.45
  840.8 33.1 all-reduce.47
  900.3 32.8 all-reduce.49
  966.4 33.1 all-reduce.51
  1025.1 32.8 all-reduce.53
  1099.2 33.0 all-reduce.55
  1157.9 32.8 all-reduce.57
  1220.9 36.0 all-reduce.59
  1282.5 67.8 all-reduce.61
where the time goes:
time: 1380 us; the launch traced here: 1360 us
  waiting for transfers between devices  621 us (45%)
  other arithmetic  249 us (18%)
  local copies, waits for them, and re-layouts  226 us (16%)
  matrix products  216 us (16%)
  starting transfers between devices  22.1 us (2%)
  between operations  18.2 us (1%)
    psum x5, waiting for transfers between devices, layer_forward(): lax.psum(jnp.einsum('tj,dj->td', active, down_w, preferred_element_type=j...  152 us
    psum x5, waiting for transfers between devices, layer_forward(): lax.psum(jnp.dot(mixed_heads, out_w, preferred_element_type=jnp.float32)....  140 us
    psum x5, waiting for transfers between devices, layer_backward(): lax.psum(jnp.einsum('tj,dj->td', grad_up_proj, up_w, preferred_element_ty...  118 us
    psum x4, waiting for transfers between devices, layer_backward(): lax.psum(jnp.einsum('ctj,cdj->td', grad_proj, qkv_w, preferred_element_ty...  102 us
    ppermute x8, waiting for transfers between devices, shifted_2(): return lax.ppermute(block, axis, route)  57.5 us
    psum x1, waiting for transfers between devices, local(): lax.psum(weight_totals[0].astype(jnp.bfloat16), 'dp').astype(jnp.float32)  51.8 us
    dynamic_update_slice x21, other arithmetic, write_block(): lax.dynamic_update_index_in_dim(buffer, jnp.where(is_valid, new_value, ol...  40.8 us
    reduce_sum x15, other arithmetic, layer_norm(): return shifted * lax.rsqrt(spread + EPS) * gain_vec + bias_vec  40.7 us
  transfers between devices with their start and end apart: 28, of which 27 were waited for; matrix products, arithmetic and copies ran while one was open for 19% of the time, Pallas kernels for 0%

commit v1 on v0

v1 whole, which is shorter than its diff:
```python
import functools

import jax
import jax.numpy as jnp
from jax import lax
from jax.experimental import pallas as pl
from jax.experimental.pallas import tpu as pltpu
from jax.sharding import PartitionSpec as P

E = 64
SEQ = 1024
LANES = 128
PAIR = 2 * LANES
CHUNK = 128
EPS = 1e-05
F32 = jnp.float32
BF16 = jnp.bfloat16
ROWS = 128
GELU_C = 0.7978845608028654
GELU_A = 0.044715
SPLIT = 1.0 / 32.0
VMEM_LIMIT = 60 * 1024 * 1024

PAD, SEG, CARRY_IN, TAIL_OUT, CARRIED, TAIL = range(6)


def nn(a, b):
    return jnp.dot(a, b, preferred_element_type=F32)


def nt(a, b):
    return lax.dot_general(a, b, (((1,), (1,)), ((), ())), preferred_element_type=F32)


def tn(a, b):
    return lax.dot_general(a, b, (((0,), (0,)), ((), ())), preferred_element_type=F32)


def first_head(shape):
    return lax.broadcasted_iota(jnp.int32, shape, len(shape) - 1) % LANES < E


def diagonal_blocks():
    row = lax.broadcasted_iota(jnp.int32, (LANES, PAIR), 0) < E
    return (row == first_head((LANES, PAIR))).astype(F32)


def split_pair(block):
    in_a = first_head(block.shape)
    zero = jnp.zeros_like(block)
    return jnp.concatenate([jnp.where(in_a, block, zero), jnp.where(in_a, zero, block)], axis=0)


def side(block, fill):
    return jnp.concatenate([block, jnp.full(block.shape, fill, block.dtype)], axis=1)


def normalise(values):
    centre = jnp.mean(values, axis=-1, keepdims=True)
    shifted = values - centre
    scale = lax.rsqrt(jnp.mean(shifted * shifted, axis=-1, keepdims=True) + EPS)
    return shifted * scale, scale


def norm_backward(grad, unit, scale, gain):
    grad_unit = grad * gain
    mean_grad = jnp.mean(grad_unit, axis=-1, keepdims=True)
    mean_dot = jnp.mean(grad_unit * unit, axis=-1, keepdims=True)
    return scale * (grad_unit - mean_grad - unit * mean_dot)


def row_tiles(total, step=ROWS):
    def decorate(body):
        pl.loop(0, total // step)(
            lambda index: body(pl.ds(pl.multiple_of(index * step, step), step))
        )

    return decorate


def chunk_masks(cols_ref, seg_ref, mask, mask_t):
    row = lax.broadcasted_iota(jnp.int32, (CHUNK, CHUNK), 0)
    col = lax.broadcasted_iota(jnp.int32, (CHUNK, CHUNK), 1)
    for chunk in range(cols_ref.shape[0] // CHUNK):
        span = slice(chunk * CHUNK, (chunk + 1) * CHUNK)
        same = cols_ref[span, SEG : SEG + 1] == seg_ref[0:1, span]
        if mask is not None:
            lower = (same & (col <= row)).astype(F32)
            mask[chunk] = jnp.concatenate([lower, lower], axis=1)
        if mask_t is not None:
            upper = (same & (row <= col)).astype(F32)
            mask_t[chunk] = jnp.concatenate([upper, upper], axis=1)


def qkv_kernel(x, gain, bias, cols, w0, w1, w2, w3, fq, fk, vv, state, w, normed, sems):
    copies = [
        pltpu.make_async_copy(part, w.at[:, :, r * LANES : (r + 1) * LANES], sems.at[r])
        for r, part in enumerate((w0, w1, w2, w3))
    ]
    for copy in copies:
        copy.start()
    total = x.shape[0]

    @row_tiles(total)
    def _(rows):
        unit, _ = normalise(x[rows, :].astype(F32))
        normed[rows, :] = (unit * gain[0:1, :] + bias[0:1, :]).astype(BF16)

    for copy in copies:
        copy.wait()

    @row_tiles(total, 256)
    def _(rows):
        block = normed[rows, :]
        query = nn(block, w[0])
        fq[rows, :] = jnp.where(query > 0, query + 1.0, jnp.exp(jnp.minimum(query, 0.0))).astype(BF16)
        key = nn(block, w[1])
        key = jnp.where(key > 0, key + 1.0, jnp.exp(jnp.minimum(key, 0.0)))
        fk[rows, :] = (key * cols[rows, PAD : PAD + 1]).astype(BF16)
        vv[rows, :] = nn(block, w[2]).astype(BF16)

    diag = diagonal_blocks()
    for pair in range(state.shape[0]):
        lanes = slice(pair * LANES, (pair + 1) * LANES)
        tail = (fk[:, lanes] * cols[:, TAIL_OUT : TAIL_OUT + 1].astype(BF16)).astype(BF16)
        state[pair] = (diag * tn(tail, side(vv[:, lanes], 1.0))).astype(BF16)


def attention_forward(fq, fk, vv, start, cols, seg, o, inv_den, states, mask):
    chunk_masks(cols, seg, mask, None)
    diag = diagonal_blocks()

    @pl.loop(0, start.shape[0])
    def _(pair):
        lanes = pl.ds(pl.multiple_of(pair * LANES, LANES), LANES)
        state = start[pair].astype(F32)
        for chunk in range(fq.shape[0] // CHUNK):
            span = slice(chunk * CHUNK, (chunk + 1) * CHUNK)
            query, key, value = fq[span, lanes], fk[span, lanes], vv[span, lanes]
            carried = cols[span, CARRIED : CARRIED + 1]
            tail = cols[span, TAIL : TAIL + 1].astype(BF16)
            state_low = state.astype(BF16)
            if states is not None:
                states[pair, chunk] = state_low
            scores = (nt(query, split_pair(key)) * mask[chunk]).astype(BF16)
            ones = split_pair(jnp.ones_like(value))
            values = jnp.concatenate([split_pair(value), ones], axis=1)
            both = nn(scores, values) + carried * nn(query, state_low)
            inverse = 1.0 / (both[:, LANES:] + 1.0)
            o[span, lanes] = (both[:, :LANES] * inverse).astype(BF16)
            if inv_den is not None:
                inv_den[span, lanes] = inverse
            keep = carried[CHUNK - 1 : CHUNK, :]
            state = keep * state + diag * tn(key * tail, side(value, 1.0))


def start_copies(parts, place, sems, base):
    copies = [
        pltpu.make_async_copy(part, place(r), sems.at[base + r]) for r, part in enumerate(parts)
    ]
    for copy in copies:
        copy.start()
    return copies


def out_and_norm(o, x, out_w, gain, bias, mid, normed_two):
    @row_tiles(o.shape[0], 256)
    def _(rows):
        mid[rows, :] = x[rows, :].astype(F32) + nn(o[rows, :], out_w[...])

    @row_tiles(o.shape[0])
    def _(rows):
        unit, _ = normalise(mid[rows, :])
        normed_two[rows, :] = (unit * gain[1:2, :] + bias[1:2, :]).astype(BF16)


def gelu_parts(up, with_slope):
    square = up * up
    inner = jnp.tanh(GELU_C * up * (1.0 + GELU_A * square))
    half = 0.5 * (1.0 + inner)
    if not with_slope:
        return up * half, None
    slope = half + up * (0.5 * GELU_C) * (1.0 - inner * inner) * (1.0 + 3.0 * GELU_A * square)
    return up * half, slope


def attention_kernel(
    fq, fk, vv, start, cols, seg, x, gain, bias, w0, w1, w2, w3, mid, normed_two, mask, o, w, sems
):
    copies = start_copies(
        (w0, w1, w2, w3), lambda r: w.at[r * LANES : (r + 1) * LANES, :], sems, 0
    )
    attention_forward(fq, fk, vv, start, cols, seg, o, None, None, mask)
    for copy in copies:
        copy.wait()
    out_and_norm(o, x, w, gain, bias, mid, normed_two)


def up_kernel(normed_two, w0, w1, w2, w3, active):
    width = w0.shape[1]
    for r, w in enumerate((w0, w1, w2, w3)):

        @row_tiles(normed_two.shape[0], 256)
        def _(rows, r=r, w=w):
            up = nn(normed_two[rows, :], w[...])
            active[rows, r * width : (r + 1) * width] = gelu_parts(up, False)[0].astype(BF16)


def down_kernel(mid, active, w0, w1, w2, w3, y):
    width = w0.shape[1]

    @row_tiles(mid.shape[0], 256)
    def _(rows):
        total = mid[rows, :]
        for r, w in enumerate((w0, w1, w2, w3)):
            total = total + nt(active[rows, r * width : (r + 1) * width], w[...])
        y[rows, :] = total.astype(BF16)


def block_kernel(
    fq, fk, vv, start, cols, seg, x, gain, bias, *rest
):
    outs, ups, downs = rest[0:4], rest[4:8], rest[8:12]
    y, mid, o, inv_den, states, active, slope = rest[12:19]
    mask, normed_two, out_w, up_w, down_w, sems = rest[19:]
    out_copies = start_copies(
        outs, lambda r: out_w.at[r * LANES : (r + 1) * LANES, :], sems, 0
    )
    up_copies = start_copies(ups, lambda r: up_w.at[r], sems, 4)
    down_copies = start_copies(downs, lambda r: down_w.at[r], sems, 8)
    attention_forward(fq, fk, vv, start, cols, seg, o, inv_den, states, mask)
    for copy in out_copies:
        copy.wait()
    out_and_norm(o, x, out_w, gain, bias, mid, normed_two)
    for copy in up_copies + down_copies:
        copy.wait()
    width = up_w.shape[2]

    @row_tiles(x.shape[0], 256)
    def _(rows):
        total = mid[rows, :]
        for r in range(4):
            units = slice(r * width, (r + 1) * width)
            value, steep = gelu_parts(nn(normed_two[rows, :], up_w[r]), True)
            value = value.astype(BF16)
            active[rows, units] = value
            slope[rows, units] = steep.astype(BF16)
            total = total + nt(value, down_w[r])
        y[rows, :] = total.astype(BF16)


def ffn_back_kernel(with_weights, gy, slope, mid, o, inv_den, fq, cols, gain, *rest):
    outs, ups, downs = rest[0:4], rest[4:8], rest[8:12]
    rest = rest[12:]
    grad_mid, dnum, dden, grad_state = rest[0:4]
    rest = rest[4:]
    if with_weights:
        dup_out, dattn, sums = rest[0:3]
        rest = rest[3:]
    else:
        dattn, rest = rest[0], rest[1:]
    out_w, up_w, down_w, sems = rest
    down_copies = start_copies(downs, lambda r: down_w.at[r], sems, 8)
    up_copies = start_copies(ups, lambda r: up_w.at[r], sems, 4)
    out_copies = start_copies(
        outs, lambda r: out_w.at[r * LANES : (r + 1) * LANES, :], sems, 0
    )
    width = up_w.shape[2]
    total = gy.shape[0]
    for copy in down_copies + up_copies:
        copy.wait()

    @row_tiles(total, 256)
    def _(rows):
        dffn = gy[rows, :].astype(BF16)
        grad = jnp.zeros(gy[rows, :].shape, F32)
        for r in range(4):
            units = slice(r * width, (r + 1) * width)
            dup = (slope[rows, units].astype(F32) * nn(dffn, down_w[r])).astype(BF16)
            if with_weights:
                dup_out[rows, units] = dup
            grad = grad + nt(dup, up_w[r])
        grad_mid[rows, :] = grad

    if with_weights:
        sums[...] = jnp.zeros_like(sums)

    @row_tiles(total)
    def _(rows):
        unit, scale = normalise(mid[rows, :])
        grad = grad_mid[rows, :]
        if with_weights:
            sums[0:1, :] += jnp.sum(grad * unit, axis=0, keepdims=True)
            sums[1:2, :] += jnp.sum(grad, axis=0, keepdims=True)
        grad = gy[rows, :].astype(F32) + norm_backward(grad, unit, scale, gain[1:2, :])
        grad_mid[rows, :] = grad
        dattn[rows, :] = grad.astype(BF16)

    for copy in out_copies:
        copy.wait()

    row_a = lax.broadcasted_iota(jnp.int32, (LANES, LANES), 0) < E
    spread = (row_a == first_head((LANES, LANES))).astype(BF16)
    use_low = lax.broadcasted_iota(jnp.int32, (256, LANES), 1) % E >= E // 2

    @row_tiles(total, 256)
    def _(rows):
        grad_heads = nt(dattn[rows, :], out_w[...])
        scaled = grad_heads * inv_den[rows, :]
        dnum[rows, :] = scaled.astype(BF16)
        product = -scaled * o[rows, :].astype(F32)
        for pair in range(grad_state.shape[0]):
            lanes = slice(pair * LANES, (pair + 1) * LANES)
            part = product[:, lanes]
            high = part.astype(BF16)
            low = (part - high.astype(F32)).astype(BF16)
            whole = nn(high, spread) + nn(low, spread)
            high = whole.astype(BF16)
            low = (whole - high.astype(F32)).astype(BF16)
            dden[rows, lanes] = jnp.where(use_low, low, high)

    diag = diagonal_blocks()
    carry_in = cols[:, CARRY_IN : CARRY_IN + 1].astype(BF16)
    for pair in range(grad_state.shape[0]):
        lanes = slice(pair * LANES, (pair + 1) * LANES)
        both = jnp.concatenate([dnum[:, lanes], dden[:, lanes]], axis=1)
        grad_state[pair] = (diag * tn(fq[:, lanes] * carry_in, both)).astype(BF16)


def attention_back_kernel(
    with_weights, fq, fk, vv, dnum, dden, states, end, cols, seg, x, grad_mid, gain, bias,
    w0, w1, w2, w3, grad_x, dproj, *rest
):
    if with_weights:
        normed, sums = rest[0:2]
        rest = rest[2:]
    mask, mask_t, w, acc, sems = rest
    copies = start_copies(
        (w0, w1, w2, w3), lambda r: w.at[:, :, r * LANES : (r + 1) * LANES], sems, 0
    )
    chunk_masks(cols, seg, mask, mask_t)
    diag = diagonal_blocks()
    lane = lax.broadcasted_iota(jnp.int32, (1, PAIR), 1)
    share = jnp.where(lane < LANES, 1.0, SPLIT)

    @pl.loop(0, end.shape[0])
    def _(pair):
        lanes = pl.ds(pl.multiple_of(pair * LANES, LANES), LANES)
        grad_state = end[pair].astype(F32)
        for chunk in reversed(range(fq.shape[0] // CHUNK)):
            span = slice(chunk * CHUNK, (chunk + 1) * CHUNK)
            query, key, value = fq[span, lanes], fk[span, lanes], vv[span, lanes]
            grad_n, grad_d = dnum[span, lanes], dden[span, lanes]
            carried = cols[span, CARRIED : CARRIED + 1]
            tail = cols[span, TAIL : TAIL + 1]
            keep = carried[CHUNK - 1 : CHUNK, :]
            query_two = split_pair(query)
            grad_n_two = split_pair(grad_n)
            both = jnp.concatenate([grad_n, grad_d], axis=1)
            both_two = jnp.concatenate([grad_n_two, split_pair(grad_d)], axis=1)
            share_two = split_pair(jnp.full(value.shape, SPLIT, BF16))
            values_two = jnp.concatenate([split_pair(value), share_two], axis=1)
            values = side(value, SPLIT)
            scores_t = (nt(key, query_two) * mask_t[chunk]).astype(BF16)
            dscores = (nt(both, values_two) * mask[chunk]).astype(BF16)
            dscores_t = (nt(values, both_two) * mask_t[chunk]).astype(BF16)
            state = (states[pair, chunk].astype(F32) * share).astype(BF16)
            grad_low = grad_state.astype(BF16)
            dfq = nn(dscores, split_pair(key)) + carried * nt(both, state)
            dfk = nn(dscores_t, query_two) + tail * nt(values, grad_low)
            dvv = nn(scores_t, grad_n_two) + tail * nn(key, grad_low[:, :LANES])
            dproj[0, span, lanes] = (jnp.minimum(query.astype(F32), 1.0) * dfq).astype(BF16)
            dproj[1, span, lanes] = (jnp.minimum(key.astype(F32), 1.0) * dfk).astype(BF16)
            dproj[2, span, lanes] = dvv.astype(BF16)
            moved = diag * tn(query * carried.astype(BF16), both)
            grad_state = keep * grad_state + moved

    for copy in copies:
        copy.wait()

    @row_tiles(x.shape[0], 256)
    def _(rows):
        acc[rows, :] = (
            nt(dproj[0, rows, :], w[0]) + nt(dproj[1, rows, :], w[1]) + nt(dproj[2, rows, :], w[2])
        )

    if with_weights:
        sums[...] = jnp.zeros_like(sums)

    @row_tiles(x.shape[0])
    def _(rows):
        unit, scale = normalise(x[rows, :].astype(F32))
        grad = acc[rows, :]
        if with_weights:
            normed[rows, :] = (unit * gain[0:1, :] + bias[0:1, :]).astype(BF16)
            sums[0:1, :] += jnp.sum(grad * unit, axis=0, keepdims=True)
            sums[1:2, :] += jnp.sum(grad, axis=0, keepdims=True)
        grad = grad_mid[rows, :] + norm_backward(grad, unit, scale, gain[0:1, :])
        grad_x[rows, :] = grad.astype(BF16)


def down_grad_kernel(gy, active, keep, send, turned):
    turned[...] = gy[...].astype(BF16).T
    width = active.shape[1] // 4
    for r, (place, slot) in enumerate(((keep, 0), (send, 0), (keep, 1), (send, 1))):
        place[slot] = nn(turned[...], active[:, r * width : (r + 1) * width]).astype(BF16)


def up_grad_kernel(mid, gain, bias, dup, keep, send, normed_two, turned):
    @row_tiles(mid.shape[0])
    def _(rows):
        unit, _ = normalise(mid[rows, :])
        normed_two[rows, :] = (unit * gain[1:2, :] + bias[1:2, :]).astype(BF16)

    turned[...] = normed_two[...].T
    width = dup.shape[1] // 4
    for r, (place, slot) in enumerate(((keep, 0), (send, 0), (keep, 1), (send, 1))):
        place[slot] = nn(turned[...], dup[:, r * width : (r + 1) * width]).astype(BF16)


def late_grad_kernel(normed, dproj, o, dattn, sums_one, sums_two, keep, send, turned):
    width = normed.shape[1]
    base = 3 * width
    last = base + width
    places = ((keep, 0), (send, 0), (keep, 1), (send, 1))
    turned[...] = normed[...].T
    for c in range(3):
        whole = nn(turned[...], dproj[c]).astype(BF16)
        for r, (place, slot) in enumerate(places):
            place[slot, c * width : (c + 1) * width, :] = whole[:, r * LANES : (r + 1) * LANES]
    turned[...] = o[...].T
    for r, (place, slot) in enumerate(places):
        rows = slice(r * LANES, (r + 1) * LANES)
        whole = nn(turned[rows, :], dattn[...]).astype(BF16)
        for n in range(width // LANES):
            to = base + n * LANES
            place[slot, to : to + LANES, :] = whole[:, n * LANES : (n + 1) * LANES]
    four = (sums_one[0:1], sums_two[0:1], sums_one[1:2], sums_two[1:2])
    small = jnp.concatenate(
        [v[:, n * LANES : (n + 1) * LANES] for v in four for n in range(width // LANES)], axis=0
    ).astype(BF16)
    for place, slot in places:
        place[slot, last : last + small.shape[0], :] = small
        left = place.shape[1] - last - small.shape[0]
        place[slot, last + small.shape[0] :, :] = jnp.zeros((left, LANES), BF16)


IN_VMEM = pl.BlockSpec(memory_space=pltpu.VMEM)
ANYWHERE = pl.BlockSpec(memory_space=pl.ANY)


def call(kernel, operands, outputs, scratch, name, gflop, far=()):
    near = [jax.ShapeDtypeStruct(shape, dtype) for shape, dtype in outputs]
    moved = sum(v.size * v.dtype.itemsize for v in (*operands, *far))
    return pl.pallas_call(
        kernel,
        out_shape=near,
        in_specs=[IN_VMEM] * len(operands) + [ANYWHERE] * len(far),
        out_specs=[IN_VMEM] * len(near),
        scratch_shapes=scratch,
        compiler_params=pltpu.CompilerParams(vmem_limit_bytes=VMEM_LIMIT),
        cost_estimate=pl.CostEstimate(
            flops=int(gflop * 1e9), bytes_accessed=int(moved), transcendentals=0
        ),
        name=name,
    )(*operands, *far)


def across(block, distance, axis="head"):
    size = lax.axis_size(axis)
    return lax.ppermute(block, axis, [(i, i ^ distance) for i in range(size)])


def gather_shares(block):
    far = across(block, 2)
    return (block, across(block, 1), far, across(far, 1))


def reduce_shares(keep, send):
    came = across(send, 1)
    pair_sum = keep.astype(F32) + came.astype(F32)
    far = across(pair_sum[1].astype(BF16), 2)
    return (pair_sum[0] + far.astype(F32)).astype(BF16)


def token_table(segment_start, pad_mask, place, tokens, parts):
    row_count = segment_start.shape[0] // SEQ
    ids = jnp.cumsum(segment_start.reshape(row_count, SEQ), axis=1).reshape(-1)
    begin = place * tokens
    own = lax.dynamic_slice(ids, (begin,), (tokens,))
    before = lax.dynamic_slice(ids, (jnp.maximum(begin - 1, 0),), (1,))
    before = jnp.where(place % parts == 0, jnp.full_like(before, -1), before)
    last = own.reshape(-1, CHUNK)[:, -1]
    previous = jnp.concatenate([before, last[:-1]])
    pad = lax.dynamic_slice(pad_mask, (begin,), (tokens,))
    columns = [
        pad,
        own,
        own == before,
        own == last[-1:],
        own == jnp.repeat(previous, CHUNK),
        own == jnp.repeat(last, CHUNK),
    ]
    columns = jnp.stack([c.astype(F32) for c in columns], axis=1)
    rows = jnp.broadcast_to(own.astype(F32)[None], (8, tokens))
    return columns, rows


def local(
    block_input, cotangent, segment_start, pad_mask, qkv_weight, out_weight, up_weight,
    down_weight, norm_gain, norm_bias,
):
    heads = lax.axis_size("head")
    row_count = block_input.shape[0] // SEQ
    parts = heads // row_count
    assert heads == 4 and parts == 2
    tokens = block_input.shape[0] // heads
    width = block_input.shape[1]
    units = up_weight.shape[-1] * heads
    pairs = width // LANES
    chunks = tokens // CHUNK
    section = lax.axis_index("section")
    place = lax.axis_index("head")

    gain, bias = norm_gain[0], norm_bias[0]
    qkv = gather_shares(qkv_weight[0])
    out_w = gather_shares(out_weight[0])
    up_w = gather_shares(up_weight[0])
    down_w = gather_shares(down_weight[0])

    cols, seg = token_table(segment_start, pad_mask, place, tokens, parts)
    own_x = lax.dynamic_slice(block_input, (place * tokens, 0), (tokens, width))
    own_g = lax.dynamic_slice(cotangent, (place * tokens, 0), (tokens, width))

    wide = (tokens, width)
    state_shape = (pairs, LANES, PAIR)
    dma = pltpu.SemaphoreType.DMA
    mask_mem = pltpu.VMEM((chunks, CHUNK, PAIR), F32)
    qkv_mem = pltpu.VMEM((3, width, width), BF16)
    out_mem = pltpu.VMEM((width, width), BF16)
    ffn_mem = pltpu.VMEM((4, width, units // 4), BF16)
    row_mem = pltpu.VMEM(wide, BF16)

    def features(x, name):
        fq, fk, vv, state = call(
            qkv_kernel, (x, gain, bias, cols),
            [(wide, BF16)] * 3 + [(state_shape, BF16)],
            [qkv_mem, row_mem, dma((4,))], name, 0.9, far=qkv,
        )
        came = across(state, 1)
        start = came.reshape(2, 2, LANES, PAIR)[:, ::-1].reshape(state_shape)
        return fq, fk, vv, start

    fq, fk, vv, start = features(own_x, "qkv_first")
    mid, normed_two = call(
        attention_kernel, (fq, fk, vv, start, cols, seg, own_x, gain, bias),
        [(wide, F32), (wide, BF16)],
        [mask_mem, row_mem, out_mem, dma((4,))], "attention_first", 0.8, far=out_w,
    )
    (active,) = call(
        up_kernel, (normed_two, *up_w), [((tokens, units), BF16)], [], "up_first", 1.1
    )
    (y,) = call(down_kernel, (mid, active, *down_w), [(wide, BF16)], [], "down_first", 1.1)
    came = across(y, 1, "section")
    x = jnp.where(section == 0, own_x, came)

    fq, fk, vv, start = features(x, "qkv_second")
    y, mid, o, inv_den, states, active, slope = call(
        block_kernel, (fq, fk, vv, start, cols, seg, x, gain, bias),
        [
            (wide, BF16), (wide, F32), (wide, BF16), (wide, F32),
            ((pairs, chunks, LANES, PAIR), BF16), ((tokens, units), BF16), ((tokens, units), BF16),
        ],
        [mask_mem, row_mem, out_mem, ffn_mem, ffn_mem, dma((12,))],
        "block_second", 3.0, far=(*out_w, *up_w, *down_w),
    )
    activations = lax.all_gather(y, "head", tiled=True).astype(F32)
    token_rms = jnp.sqrt(jnp.mean(activations * activations, axis=-1) + 1e-06)

    def backward(gy, with_weights, name):
        extra = [((tokens, units), BF16), (wide, BF16), ((8, width), F32)] if with_weights else []
        grad_mid, dnum, dden, moved, *saved = call(
            functools.partial(ffn_back_kernel, with_weights),
            (gy, slope, mid, o, inv_den, fq, cols, gain),
            [(wide, F32), (wide, BF16), (wide, BF16), (state_shape, BF16)] + extra,
            ([] if with_weights else [row_mem]) + [out_mem, ffn_mem, ffn_mem, dma((12,))],
            "ffn_back" + name, 2.6, far=(*out_w, *up_w, *down_w),
        )
        came = across(moved, 1)
        end = came.reshape(2, 2, LANES, PAIR)[:, ::-1].reshape(state_shape)
        extra = [(wide, BF16), ((8, width), F32)] if with_weights else []
        grad_x, dproj, *saved_two = call(
            functools.partial(attention_back_kernel, with_weights),
            (fq, fk, vv, dnum, dden, states, end, cols, seg, x, grad_mid, gain, bias),
            [(wide, BF16), ((3, *wide), BF16)] + extra,
            [mask_mem, mask_mem, qkv_mem, pltpu.VMEM(wide, F32), dma((4,))],
            "attention_back" + name, 1.5, far=qkv,
        )
        return grad_x, dproj, saved, saved_two

    grad_x = backward(own_g, False, "_first")[0]
    came = across(grad_x, 1, "section")
    gy = jnp.where(section == 1, own_g, came.astype(F32))

    half = (2, width, units // 4)
    keep, send = call(
        down_grad_kernel, (gy, active), [(half, BF16)] * 2, [row_mem_t(width, tokens)], "down_grad", 1.1
    )
    down_total = reduce_shares(keep, send)
    grad_x, dproj, (dup, dattn, sums_two), (normed, sums_one) = backward(gy, True, "_second")
    keep, send = call(
        up_grad_kernel, (mid, gain, bias, dup), [(half, BF16)] * 2,
        [row_mem, row_mem_t(width, tokens)], "up_grad", 1.1,
    )
    up_total = reduce_shares(keep, send)
    late = 4 * width + 64
    keep, send = call(
        late_grad_kernel, (normed, dproj, o, dattn, sums_one, sums_two),
        [((2, late, LANES), BF16)] * 2, [row_mem_t(width, tokens)], "late_grad", 1.1,
    )
    late_total = reduce_shares(keep, send)
    input_grad = lax.all_gather(grad_x, "head", tiled=True).astype(F32)

    down_total = lax.psum(down_total, "dp").astype(F32)
    up_total = lax.psum(up_total, "dp").astype(F32)
    late_total = lax.psum(late_total, "dp").astype(F32)
    qkv_total = late_total[: 3 * width].reshape(3, width, LANES)
    out_total = late_total[3 * width : 4 * width].reshape(pairs, LANES, LANES)
    out_total = out_total.transpose(1, 0, 2).reshape(LANES, width)
    norm_total = late_total[4 * width : 4 * width + 4 * pairs].reshape(2, 2, width)
    return (
        activations[None], input_grad[None], token_rms[None], qkv_total[None], out_total[None],
        up_total[None], down_total[None], norm_total[0][None], norm_total[1][None],
    )


def row_mem_t(width, tokens):
    return pltpu.VMEM((width, tokens), BF16)


def solution(mesh):
    placed = (
        P("dp", None),
        P("dp", None),
        P("dp"),
        P("dp"),
        P("section", None, None, "head"),
        P("section", "head", None),
        P("section", None, "head"),
        P("section", None, "head"),
        P("section", None, None),
        P("section", None, None),
    )
    return jax.shard_map(
        local,
        mesh=mesh,
        in_specs=placed,
        out_specs=(
            P("section", "dp", None),
            P("section", "dp", None),
            P("section", "dp"),
            P("section", None, None, "head"),
            P("section", "head", None),
            P("section", None, "head"),
            P("section", None, "head"),
            P("section", None, None),
            P("section", None, None),
        ),
        check_vma=False,
    )
```

time: 1380 us -> 331 us (0.24); the launches traced: 1360 us -> 330 us
  waiting for transfers between devices: 621 us -> 148 us
  other arithmetic: 249 us -> 25.6 us
  matrix products: 216 us -> 0 us
  local copies, waits for them, and re-layouts: 226 us -> 19.9 us
  Pallas kernels: 0 us -> 103 us
    psum x20 -> x1, waiting for transfers between devices: 564 us -> 62.4 us  [local(): late_total = lax.psum(late_total, 'dp').astype(F32)]
    dot_general x148 -> x0, matrix products: 216 us -> none  [the longest x10 18.6 us: core_forward(): jnp.einsum('bhte,bhse->bhts', query_feat, key_feat, preferred_element_typ...]
    pallas_call x0 -> x13, Pallas kernels: none -> 103 us  [call(): pl.pallas_call(kernel, out_shape=near, in_specs=[IN_VMEM] * len(operands)...]
    reduce_sum x58 -> x0, other arithmetic: 86.6 us -> none  [the longest x15 40.7 us: layer_norm(): return shifted * lax.rsqrt(spread + EPS) * gain_vec + bias_vec]
    convert_element_type x40 -> x3, local copies, waits for them, and re-layouts: 41.4 us -> 0.19 us  [reduce_shares(): far = across(pair_sum[1].astype(BF16), 2)]
    convert_element_type x45 -> x1, other arithmetic: 41.8 us -> 0.94 us  [reduce_shares(): return (pair_sum[0] + far.astype(F32)).astype(BF16)]
    dynamic_update_slice x21 -> x0, other arithmetic: 40.8 us -> none  [write_block(): lax.dynamic_update_index_in_dim(buffer, jnp.where(is_valid, new_value, ol...]
    reshape x21 -> x0, local copies, waits for them, and re-layouts: 40.1 us -> none  [the longest x20 40.1 us: from_heads(): head_major.transpose(0, 2, 1, 3)]
  transfers between devices with their start and end apart: 28 -> 27, of which waited for: 27 -> 11; matrix products, arithmetic and copies ran while one was open for 19% -> 10% of each run, Pallas kernels for 0% -> 24%
where the time goes in v1:
time: 331 us; the launch traced here: 330 us
  waiting for transfers between devices  148 us (45%)
  Pallas kernels  103 us (31%)
  other arithmetic  25.6 us (8%)
  local copies, waits for them, and re-layouts  19.9 us (6%)
  starting transfers between devices  16.6 us (5%)
  between operations  16.5 us (5%)
    pallas_call x13, Pallas kernels, call(): pl.pallas_call(kernel, out_shape=near, in_specs=[IN_VMEM] * len(operands)...  103 us
    ppermute x24, waiting for transfers between devices, across(): return lax.ppermute(block, axis, [(i, i ^ distance) for i in range(size)])  85.7 us
    psum x1, waiting for transfers between devices, local(): late_total = lax.psum(late_total, 'dp').astype(F32)  62.4 us
    ppermute x24, starting transfers between devices, across(): return lax.ppermute(block, axis, [(i, i ^ distance) for i in range(size)])  16.1 us
  transfers between devices with their start and end apart: 27, of which 11 were waited for; matrix products, arithmetic and copies ran while one was open for 10% of the time, Pallas kernels for 24%

profile of v1, /device:TPU:0, one launch (start us, length us, event | category | flops | bytes accessed | tf_op | source)
XLA Modules:
  0.0 330.2 jit_solution(9598164675668037327)
XLA Ops:
  8.1 3.0 collective-permute-start.1
  11.2 1.9 collective-permute-start.8
  13.3 1.2 reduce-window.6
  15.0 0.6 dynamic_slice.18
  16.2 0.8 dynamic-slice_bitcast_fusion
  17.4 3.9 %collective-permute-done.1.w2 = bf16[3,512,128]{2,1,0:T(8,128)(2,1)S(1)} collective-permute-done((bf16[3,512,128]{2,1,0:T(8,128)(2,1)}, bf16[3,512,128]{2,1,0:T(8,128)(2,1)S(1)}, u32[]{:S(2)}, u32[]{:S(2)}) %collective-permute-start.1) | collective-permute-done | bytes 393248 | tf_op jit(solution)/shard_map/ppermute | solution.py:471
  21.9 0.7 fusion.13
  22.6 1.9 constant_dynamic-slice_fusion.1.x
  24.6 0.9 copy.34.cols
  25.9 9.3 %collective-permute-done.8.w2.rest_6_ = bf16[512,512]{1,0:T(8,128)(2,1)S(1)} collective-permute-done((bf16[512,512]{1,0:T(8,128)(2,1)}, bf16[512,512]{1,0:T(8,128)(2,1)S(1)}, u32[]{:S(2)}, u32[]{:S(2)}) %collective-permute-start.8) | collective-permute-done | bytes 524320 | tf_op jit(solution)/shard_map/ppermute | solution.py:471
  35.8 5.0 %qkv_first.1 = (bf16[512,512]{1,0:T(8,128)(2,1)}, bf16[512,512]{1,0:T(8,128)(2,1)}, bf16[512,512]{1,0:T(8,128)(2,1)}, bf16[4,128,256]{2,1,0:T(8,128)(2,1)}) custom-call(bf16[512,512]{1,0:T(8,128)(2,1)} %constant_dynamic-slice_fusion.1.x, f32[2,512]{1,0:T(2,128)} %bitcast.113, f32[2,512]{1,0:T(2,128)} %bitcast.122, f32[512,6]{1,0:T(8,128)} %copy.34.cols, ...), custom_call_target="tpu_custom_call" | custom-call | flops 900000000 | bytes 2117632 | tf_op jit(solution)/shard_map/qkv_first/pallas_call | solution.py:455
  41.4 4.2 %collective-permute-done.11.w2.rest_10_ = bf16[512,512]{1,0:T(8,128)(2,1)S(1)} collective-permute-done((bf16[512,512]{1,0:T(8,128)(2,1)}, bf16[512,512]{1,0:T(8,128)(2,1)S(1)}, u32[]{:S(2)}, u32[]{:S(2)}) %collective-permute-start.11) | collective-permute-done | bytes 524320 | tf_op jit(solution)/shard_map/ppermute | solution.py:471
  45.7 0.7 copy-done.17
  46.9 1.7 rev.12
  48.6 0.6 broadcast_in_dim.36.seg
  49.2 7.8 %attention_first.1 = (f32[512,512]{1,0:T(8,128)}, bf16[512,512]{1,0:T(8,128)(2,1)}) custom-call(bf16[512,512]{1,0:T(8,128)(2,1)} %get-tuple-element.48.fq, bf16[512,512]{1,0:T(8,128)(2,1)} %get-tuple-element.49.fk, bf16[512,512]{1,0:T(8,128)(2,1)} %get-tuple-element.50.vv, bf16[4,128,256]{2,1,0:T(8,128)(2,1)} %bitcast.104, f32[512,6]{1,0:T(8,128)} %copy.34.cols, ...), custom_call_target="tpu_custom_call" | custom-call | flops 800000000 | bytes 2920448 | tf_op jit(solution)/shard_map/attention_first/pallas_call | solution.py:455
  57.1 0.8 copy-done.2
  58.0 6.2 %up_first.1.active = bf16[512,2048]{1,0:T(8,128)(2,1)} custom-call(bf16[512,512]{1,0:T(8,128)(2,1)} %get-tuple-element.53.normed_two, bf16[512,512]{1,0:T(8,128)(2,1)} %bitcast.81, bf16[512,512]{1,0:T(8,128)(2,1)} %copy-done.2, bf16[512,512]{1,0:T(8,128)(2,1)} %copy-done.1, bf16[512,512]{1,0:T(8,128)(2,1)} %copy-done.3), custom_call_target="tpu_custom_call" | custom-call | flops 1100000000 | bytes 2621440 | tf_op jit(solution)/shard_map/up_first/pallas_call | solution.py:455
  64.3 0.8 copy-done.6
  65.1 4.7 %down_first.1 = bf16[512,512]{1,0:T(8,128)(2,1)} custom-call(f32[512,512]{1,0:T(8,128)} %get-tuple-element.52.mid, bf16[512,2048]{1,0:T(8,128)(2,1)} %up_first.1.active, bf16[512,512]{1,0:T(8,128)(2,1)} %bitcast.86, bf16[512,512]{1,0:T(8,128)(2,1)} %copy-done.6, bf16[512,512]{1,0:T(8,128)(2,1)} %copy-done.5, bf16[512,512]{1,0:T(8,128)(2,1)} %collective-permute-done.12.w3.rest_11_), custom_call_target="tpu_custom_call" | custom-call | flops 1100000000 | bytes 5242880 | tf_op jit(solution)/shard_map/down_first/pallas_call | solution.py:455
  69.8 1.8 collective-permute-start.13
  71.6 12.4 %collective-permute-done.13 = bf16[512,512]{1,0:T(8,128)(2,1)S(1)} collective-permute-done((bf16[512,512]{1,0:T(8,128)(2,1)}, bf16[512,512]{1,0:T(8,128)(2,1)S(1)}, u32[]{:S(2)}, u32[]{:S(2)}) %collective-permute-start.13) | collective-permute-done | bytes 524320 | tf_op jit(solution)/shard_map/ppermute | solution.py:471
  83.9 2.0 broadcast_select_fusion.x
  85.9 5.0 %qkv_second.1 = (bf16[512,512]{1,0:T(8,128)(2,1)}, bf16[512,512]{1,0:T(8,128)(2,1)}, bf16[512,512]{1,0:T(8,128)(2,1)}, bf16[4,128,256]{2,1,0:T(8,128)(2,1)}) custom-call(bf16[512,512]{1,0:T(8,128)(2,1)} %broadcast_select_fusion.x, f32[2,512]{1,0:T(2,128)} %bitcast.115, f32[2,512]{1,0:T(2,128)} %bitcast.124, f32[512,6]{1,0:T(8,128)} %copy.34.cols, ...), custom_call_target="tpu_custom_call" | custom-call | flops 900000000 | bytes 2117632 | tf_op jit(solution)/shard_map/qkv_second/pallas_call | solution.py:455
  90.9 1.7 collective-permute-done.14
  92.7 0.7 rev.13
  93.4 14.0 %block_second.1 = (bf16[512,512]{1,0:T(8,128)(2,1)}, f32[512,512]{1,0:T(8,128)}, bf16[512,512]{1,0:T(8,128)(2,1)}, f32[512,512]{1,0:T(8,128)}, bf16[4,4,128,256]...) custom-call(bf16[512,512]{1,0:T(8,128)(2,1)} %get-tuple-element.54.fq, ...), custom_call_target="tpu_custom_call" | custom-call | flops 3000000000 | bytes 7114752 | tf_op jit(solution)/shard_map/block_second/pallas_call | solution.py:455
  107.6 2.3 constant_dynamic-slice_fusion.gy
  109.9 11.7 %ffn_back_first.1 = (f32[512,512]{1,0:T(8,128)}, bf16[512,512]{1,0:T(8,128)(2,1)}, bf16[512,512]{1,0:T(8,128)(2,1)}, bf16[4,128,256]{2,1,0:T(8,128)(2,1)}) custom-call(f32[512,512]{1,0:T(8,128)} %constant_dynamic-slice_fusion.gy, bf16[512,2048]{1,0:T(8,128)(2,1)} %get-tuple-element.59.slope, f32[512,512]{1,0:T(8,128)} %get-tuple-element.60.mid, ...), custom_call_target="tpu_custom_call" | custom-call | flops 2600000000 | bytes 11026432 | tf_op jit(solution)/shard_map/ffn_back_first/pallas_call | solution.py:455
  121.7 1.7 collective-permute-done.15
  123.4 0.7 rev.14
  124.1 11.2 %attention_back_first.1 = (bf16[512,512]{1,0:T(8,128)(2,1)}, bf16[3,512,512]{2,1,0:T(8,128)(2,1)}) custom-call(bf16[512,512]{1,0:T(8,128)(2,1)} %get-tuple-element.54.fq, bf16[512,512]{1,0:T(8,128)(2,1)} %get-tuple-element.55.fk, bf16[512,512]{1,0:T(8,128)(2,1)} %get-tuple-element.56.vv, bf16[512,512]{1,0:T(8,128)(2,1)} %get-tuple-element.63.dnum, ...), custom_call_target="tpu_custom_call" | custom-call | flops 1500000000 | bytes 7114752 | tf_op jit(solution)/shard_map/attention_back_first/pallas_call | solution.py:455
  135.3 1.8 collective-permute-start.16
  137.1 12.5 %collective-permute-done.16 = bf16[512,512]{1,0:T(8,128)(2,1)S(1)} collective-permute-done((bf16[512,512]{1,0:T(8,128)(2,1)}, bf16[512,512]{1,0:T(8,128)(2,1)S(1)}, u32[]{:S(2)}, u32[]{:S(2)}) %collective-permute-start.16) | collective-permute-done | bytes 524320 | tf_op jit(solution)/shard_map/ppermute | solution.py:471
  149.6 2.4 convert_select_fusion.gy
  151.9 4.3 %down_grad.1 = (bf16[2,512,512]{2,1,0:T(8,128)(2,1)}, bf16[2,512,512]{2,1,0:T(8,128)(2,1)}) custom-call(f32[512,512]{1,0:T(8,128)} %convert_select_fusion.gy, bf16[512,2048]{1,0:T(8,128)(2,1)} %get-tuple-element.84.active), custom_call_target="tpu_custom_call" | custom-call | flops 1100000000 | bytes 3145728 | tf_op jit(solution)/shard_map/down_grad/pallas_call | solution.py:455
  156.3 12.4 %ffn_back_second.1 = (f32[512,512]{1,0:T(8,128)}, bf16[512,512]{1,0:T(8,128)(2,1)}, bf16[512,512]{1,0:T(8,128)(2,1)}, bf16[4,128,256]{2,1,0:T(8,128)(2,1)}, bf16...) custom-call(f32[512,512]{1,0:T(8,128)} %convert_select_fusion.gy, ...), custom_call_target="tpu_custom_call" | custom-call | flops 2600000000 | bytes 11026432 | tf_op jit(solution)/shard_map/ffn_back_second/pallas_call | solution.py:455
  169.2 5.2 %up_grad.1 = (bf16[2,512,512]{2,1,0:T(8,128)(2,1)}, bf16[2,512,512]{2,1,0:T(8,128)(2,1)}) custom-call(f32[512,512]{1,0:T(8,128)} %get-tuple-element.60.mid, f32[2,512]{1,0:T(2,128)} %bitcast.120, f32[2,512]{1,0:T(2,128)} %bitcast.127, bf16[512,2048]{1,0:T(8,128)(2,1)} %get-tuple-element.81.dup), custom_call_target="tpu_custom_call" | custom-call | flops 1100000000 | bytes 3153920 | tf_op jit(solution)/shard_map/up_grad/pallas_call | solution.py:455
  174.4 0.7 rev.15
  175.1 11.5 %attention_back_second.1 = (bf16[512,512]{1,0:T(8,128)(2,1)}, bf16[3,512,512]{2,1,0:T(8,128)(2,1)}, bf16[512,512]{1,0:T(8,128)(2,1)}, f32[8,512]{1,0:T(8,128)}) custom-call(bf16[512,512]{1,0:T(8,128)(2,1)} %get-tuple-element.54.fq, bf16[512,512]{1,0:T(8,128)(2,1)} %get-tuple-element.55.fk, bf16[512,512]{1,0:T(8,128)(2,1)} %get-tuple-element.56.vv, ...), custom_call_target="tpu_custom_call" | custom-call | flops 1500000000 | bytes 7114752 | tf_op jit(solution)/shard_map/attention_back_second/pallas_call | solution.py:455
  186.7 4.5 %late_grad.1 = (bf16[2,2112,128]{2,1,0:T(8,128)(2,1)}, bf16[2,2112,128]{2,1,0:T(8,128)(2,1)}) custom-call(bf16[512,512]{1,0:T(8,128)(2,1)} %get-tuple-element.74.normed, bf16[3,512,512]{2,1,0:T(8,128)(2,1)} %get-tuple-element.75.dproj, bf16[512,512]{1,0:T(8,128)(2,1)} %get-tuple-element.61.o, bf16[512,512]{1,0:T(8,128)(2,1)} %get-tuple-element.76.dattn, ...), custom_call_target="tpu_custom_call" | custom-call | flops 1100000000 | bytes 3178496 | tf_op jit(solution)/shard_map/late_grad/pallas_call | solution.py:455
  192.0 1.6 convert_add_fusion.1
  193.7 1.8 collective-permute-start.23
  195.5 1.6 convert_add_fusion.2
  197.9 1.8 collective-permute-start.19
  199.7 14.7 %collective-permute-done.23 = bf16[512,512]{1,0:T(8,128)(2,1)S(1)} collective-permute-done((bf16[512,512]{1,0:T(8,128)(2,1)S(1)}, bf16[512,512]{1,0:T(8,128)(2,1)S(1)}, u32[]{:S(2)}, u32[]{:S(2)}) %collective-permute-start.23) | collective-permute-done | bytes 524320 | tf_op jit(solution)/shard_map/ppermute | solution.py:471
  214.4 1.0 fusion.10
  215.4 15.6 %collective-permute-done.21 = bf16[512,512]{1,0:T(8,128)(2,1)S(1)} collective-permute-done((bf16[512,512]{1,0:T(8,128)(2,1)S(1)}, bf16[512,512]{1,0:T(8,128)(2,1)S(1)}, u32[]{:S(2)}, u32[]{:S(2)}) %collective-permute-start.21) | collective-permute-done | bytes 524320 | tf_op jit(solution)/shard_map/ppermute | solution.py:471
  231.0 1.0 fusion.8
  232.0 9.7 %collective-permute-done.19 = bf16[2112,128]{1,0:T(8,128)(2,1)S(1)} collective-permute-done((bf16[2112,128]{1,0:T(8,128)(2,1)S(1)}, bf16[2112,128]{1,0:T(8,128)(2,1)S(1)}, u32[]{:S(2)}, u32[]{:S(2)}) %collective-permute-start.19) | collective-permute-done | bytes 540704 | tf_op jit(solution)/shard_map/ppermute | solution.py:471
  241.7 0.9 fusion.2
  242.7 2.2 fusion
  244.9 0.6 add_sqrt_fusion
  245.5 2.6 convert_bitcast_fusion
  248.1 4.2 %bitcast_convert_fusion = f32[1,2048,512]{2,1,0:T(8,128)} fusion(bf16[2048,512]{1,0:T(8,128)(2,1)} %all-gather.5.cloned.1.call-done), kind=kLoop, calls=%fused_computation.4 | loop fusion | flops 1048576 | bytes 6291456 | tf_op jit(solution)/shard_map/broadcast_in_dim | solution.py:632
  252.3 62.4 %all-reduce.3.cloned.1.call-done = (bf16[2112,128]{1,0:T(8,128)(2,1)}, bf16[1,512,512]{2,1,0:T(8,128)(2,1)}, bf16[1,512,512]{2,1,0:T(8,128)(2,1)}) async-done(((bf16[2112,128]{1,0:T(8,128)(2,1)}, bf16[1,512,512]{2,1,0:T(8,128)(2,1)}, bf16[1,512,512]{2,1,0:T(8,128)(2,1)}), (bf16[2112,128]{1,0:T(8,128)(2,1)}, bf16[1,512,512]{2,1,0:T(8,128)(2,1)}, bf16[1,512,512]{2,1,0:T(8,128)(2,1)})) %all-reduce.3.cloned.1.call-update) | async-done | bytes 1589264 | tf_op jit(solution)/shard_map/psum | solution.py:626
  314.7 2.0 slice.84
  316.7 0.9 slice.85
  317.7 0.7 fusion.14
  318.3 1.1 broadcast_in_dim.41
  319.4 1.1 broadcast_in_dim.43
  320.7 0.8 broadcast_in_dim_reshape.7
  321.5 0.6 slice.78
  322.1 0.6 slice.80
  (86 shorter events, 7.2 us)
Async XLA Ops:
  8.0 234.6 %all-gather.3.cloned.1.call-start = ((), (), s32[]{:S(2)}) async-start(), calls=%async_computation | async-start | bytes 2621440 | tf_op jit(solution)/shard_map/all_gather | solution.py:577
  8.1 13.2 %collective-permute-start.1 = (bf16[3,512,128]{2,1,0:T(8,128)(2,1)}, bf16[3,512,128]{2,1,0:T(8,128)(2,1)S(1)}, u32[]{:S(2)}, u32[]{:S(2)}) collective-permute-start(bf16[3,512,128]{2,1,0:T(8,128)(2,1)} %bitcast.91), channel_id=1, source_target_pairs={{0,2},{1,3},{2,0},{3,1},{4,6},{5,7},{6,4},{7,5},{8,10},{9,11},{10,... | collective-permute-start | bytes 1179656 | tf_op jit(solution)/shard_map/ppermute | solution.py:471
  11.1 14.4 %collective-permute-start = (bf16[3,512,128]{2,1,0:T(8,128)(2,1)}, bf16[3,512,128]{2,1,0:T(8,128)(2,1)S(1)}, u32[]{:S(2)}, u32[]{:S(2)}) collective-permute-start(bf16[3,512,128]{2,1,0:T(8,128)(2,1)} %bitcast.92), channel_id=1, source_target_pairs={{0,1},{1,0},{2,3},{3,2},{4,5},{5,4},{6,7},{7,6},{8,9},{9,8},{10,11... | collective-permute-start | bytes 1179656 | tf_op jit(solution)/shard_map/ppermute | solution.py:471
  11.1 29.7 %collective-permute-start.5 = (bf16[128,512]{1,0:T(8,128)(2,1)}, bf16[128,512]{1,0:T(8,128)(2,1)S(1)}, u32[]{:S(2)}, u32[]{:S(2)}) collective-permute-start(bf16[128,512]{1,0:T(8,128)(2,1)} %bitcast.97), channel_id=1, source_target_pairs={{0,2},{1,3},{2,0},{3,1},{4,6},{5,7},{6,4},{7,5},{8,10},{9,11},{10,... | collective-permute-start | bytes 393224 | tf_op jit(solution)/shard_map/ppermute | solution.py:471
  11.2 24.0 %collective-permute-start.8 = (bf16[512,512]{1,0:T(8,128)(2,1)}, bf16[512,512]{1,0:T(8,128)(2,1)S(1)}, u32[]{:S(2)}, u32[]{:S(2)}) collective-permute-start(bf16[512,512]{1,0:T(8,128)(2,1)} %bitcast.79), channel_id=1, source_target_pairs={{0,2},{1,3},{2,0},{3,1},{4,6},{5,7},{6,4},{7,5},{8,10},{9,11},{10,... | collective-permute-start | bytes 1572872 | tf_op jit(solution)/shard_map/ppermute | solution.py:471
  13.1 32.6 %collective-permute-start.11 = (bf16[512,512]{1,0:T(8,128)(2,1)}, bf16[512,512]{1,0:T(8,128)(2,1)S(1)}, u32[]{:S(2)}, u32[]{:S(2)}) collective-permute-start(bf16[512,512]{1,0:T(8,128)(2,1)} %bitcast.85), channel_id=1, source_target_pairs={{0,2},{1,3},{2,0},{3,1},{4,6},{5,7},{6,4},{7,5},{8,10},{9,11},{10,... | collective-permute-start | bytes 1572872 | tf_op jit(solution)/shard_map/ppermute | solution.py:471
  21.2 14.6 %copy-start.7 = (bf16[3,512,128]{2,1,0:T(8,128)(2,1)}, bf16[3,512,128]{2,1,0:T(8,128)(2,1)S(1)}, u32[]{:S(2)}) copy-start(bf16[3,512,128]{2,1,0:T(8,128)(2,1)S(1)} %collective-permute-done.1.w2) | copy-start | bytes 1179652
  21.2 14.1 %collective-permute-start.2 = (bf16[3,512,128]{2,1,0:T(8,128)(2,1)S(1)}, bf16[3,512,128]{2,1,0:T(8,128)(2,1)}, u32[]{:S(2)}, u32[]{:S(2)}) collective-permute-start(bf16[3,512,128]{2,1,0:T(8,128)(2,1)S(1)} %collective-permute-done.1.w2), channel_id=1, source_target_pairs={{0,1},{1,0},{2,3},{3,2},{4,5},{5,4},{6,7},{7,6},{8,9},{9,8},{10,11... | collective-permute-start | bytes 1179656 | tf_op jit(solution)/shard_map/ppermute | solution.py:471
  22.6 18.3 %copy-start.4 = (bf16[1,512,512]{2,1,0:T(8,128)(2,1)S(1)}, bf16[1,512,512]{2,1,0:T(8,128)(2,1)}, u32[]{:S(2)}) copy-start(bf16[1,512,512]{2,1,0:T(8,128)(2,1)} %param.17) | copy-start | bytes 1572868
  25.4 10.4 %copy-start.8 = (bf16[3,512,128]{2,1,0:T(8,128)(2,1)}, bf16[3,512,128]{2,1,0:T(8,128)(2,1)S(1)}, u32[]{:S(2)}) copy-start(bf16[3,512,128]{2,1,0:T(8,128)(2,1)S(1)} %collective-permute-done.w1) | copy-start | bytes 1179652
  25.4 15.5 %collective-permute-start.4 = (bf16[128,512]{1,0:T(8,128)(2,1)}, bf16[128,512]{1,0:T(8,128)(2,1)S(1)}, u32[]{:S(2)}, u32[]{:S(2)}) collective-permute-start(bf16[128,512]{1,0:T(8,128)(2,1)} %bitcast.98), channel_id=1, source_target_pairs={{0,1},{1,0},{2,3},{3,2},{4,5},{5,4},{6,7},{7,6},{8,9},{9,8},{10,11... | collective-permute-start | bytes 393224 | tf_op jit(solution)/shard_map/ppermute | solution.py:471
  35.3 21.8 %copy-start.1 = (bf16[512,512]{1,0:T(8,128)(2,1)}, bf16[512,512]{1,0:T(8,128)(2,1)S(1)}, u32[]{:S(2)}) copy-start(bf16[512,512]{1,0:T(8,128)(2,1)S(1)} %collective-permute-done.8.w2.rest_6_) | copy-start | bytes 1572868
  35.3 21.8 %collective-permute-start.7 = (bf16[512,512]{1,0:T(8,128)(2,1)}, bf16[512,512]{1,0:T(8,128)(2,1)S(1)}, u32[]{:S(2)}, u32[]{:S(2)}) collective-permute-start(bf16[512,512]{1,0:T(8,128)(2,1)} %bitcast.80), channel_id=1, source_target_pairs={{0,1},{1,0},{2,3},{3,2},{4,5},{5,4},{6,7},{7,6},{8,9},{9,8},{10,11... | collective-permute-start | bytes 1572872 | tf_op jit(solution)/shard_map/ppermute | solution.py:471
  35.3 21.8 %collective-permute-start.9 = (bf16[512,512]{1,0:T(8,128)(2,1)S(1)}, bf16[512,512]{1,0:T(8,128)(2,1)S(1)}, u32[]{:S(2)}, u32[]{:S(2)}) collective-permute-start(bf16[512,512]{1,0:T(8,128)(2,1)S(1)} %collective-permute-done.8.w2.rest_6_), channel_id=1, source_target_pairs={{0,1},{1,0},{2,3},{3,2},{4,5},{5,4},{6,7},{7,6},{8,9},{9,8},{10,11... | collective-permute-start | bytes 1572872 | tf_op jit(solution)/shard_map/ppermute | solution.py:471
  40.8 8.5 %copy-start.9 = (bf16[128,512]{1,0:T(8,128)(2,1)}, bf16[128,512]{1,0:T(8,128)(2,1)S(1)}, u32[]{:S(2)}) copy-start(bf16[128,512]{1,0:T(8,128)(2,1)S(1)} %collective-permute-done.5.w2.rest_2_) | copy-start | bytes 393220
  40.8 4.9 %collective-permute-start.3 = (bf16[4,128,256]{2,1,0:T(8,128)(2,1)}, bf16[4,128,256]{2,1,0:T(8,128)(2,1)S(1)}, u32[]{:S(2)}, u32[]{:S(2)}) collective-permute-start(bf16[4,128,256]{2,1,0:T(8,128)(2,1)} %get-tuple-element.51), channel_id=1, source_target_pairs={{0,1},{1,0},{2,3},{3,2},{4,5},{5,4},{6,7},{7,6},{8,9},{9,8},{10,11... | collective-permute-start | bytes 786440 | tf_op jit(solution)/shard_map/ppermute | solution.py:471
  40.9 4.8 %copy-start.10 = (bf16[128,512]{1,0:T(8,128)(2,1)}, bf16[128,512]{1,0:T(8,128)(2,1)S(1)}, u32[]{:S(2)}) copy-start(bf16[128,512]{1,0:T(8,128)(2,1)S(1)} %collective-permute-done.4.w1.rest_1_) | copy-start | bytes 393220
  40.9 23.4 %collective-permute-start.10 = (bf16[512,512]{1,0:T(8,128)(2,1)S(1)}, bf16[512,512]{1,0:T(8,128)(2,1)S(1)}, u32[]{:S(2)}, u32[]{:S(2)}) collective-permute-start(bf16[512,512]{1,0:T(8,128)(2,1)S(1)} %bitcast.90), channel_id=1, source_target_pairs={{0,1},{1,0},{2,3},{3,2},{4,5},{5,4},{6,7},{7,6},{8,9},{9,8},{10,11... | collective-permute-start | bytes 1572872 | tf_op jit(solution)/shard_map/ppermute | solution.py:471
  45.7 18.6 %copy-start.5 = (bf16[512,512]{1,0:T(8,128)(2,1)}, bf16[512,512]{1,0:T(8,128)(2,1)S(1)}, u32[]{:S(2)}) copy-start(bf16[512,512]{1,0:T(8,128)(2,1)S(1)} %collective-permute-done.11.w2.rest_10_) | copy-start | bytes 1572868
  45.7 18.6 %collective-permute-start.12 = (bf16[512,512]{1,0:T(8,128)(2,1)S(1)}, bf16[512,512]{1,0:T(8,128)(2,1)}, u32[]{:S(2)}, u32[]{:S(2)}) collective-permute-start(bf16[512,512]{1,0:T(8,128)(2,1)S(1)} %collective-permute-done.11.w2.rest_10_), channel_id=1, source_target_pairs={{0,1},{1,0},{2,3},{3,2},{4,5},{5,4},{6,7},{7,6},{8,9},{9,8},{10,11... | collective-permute-start | bytes 1572872 | tf_op jit(solution)/shard_map/ppermute | solution.py:471
  45.7 0.8 copy-start.17
  46.4 2.1 collective-permute-start.6
  48.6 0.7 copy-start.11
  57.0 0.8 copy-start.2
  57.1 1.0 copy-start.3
  64.3 0.8 copy-start.6
  69.8 14.1 %collective-permute-start.13 = (bf16[512,512]{1,0:T(8,128)(2,1)}, bf16[512,512]{1,0:T(8,128)(2,1)S(1)}, u32[]{:S(2)}, u32[]{:S(2)}) collective-permute-start(bf16[512,512]{1,0:T(8,128)(2,1)} %down_first.1), channel_id=1, source_target_pairs={{0,16},{16,0},{1,17},{17,1},{2,18},{18,2},{3,19},{19,3},{4,20},{20... | collective-permute-start | bytes 1572872 | tf_op jit(solution)/shard_map/ppermute | solution.py:471
  90.9 1.8 collective-permute-start.14
  107.4 140.7 %all-gather.5.cloned.1.call-start = ((), (), s32[]{:S(2)}) async-start(), calls=%async_computation.1 | async-start | bytes 2621440 | tf_op jit(solution)/shard_map/all_gather | solution.py:622
  121.5 1.8 collective-permute-start.15
  135.3 14.2 %collective-permute-start.16 = (bf16[512,512]{1,0:T(8,128)(2,1)}, bf16[512,512]{1,0:T(8,128)(2,1)S(1)}, u32[]{:S(2)}, u32[]{:S(2)}) collective-permute-start(bf16[512,512]{1,0:T(8,128)(2,1)} %get-tuple-element.68), channel_id=1, source_target_pairs={{0,16},{16,0},{1,17},{17,1},{2,18},{18,2},{3,19},{19,3},{4,20},{20... | collective-permute-start | bytes 1572872 | tf_op jit(solution)/shard_map/ppermute | solution.py:471
  156.3 35.7 %collective-permute-start.22 = (bf16[2,512,512]{2,1,0:T(8,128)(2,1)}, bf16[2,512,512]{2,1,0:T(8,128)(2,1)}, u32[]{:S(2)}, u32[]{:S(2)}) collective-permute-start(bf16[2,512,512]{2,1,0:T(8,128)(2,1)} %get-tuple-element.86), channel_id=1, source_target_pairs={{0,1},{1,0},{2,3},{3,2},{4,5},{5,4},{6,7},{7,6},{8,9},{9,8},{10,11... | collective-permute-start | bytes 3145736 | tf_op jit(solution)/shard_map/ppermute | solution.py:471
  168.6 5.8 %collective-permute-start.17 = (bf16[4,128,256]{2,1,0:T(8,128)(2,1)}, bf16[4,128,256]{2,1,0:T(8,128)(2,1)S(1)}, u32[]{:S(2)}, u32[]{:S(2)}) collective-permute-start(bf16[4,128,256]{2,1,0:T(8,128)(2,1)} %get-tuple-element.71), channel_id=1, source_target_pairs={{0,1},{1,0},{2,3},{3,2},{4,5},{5,4},{6,7},{7,6},{8,9},{9,8},{10,11... | collective-permute-start | bytes 786440 | tf_op jit(solution)/shard_map/ppermute | solution.py:471
  174.4 21.1 %collective-permute-start.20 = (bf16[2,512,512]{2,1,0:T(8,128)(2,1)}, bf16[2,512,512]{2,1,0:T(8,128)(2,1)}, u32[]{:S(2)}, u32[]{:S(2)}) collective-permute-start(bf16[2,512,512]{2,1,0:T(8,128)(2,1)} %get-tuple-element.83), channel_id=1, source_target_pairs={{0,1},{1,0},{2,3},{3,2},{4,5},{5,4},{6,7},{7,6},{8,9},{9,8},{10,11... | collective-permute-start | bytes 3145736 | tf_op jit(solution)/shard_map/ppermute | solution.py:471
  186.6 5.3 %copy-start.13 = (bf16[2,512,512]{2,1,0:T(8,128)(2,1)S(1)}, bf16[2,512,512]{2,1,0:T(8,128)(2,1)}, u32[]{:S(2)}) copy-start(bf16[2,512,512]{2,1,0:T(8,128)(2,1)} %get-tuple-element.85) | copy-start | bytes 3145732
  191.2 6.4 %collective-permute-start.18 = (bf16[2,2112,128]{2,1,0:T(8,128)(2,1)}, bf16[2,2112,128]{2,1,0:T(8,128)(2,1)S(1)}, u32[]{:S(2)}, u32[]{:S(2)}) collective-permute-start(bf16[2,2112,128]{2,1,0:T(8,128)(2,1)} %get-tuple-element.80), channel_id=1, source_target_pairs={{0,1},{1,0},{2,3},{3,2},{4,5},{5,4},{6,7},{7,6},{8,9},{9,8},{10,11... | collective-permute-start | bytes 3244040 | tf_op jit(solution)/shard_map/ppermute | solution.py:471
  191.7 123.0 %all-reduce.3.cloned.1.call-start = ((), (), s32[]{:S(2)}) async-start(), calls=%async_computation.2 | async-start | bytes 3178496 | tf_op jit(solution)/shard_map/psum | solution.py:626
  192.0 3.5 %copy-start.14 = (bf16[2,512,512]{2,1,0:T(8,128)(2,1)S(1)}, bf16[2,512,512]{2,1,0:T(8,128)(2,1)}, u32[]{:S(2)}) copy-start(bf16[2,512,512]{2,1,0:T(8,128)(2,1)} %get-tuple-element.82) | copy-start | bytes 3145732
  193.7 20.7 %collective-permute-start.23 = (bf16[512,512]{1,0:T(8,128)(2,1)S(1)}, bf16[512,512]{1,0:T(8,128)(2,1)S(1)}, u32[]{:S(2)}, u32[]{:S(2)}) collective-permute-start(bf16[512,512]{1,0:T(8,128)(2,1)S(1)} %fusion.11), channel_id=1, source_target_pairs={{0,2},{1,3},{2,0},{3,1},{4,6},{5,7},{6,4},{7,5},{8,10},{9,11},{10,... | collective-permute-start | bytes 1572872 | tf_op jit(solution)/shard_map/ppermute | solution.py:471
  195.5 2.1 copy-start.12
  197.2 33.8 %collective-permute-start.21 = (bf16[512,512]{1,0:T(8,128)(2,1)S(1)}, bf16[512,512]{1,0:T(8,128)(2,1)S(1)}, u32[]{:S(2)}, u32[]{:S(2)}) collective-permute-start(bf16[512,512]{1,0:T(8,128)(2,1)S(1)} %fusion.9), channel_id=1, source_target_pairs={{0,2},{1,3},{2,0},{3,1},{4,6},{5,7},{6,4},{7,5},{8,10},{9,11},{10,... | collective-permute-start | bytes 1572872 | tf_op jit(solution)/shard_map/ppermute | solution.py:471
  197.9 43.8 %collective-permute-start.19 = (bf16[2112,128]{1,0:T(8,128)(2,1)S(1)}, bf16[2112,128]{1,0:T(8,128)(2,1)S(1)}, u32[]{:S(2)}, u32[]{:S(2)}) collective-permute-start(bf16[2112,128]{1,0:T(8,128)(2,1)S(1)} %fusion.7), channel_id=1, source_target_pairs={{0,2},{1,3},{2,0},{3,1},{4,6},{5,7},{6,4},{7,5},{8,10},{9,11},{10,... | collective-permute-start | bytes 1622024 | tf_op jit(solution)/shard_map/ppermute | solution.py:471
  242.6 2.8 copy-start
  314.7 3.6 %copy-start.16 = (bf16[1,512,512]{2,1,0:T(8,128)(2,1)S(1)}, bf16[1,512,512]{2,1,0:T(8,128)(2,1)}, u32[]{:S(2)}) copy-start(bf16[1,512,512]{2,1,0:T(8,128)(2,1)} %get-tuple-element.88) | copy-start | bytes 1572868
  314.7 4.7 %copy-start.15 = (bf16[1,512,512]{2,1,0:T(8,128)(2,1)S(1)}, bf16[1,512,512]{2,1,0:T(8,128)(2,1)}, u32[]{:S(2)}) copy-start(bf16[1,512,512]{2,1,0:T(8,128)(2,1)} %get-tuple-element.89) | copy-start | bytes 1572868
Sparse Core Ops, SparseCore 0:
  107.5 24.0 all-gather.2
  191.8 35.4 all-gather.4
Sparse Core Ops, SparseCore 1:
  242.7 71.9 all-reduce.2

commit v2 on v1

v2 whole, which is shorter than its diff:
```python
import functools

import jax
import jax.numpy as jnp
from jax import lax
from jax.experimental import pallas as pl
from jax.experimental.pallas import tpu as pltpu
from jax.sharding import PartitionSpec as P

E = 64
SEQ = 1024
LANES = 128
PAIR = 2 * LANES
CHUNK = 128
EPS = 1e-05
F32 = jnp.float32
BF16 = jnp.bfloat16
ROWS = 128
GELU_C = 0.7978845608028654
GELU_A = 0.044715
SPLIT = 1.0 / 32.0
VMEM_LIMIT = 16 * 1024 * 1024

SECTION, PLACE, DEPTH = range(3)

PAD, SEG, CARRY_IN, TAIL_OUT, CARRIED, TAIL = range(6)


def nn(a, b):
    return jnp.dot(a, b, preferred_element_type=F32)


def nt(a, b):
    return lax.dot_general(a, b, (((1,), (1,)), ((), ())), preferred_element_type=F32)


def tn(a, b):
    return lax.dot_general(a, b, (((0,), (0,)), ((), ())), preferred_element_type=F32)


def first_head(shape):
    return lax.broadcasted_iota(jnp.int32, shape, len(shape) - 1) % LANES < E


def diagonal_blocks():
    row = lax.broadcasted_iota(jnp.int32, (LANES, PAIR), 0) < E
    return (row == first_head((LANES, PAIR))).astype(F32)


def split_pair(block):
    in_a = first_head(block.shape)
    zero = jnp.zeros_like(block)
    return jnp.concatenate([jnp.where(in_a, block, zero), jnp.where(in_a, zero, block)], axis=0)


def side(block, fill):
    return jnp.concatenate([block, jnp.full(block.shape, fill, block.dtype)], axis=1)


def normalise(values):
    centre = jnp.mean(values, axis=-1, keepdims=True)
    shifted = values - centre
    scale = lax.rsqrt(jnp.mean(shifted * shifted, axis=-1, keepdims=True) + EPS)
    return shifted * scale, scale


def norm_backward(grad, unit, scale, gain):
    grad_unit = grad * gain
    mean_grad = jnp.mean(grad_unit, axis=-1, keepdims=True)
    mean_dot = jnp.mean(grad_unit * unit, axis=-1, keepdims=True)
    return scale * (grad_unit - mean_grad - unit * mean_dot)


def row_tiles(total, step=ROWS):
    def decorate(body):
        pl.loop(0, total // step)(
            lambda index: body(pl.ds(pl.multiple_of(index * step, step), step))
        )

    return decorate


def start_copies(parts, place, sems, base):
    copies = [
        pltpu.make_async_copy(part, place(r), sems.at[base + r]) for r, part in enumerate(parts)
    ]
    for copy in copies:
        copy.start()
    return copies


def chunk_masks(cols_ref, seg_ref, mask, mask_t):
    row = lax.broadcasted_iota(jnp.int32, (CHUNK, CHUNK), 0)
    col = lax.broadcasted_iota(jnp.int32, (CHUNK, CHUNK), 1)
    for chunk in range(cols_ref.shape[0] // CHUNK):
        span = slice(chunk * CHUNK, (chunk + 1) * CHUNK)
        same = cols_ref[span, SEG : SEG + 1] == seg_ref[0:1, span]
        if mask is not None:
            lower = (same & (col <= row)).astype(F32)
            mask[chunk] = jnp.concatenate([lower, lower], axis=1)
        if mask_t is not None:
            upper = (same & (row <= col)).astype(F32)
            mask_t[chunk] = jnp.concatenate([upper, upper], axis=1)


def qkv_kernel(second, where, own, *rest):
    if second:
        came, gain, bias, cols, w, fq, fk, vv, state, normed, x_out = rest
        copies = []
    else:
        gain, bias, cols, w0, w1, w2, w3, fq, fk, vv, state, w, normed, sems = rest
        copies = start_copies(
            (w0, w1, w2, w3), lambda r: w.at[:, :, r * LANES : (r + 1) * LANES], sems, 0
        )
    total = own.shape[0]

    @row_tiles(total)
    def _(rows):
        x = own[rows, :].astype(F32)
        if second:
            x = jnp.where(where[SECTION] == 0, x, came[rows, :].astype(F32))
            x_out[rows, :] = x.astype(BF16)
        unit, _ = normalise(x)
        normed[rows, :] = (unit * gain[0:1, :] + bias[0:1, :]).astype(BF16)

    for copy in copies:
        copy.wait()

    @row_tiles(total, 256)
    def _(rows):
        block = normed[rows, :]
        query = nn(block, w[0])
        fq[rows, :] = jnp.where(query > 0, query + 1.0, jnp.exp(jnp.minimum(query, 0.0))).astype(BF16)
        key = nn(block, w[1])
        key = jnp.where(key > 0, key + 1.0, jnp.exp(jnp.minimum(key, 0.0)))
        fk[rows, :] = (key * cols[rows, PAD : PAD + 1]).astype(BF16)
        vv[rows, :] = nn(block, w[2]).astype(BF16)

    diag = diagonal_blocks()
    for pair in range(state.shape[0]):
        lanes = slice(pair * LANES, (pair + 1) * LANES)
        tail = (fk[:, lanes] * cols[:, TAIL_OUT : TAIL_OUT + 1].astype(BF16)).astype(BF16)
        state[pair] = (diag * tn(tail, side(vv[:, lanes], 1.0))).astype(BF16)


def attention_forward(fq, fk, vv, start, cols, seg, o, inv_den, states, mask):
    chunk_masks(cols, seg, mask, None)
    diag = diagonal_blocks()

    @pl.loop(0, start.shape[0])
    def _(pair):
        lanes = pl.ds(pl.multiple_of(pair * LANES, LANES), LANES)
        state = start[pair ^ 1].astype(F32)
        for chunk in range(fq.shape[0] // CHUNK):
            span = slice(chunk * CHUNK, (chunk + 1) * CHUNK)
            query, key, value = fq[span, lanes], fk[span, lanes], vv[span, lanes]
            carried = cols[span, CARRIED : CARRIED + 1]
            tail = cols[span, TAIL : TAIL + 1].astype(BF16)
            state_low = state.astype(BF16)
            if states is not None:
                states[pair, chunk] = state_low
            scores = (nt(query, split_pair(key)) * mask[chunk]).astype(BF16)
            ones = split_pair(jnp.ones_like(value))
            values = jnp.concatenate([split_pair(value), ones], axis=1)
            both = nn(scores, values) + carried * nn(query, state_low)
            inverse = 1.0 / (both[:, LANES:] + 1.0)
            o[span, lanes] = (both[:, :LANES] * inverse).astype(BF16)
            if inv_den is not None:
                inv_den[span, lanes] = inverse
            keep = carried[CHUNK - 1 : CHUNK, :]
            state = keep * state + diag * tn(key * tail, side(value, 1.0))


def out_and_norm(o, x, out_w, gain, bias, mid, normed_two):
    @row_tiles(o.shape[0], 256)
    def _(rows):
        mid[rows, :] = x[rows, :].astype(F32) + nn(o[rows, :], out_w[...])

    @row_tiles(o.shape[0])
    def _(rows):
        unit, _ = normalise(mid[rows, :])
        normed_two[rows, :] = (unit * gain[1:2, :] + bias[1:2, :]).astype(BF16)


def gelu_parts(up, with_slope):
    square = up * up
    inner = jnp.tanh(GELU_C * up * (1.0 + GELU_A * square))
    half = 0.5 * (1.0 + inner)
    if not with_slope:
        return up * half, None
    slope = half + up * (0.5 * GELU_C) * (1.0 - inner * inner) * (1.0 + 3.0 * GELU_A * square)
    return up * half, slope


def attention_kernel(
    fq, fk, vv, start, cols, seg, x, gain, bias, w0, w1, w2, w3, mid, normed_two, w, mask, o, sems
):
    copies = start_copies(
        (w0, w1, w2, w3), lambda r: w.at[r * LANES : (r + 1) * LANES, :], sems, 0
    )
    attention_forward(fq, fk, vv, start, cols, seg, o, None, None, mask)
    for copy in copies:
        copy.wait()
    out_and_norm(o, x, w, gain, bias, mid, normed_two)


def up_kernel(normed_two, w0, w1, w2, w3, active):
    width = w0.shape[1]
    for r, w in enumerate((w0, w1, w2, w3)):

        @row_tiles(normed_two.shape[0], 256)
        def _(rows, r=r, w=w):
            up = nn(normed_two[rows, :], w[...])
            active[rows, r * width : (r + 1) * width] = gelu_parts(up, False)[0].astype(BF16)


def down_kernel(mid, active, w0, w1, w2, w3, y):
    width = w0.shape[1]

    @row_tiles(mid.shape[0], 256)
    def _(rows):
        total = mid[rows, :]
        for r, w in enumerate((w0, w1, w2, w3)):
            total = total + nt(active[rows, r * width : (r + 1) * width], w[...])
        y[rows, :] = total.astype(BF16)


def block_kernel(
    fq, fk, vv, start, cols, seg, x, gain, bias, out_w, u0, u1, u2, u3, d0, d1, d2, d3,
    y, mid, o, o_send, inv_den, states, keep, send, slope, normed_two, mask,
):
    attention_forward(fq, fk, vv, start, cols, seg, o, inv_den, states, mask)
    for slot, r in enumerate((1, 3)):
        o_send[:, slot * LANES : (slot + 1) * LANES] = o[:, r * LANES : (r + 1) * LANES]
    out_and_norm(o, x, out_w, gain, bias, mid, normed_two)
    up_w, down_w = (u0, u1, u2, u3), (d0, d1, d2, d3)
    width = u0.shape[1]

    @row_tiles(x.shape[0], 256)
    def _(rows):
        total = mid[rows, :]
        for r in range(4):
            units = slice(r * width, (r + 1) * width)
            value, steep = gelu_parts(nn(normed_two[rows, :], up_w[r][...]), True)
            value = value.astype(BF16)
            half = slice(r // 2 * width, (r // 2 + 1) * width)
            (send if r % 2 else keep)[rows, half] = value
            slope[rows, units] = steep.astype(BF16)
            total = total + nt(value, down_w[r][...])
        y[rows, :] = total.astype(BF16)


def ffn_back_kernel(with_weights, where, own_g, *rest):
    if with_weights:
        came, rest = rest[0], rest[1:]
    slope, mid, o, inv_den, fq, cols, gain, out_w, *rest = rest
    up_w, down_w = rest[0:4], rest[4:8]
    grad_mid, dnum, dden, grad_state, *rest = rest[8:]
    if with_weights:
        dup_keep, dup_send, dattn, sums, gy = rest
    else:
        (dattn,) = rest
        gy = own_g
    width = up_w[0].shape[1]
    total = gy.shape[0]
    if with_weights:

        @row_tiles(total)
        def _(rows):
            gy[rows, :] = jnp.where(
                where[SECTION] == 1, own_g[rows, :], came[rows, :].astype(F32)
            )

    @row_tiles(total, 256)
    def _(rows):
        dffn = gy[rows, :].astype(BF16)
        grad = jnp.zeros(dffn.shape, F32)
        for r in range(4):
            units = slice(r * width, (r + 1) * width)
            dup = (slope[rows, units].astype(F32) * nn(dffn, down_w[r][...])).astype(BF16)
            if with_weights:
                half = slice(r // 2 * width, (r // 2 + 1) * width)
                (dup_send if r % 2 else dup_keep)[rows, half] = dup
            grad = grad + nt(dup, up_w[r][...])
        grad_mid[rows, :] = grad

    if with_weights:
        sums[...] = jnp.zeros_like(sums)

    @row_tiles(total)
    def _(rows):
        unit, scale = normalise(mid[rows, :])
        grad = grad_mid[rows, :]
        if with_weights:
            sums[0:1, :] += jnp.sum(grad * unit, axis=0, keepdims=True)
            sums[1:2, :] += jnp.sum(grad, axis=0, keepdims=True)
        grad = gy[rows, :] + norm_backward(grad, unit, scale, gain[1:2, :])
        grad_mid[rows, :] = grad
        dattn[rows, :] = grad.astype(BF16)

    row_a = lax.broadcasted_iota(jnp.int32, (LANES, LANES), 0) < E
    spread = (row_a == first_head((LANES, LANES))).astype(BF16)
    use_low = lax.broadcasted_iota(jnp.int32, (256, LANES), 1) % E >= E // 2

    @row_tiles(total, 256)
    def _(rows):
        grad_heads = nt(dattn[rows, :], out_w[...])
        scaled = grad_heads * inv_den[rows, :]
        dnum[rows, :] = scaled.astype(BF16)
        product = -scaled * o[rows, :].astype(F32)
        for pair in range(grad_state.shape[0]):
            lanes = slice(pair * LANES, (pair + 1) * LANES)
            part = product[:, lanes]
            high = part.astype(BF16)
            low = (part - high.astype(F32)).astype(BF16)
            whole = nn(high, spread) + nn(low, spread)
            high = whole.astype(BF16)
            low = (whole - high.astype(F32)).astype(BF16)
            dden[rows, lanes] = jnp.where(use_low, low, high)

    diag = diagonal_blocks()
    carry_in = cols[:, CARRY_IN : CARRY_IN + 1].astype(BF16)
    for pair in range(grad_state.shape[0]):
        lanes = slice(pair * LANES, (pair + 1) * LANES)
        both = jnp.concatenate([dnum[:, lanes], dden[:, lanes]], axis=1)
        grad_state[pair] = (diag * tn(fq[:, lanes] * carry_in, both)).astype(BF16)


def attention_back_kernel(
    with_weights, fq, fk, vv, dnum, dden, states, end, cols, seg, x, grad_mid, gain, w, *rest
):
    if with_weights:
        sums_two, grad_x, keep, send, sums, *rest = rest
    else:
        grad_x, *rest = rest
    mask, mask_t, acc, dproj = rest
    chunk_masks(cols, seg, mask, mask_t)
    diag = diagonal_blocks()
    lane = lax.broadcasted_iota(jnp.int32, (1, PAIR), 1)
    share = jnp.where(lane < LANES, 1.0, SPLIT)

    @pl.loop(0, end.shape[0])
    def _(pair):
        lanes = pl.ds(pl.multiple_of(pair * LANES, LANES), LANES)
        grad_state = end[pair ^ 1].astype(F32)
        for chunk in reversed(range(fq.shape[0] // CHUNK)):
            span = slice(chunk * CHUNK, (chunk + 1) * CHUNK)
            query, key, value = fq[span, lanes], fk[span, lanes], vv[span, lanes]
            grad_n, grad_d = dnum[span, lanes], dden[span, lanes]
            carried = cols[span, CARRIED : CARRIED + 1]
            tail = cols[span, TAIL : TAIL + 1]
            stays = carried[CHUNK - 1 : CHUNK, :]
            query_two = split_pair(query)
            grad_n_two = split_pair(grad_n)
            both = jnp.concatenate([grad_n, grad_d], axis=1)
            both_two = jnp.concatenate([grad_n_two, split_pair(grad_d)], axis=1)
            share_two = split_pair(jnp.full(value.shape, SPLIT, BF16))
            values_two = jnp.concatenate([split_pair(value), share_two], axis=1)
            values = side(value, SPLIT)
            scores_t = (nt(key, query_two) * mask_t[chunk]).astype(BF16)
            dscores = (nt(both, values_two) * mask[chunk]).astype(BF16)
            dscores_t = (nt(values, both_two) * mask_t[chunk]).astype(BF16)
            state = (states[pair, chunk].astype(F32) * share).astype(BF16)
            grad_low = grad_state.astype(BF16)
            dfq = nn(dscores, split_pair(key)) + carried * nt(both, state)
            dfk = nn(dscores_t, query_two) + tail * nt(values, grad_low)
            dvv = nn(scores_t, grad_n_two) + tail * nn(key, grad_low[:, :LANES])
            dproj[0, span, lanes] = (jnp.minimum(query.astype(F32), 1.0) * dfq).astype(BF16)
            dproj[1, span, lanes] = (jnp.minimum(key.astype(F32), 1.0) * dfk).astype(BF16)
            dproj[2, span, lanes] = dvv.astype(BF16)
            moved = diag * tn(query * carried.astype(BF16), both)
            grad_state = stays * grad_state + moved

    @row_tiles(x.shape[0], 256)
    def _(rows):
        acc[rows, :] = (
            nt(dproj[0, rows, :], w[0]) + nt(dproj[1, rows, :], w[1]) + nt(dproj[2, rows, :], w[2])
        )

    if with_weights:
        for r in range(4):
            half = slice(r // 2 * LANES, (r // 2 + 1) * LANES)
            (send if r % 2 else keep)[:, :, half] = dproj[:, :, r * LANES : (r + 1) * LANES]
        sums[...] = jnp.zeros_like(sums)
        sums[1:2, :] = sums_two[0:1, :]
        sums[3:4, :] = sums_two[1:2, :]

    @row_tiles(x.shape[0])
    def _(rows):
        unit, scale = normalise(x[rows, :].astype(F32))
        grad = acc[rows, :]
        if with_weights:
            sums[0:1, :] += jnp.sum(grad * unit, axis=0, keepdims=True)
            sums[2:3, :] += jnp.sum(grad, axis=0, keepdims=True)
        grad = grad_mid[rows, :] + norm_backward(grad, unit, scale, gain[0:1, :])
        grad_x[rows, :] = grad.astype(BF16)


def down_grad_kernel(where, own_g, other_g, came, came_two, own, other, keep, send, turned):
    total = own_g.shape[0]
    for n, (mine, arrived) in enumerate(((own_g, came), (other_g, came_two))):
        whole = jnp.where(where[SECTION] == 1, mine[...], arrived[...].astype(F32))
        turned[:, n * total : (n + 1) * total] = whole.astype(BF16).T
    width = keep.shape[1]
    for r, place in enumerate((keep, send)):
        cols = slice(r * width, (r + 1) * width)
        sum_own = nn(turned[:, :total], own[:, cols])
        place[...] = (sum_own + nn(turned[:, total:], other[:, cols])).astype(BF16)


def up_grad_kernel(normed_own, normed_other, own, other, keep, send, turned):
    total = normed_own.shape[0]
    turned[:, :total] = normed_own[...].T
    turned[:, total:] = normed_other[...].T
    width = keep.shape[1]
    for r, place in enumerate((keep, send)):
        cols = slice(r * width, (r + 1) * width)
        sum_own = nn(turned[:, :total], own[:, cols])
        place[...] = (sum_own + nn(turned[:, total:], other[:, cols])).astype(BF16)


def late_grad_kernel(
    normed_own, normed_other, own, other, o_own, o_other, dattn_own, dattn_other,
    sums_own, sums_other, keep, send, turned,
):
    total, width = normed_own.shape
    base = 3 * width
    last = base + width
    places = (keep, send)
    turned[:, :total] = normed_own[...].T
    turned[:, total:] = normed_other[...].T
    for c in range(3):
        whole = nn(turned[:, :total], own[c]) + nn(turned[:, total:], other[c])
        for r, place in enumerate(places):
            cols = slice(r * LANES, (r + 1) * LANES)
            place[c * width : (c + 1) * width, :] = whole[:, cols].astype(BF16)
    for r, place in enumerate(places):
        here = o_own[:, 2 * r * LANES : (2 * r + 1) * LANES].T
        there = o_other[:, r * LANES : (r + 1) * LANES].T
        whole = (nn(here, dattn_own[...]) + nn(there, dattn_other[...])).astype(BF16)
        for n in range(width // LANES):
            to = base + n * LANES
            place[to : to + LANES, :] = whole[:, n * LANES : (n + 1) * LANES]
    four = sums_own[0:4, :] + sums_other[0:4, :]
    small = jnp.concatenate(
        [four[v : v + 1, n * LANES : (n + 1) * LANES] for v in range(4) for n in range(width // LANES)],
        axis=0,
    ).astype(BF16)
    for place in places:
        place[last : last + small.shape[0], :] = small
        left = place.shape[0] - last - small.shape[0]
        place[last + small.shape[0] :, :] = jnp.zeros((left, LANES), BF16)


def part_rows(where, r, size):
    return pl.ds(pl.multiple_of((where[DEPTH] ^ r) * size, 16), size)


def cut_kernel(where, keep, came, *outs):
    for r, out in enumerate(outs):
        rows = part_rows(where, r, out.shape[0])
        total = keep[rows, :].astype(F32) + came[rows, :].astype(F32)
        out[...] = total.astype(out.dtype)


def add_kernel(own, one, two, three, out):
    total = own[...] + one[...].astype(F32) + two[...].astype(F32) + three[...].astype(F32)
    out[...] = total.astype(BF16)


def join_kernel(where, own, one, two, three, out):
    for r, part in enumerate((own, one, two, three)):
        out[part_rows(where, r, part.shape[0]), :] = part[...].astype(F32)


def unpack_late(source, qkv, out, gains, biases):
    width = out.shape[1]
    base = 3 * width
    last = base + width
    pairs = width // LANES
    for c in range(3):
        qkv[c] = source[c * width : (c + 1) * width, :].astype(F32)
    for n in range(pairs):
        cols = slice(n * LANES, (n + 1) * LANES)
        out[:, cols] = source[base + n * LANES : base + (n + 1) * LANES, :].astype(F32)
        for v, place in enumerate((gains, gains, biases, biases)):
            row = last + v * pairs + n
            place[v % 2 : v % 2 + 1, cols] = source[row : row + 1, :].astype(F32)


def join_late_kernel(where, own, one, two, three, qkv, out, gains, biases, whole):
    join_kernel(where, own, one, two, three, whole)
    unpack_late(whole, qkv, out, gains, biases)


def unpack_late_kernel(source, qkv, out, gains, biases, whole):
    whole[...] = source[...].astype(F32)
    unpack_late(whole, qkv, out, gains, biases)


def halves(where):
    depth = where[DEPTH]
    return (depth ^ (depth >> 1)) & 1, depth >> 1


def rows_at(index, size):
    return pl.ds(pl.multiple_of(index * size, 16), size)


def halve_first_kernel(where, keep, came, stays, goes):
    mine, _ = halves(where)
    size = stays.shape[0]
    for index, out in ((mine, stays), (1 - mine, goes)):
        rows = rows_at(index, size)
        out[...] = (keep[rows, :].astype(F32) + came[rows, :].astype(F32)).astype(out.dtype)


def halve_second_kernel(where, keep, came, stays, goes):
    _, mine = halves(where)
    size = stays.shape[0]
    for index, out in ((mine, stays), (1 - mine, goes)):
        rows = rows_at(index, size)
        out[...] = (keep[rows, :] + came[rows, :].astype(F32)).astype(out.dtype)


def sum_kernel(keep, came, out):
    out[...] = (keep[...] + came[...].astype(F32)).astype(BF16)


def pair_kernel(where, own, came, out):
    _, mine = halves(where)
    size = own.shape[0]
    out[rows_at(mine, size), :] = own[...]
    out[rows_at(1 - mine, size), :] = came[...]


def whole_kernel(where, own, came, out):
    mine, _ = halves(where)
    size = own.shape[0]
    out[rows_at(mine, size), :] = own[...].astype(F32)
    out[rows_at(1 - mine, size), :] = came[...].astype(F32)


def finish_kernel(with_rms, where, p0, p1, p2, p3, out, *rms):
    total, width = p0.shape
    for r, part in enumerate((p0, p1, p2, p3)):
        begin = where[PLACE] ^ r

        @pl.loop(0, total // LANES)
        def _(tile, part=part, begin=begin):
            block = part[pl.ds(pl.multiple_of(tile * LANES, LANES), LANES), :].astype(F32)
            to = begin * (total // LANES) + tile
            out[pl.ds(pl.multiple_of(to * LANES, LANES), LANES), :] = block
            if with_rms:
                square = block * block
                high = square.astype(BF16)
                low = (square - high.astype(F32)).astype(BF16)
                ones = jnp.ones((8, width), BF16)
                mean = (nt(ones, high) + nt(ones, low)) * (1.0 / width)
                rms[0][pl.ds(to, 1), :] = jnp.sqrt(mean[0:1, :] + 1e-06)


IN_VMEM = pl.BlockSpec(memory_space=pltpu.VMEM)
IN_SMEM = pl.BlockSpec(memory_space=pltpu.SMEM)
ANYWHERE = pl.BlockSpec(memory_space=pl.ANY)


def call(kernel, operands, outputs, scratch, name, us, far=()):
    near = [jax.ShapeDtypeStruct(shape, dtype) for shape, dtype in outputs]
    return pl.pallas_call(
        kernel,
        out_shape=near,
        in_specs=[IN_SMEM if v.dtype == jnp.int32 else IN_VMEM for v in operands]
        + [ANYWHERE] * len(far),
        out_specs=[IN_VMEM] * len(near),
        scratch_shapes=scratch,
        compiler_params=pltpu.CompilerParams(vmem_limit_bytes=VMEM_LIMIT),
        cost_estimate=pl.CostEstimate(
            flops=int(us * 1.1e9), bytes_accessed=0, transcendentals=0
        ),
        name=name,
    )(*operands, *far)


def across(block, distance, axis="head"):
    size = lax.axis_size(axis)
    return lax.ppermute(block, axis, [(i, i ^ distance) for i in range(size)])


def spread(block, far):
    return (block, across(block, 1), far, across(far, 1))


def after(value, *others):
    return lax.optimization_barrier((value, *others))[0]


def sum_rows(keep, send, where, join, name):
    came = across(send, 2)
    rows, width = keep.shape
    depth = lax.axis_size("dp")
    if depth != 4:
        total = (keep.astype(F32) + came.astype(F32)).astype(BF16)
        return join(where, lax.psum(total, "dp"))
    part = (rows // depth, width)
    own, *parts = call(
        cut_kernel, (where, keep, came), [(part, F32)] + [(part, BF16)] * 3, [], "cut" + name, 0.7
    )
    parts = [across(v, r + 1, "dp") for r, v in enumerate(parts)]
    (own,) = call(add_kernel, (own, *parts), [(part, BF16)], [], "add" + name, 0.7)
    return join(where, own, *[across(own, r, "dp") for r in (1, 2, 3)])


def halving_sum(keep, came, where, name):
    rows, width = keep.shape
    if lax.axis_size("dp") != 4:
        total = (keep.astype(F32) + came.astype(F32)).astype(BF16)
        yield total
        yield total
        yield lax.psum(total, "dp").astype(F32)
        return
    half, quarter = (rows // 2, width), (rows // 4, width)
    stays, goes = call(
        halve_first_kernel, (where, keep, came), [(half, F32), (half, BF16)], [], "halve_" + name, 0.8
    )
    came = across(goes, 1, "dp")
    yield goes
    stays, goes = call(
        halve_second_kernel, (where, stays, came), [(quarter, F32), (quarter, BF16)], [],
        "halve_again_" + name, 0.7,
    )
    came = across(goes, 3, "dp")
    yield goes
    (own,) = call(sum_kernel, (stays, came), [(quarter, BF16)], [], "sum_" + name, 0.6)
    came = across(own, 3, "dp")
    (own,) = call(pair_kernel, (where, own, came), [(half, BF16)], [], "pair_" + name, 0.6)
    came = across(own, 1, "dp")
    yield call(whole_kernel, (where, own, came), [((rows, width), F32)], [], "whole_" + name, 1.0)[0]


def finish(where, own, far, with_rms, name):
    rows, width = own.shape[0] * 4, own.shape[1]
    outputs = [((rows, width), F32)] + [((rows // LANES, LANES), F32)] * with_rms
    return call(
        functools.partial(finish_kernel, with_rms),
        (where, own, across(own, 1), far, across(far, 1)), outputs, [], name, 3.0,
    )


def token_table(segment_start, pad_mask, place, tokens, parts):
    row_count = segment_start.shape[0] // SEQ
    ids = jnp.cumsum(segment_start.reshape(row_count, SEQ), axis=1).reshape(-1)
    begin = place * tokens
    own = lax.dynamic_slice(ids, (begin,), (tokens,))
    before = lax.dynamic_slice(ids, (jnp.maximum(begin - 1, 0),), (1,))
    before = jnp.where(place % parts == 0, jnp.full_like(before, -1), before)
    last = own.reshape(-1, CHUNK)[:, -1]
    previous = jnp.concatenate([before, last[:-1]])
    pad = lax.dynamic_slice(pad_mask, (begin,), (tokens,))
    columns = [
        pad,
        own,
        own == before,
        own == last[-1:],
        own == jnp.repeat(previous, CHUNK),
        own == jnp.repeat(last, CHUNK),
    ]
    columns = jnp.stack([c.astype(F32) for c in columns], axis=1)
    rows = jnp.broadcast_to(own.astype(F32)[None], (8, tokens))
    return columns, rows


def local(
    block_input, cotangent, segment_start, pad_mask, qkv_weight, out_weight, up_weight,
    down_weight, norm_gain, norm_bias,
):
    heads = lax.axis_size("head")
    row_count = block_input.shape[0] // SEQ
    parts = heads // row_count
    assert heads == 4 and parts == 2
    tokens = block_input.shape[0] // heads
    width = block_input.shape[1]
    units = up_weight.shape[-1] * heads
    pairs = width // LANES
    chunks = tokens // CHUNK
    section = lax.axis_index("section")
    place = lax.axis_index("head")

    gain, bias = norm_gain[0], norm_bias[0]
    far_out = across(out_weight[0], 2)
    far_up = across(up_weight[0], 2)
    far_down = across(down_weight[0], 2)

    cols, seg = token_table(segment_start, pad_mask, place, tokens, parts)
    own_x = lax.dynamic_slice(block_input, (place * tokens, 0), (tokens, width))

    wide = (tokens, width)
    state_shape = (pairs, LANES, PAIR)
    dma = pltpu.SemaphoreType.DMA
    mask_mem = pltpu.VMEM((chunks, CHUNK, PAIR), F32)
    row_mem = pltpu.VMEM(wide, BF16)

    own_g = lax.dynamic_slice(cotangent, (place * tokens, 0), (tokens, width))
    other_g = lax.dynamic_slice(cotangent, ((place ^ 1) * tokens, 0), (tokens, width))
    where = jnp.stack([section, place, lax.axis_index("dp")]).astype(jnp.int32)
    turned_mem = pltpu.VMEM((width, 2 * tokens), BF16)
    grad_mem = pltpu.VMEM(wide, F32)
    half = (tokens, units // 2)
    features = [(wide, BF16)] * 3 + [(state_shape, BF16)]

    fq, fk, vv, state, qkv = call(
        functools.partial(qkv_kernel, False),
        (where, after(own_x, own_g, other_g, seg), gain, bias, cols),
        features + [((3, width, width), BF16)],
        [row_mem, dma((4,))], "qkv_first", 4.0, far=spread(qkv_weight[0], across(qkv_weight[0], 2)),
    )
    start = across(state, 1)
    mid, normed_two, out_w = call(
        attention_kernel, (fq, fk, vv, start, cols, seg, own_x, gain, bias),
        [(wide, F32), (wide, BF16), ((width, width), BF16)],
        [mask_mem, row_mem, dma((4,))], "attention_first", 5.5,
        far=spread(out_weight[0], after(far_out, fq)),
    )
    up_w = spread(up_weight[0], after(far_up, fq))
    (active,) = call(
        up_kernel, (normed_two, *up_w), [((tokens, units), BF16)], [], "up_first", 3.2
    )
    down_w = spread(down_weight[0], after(far_down, normed_two))
    (y,) = call(down_kernel, (mid, active, *down_w), [(wide, BF16)], [], "down_first", 2.8)
    came = across(y, 1, "section")

    fq, fk, vv, state, normed, x = call(
        functools.partial(qkv_kernel, True), (where, own_x, came, gain, bias, cols, qkv),
        features + [(wide, BF16)] * 2, [], "qkv_second", 3.5,
    )
    start = across(state, 1)
    y, mid, o, o_send, inv_den, states, active, active_send, slope, normed_two = call(
        block_kernel, (fq, fk, vv, start, cols, seg, x, gain, bias, out_w, *up_w, *down_w),
        [
            (wide, BF16), (wide, F32), (wide, BF16), ((tokens, width // 2), BF16), (wide, F32),
            ((pairs, chunks, LANES, PAIR), BF16), (half, BF16), (half, BF16),
            ((tokens, units), BF16), (wide, BF16),
        ],
        [mask_mem], "block_second", 10.0,
    )
    far_y = across(y, 2)
    active_two = across(active_send, 1)
    normed_other = across(normed, 1)
    normed_two_other = across(normed_two, 1)
    o_other = across(o_send, 1)

    def ffn_back(grads, name):
        second = len(grads) > 1
        extra = [(half, BF16)] * 2 + [(wide, BF16), ((2, width), F32)] if second else []
        return call(
            functools.partial(ffn_back_kernel, second),
            (where, *grads, slope, mid, o, inv_den, fq, cols, gain, out_w, *up_w, *down_w),
            [(wide, F32), (wide, BF16), (wide, BF16), (state_shape, BF16)] + extra,
            [grad_mem] if second else [row_mem], name, 7.5,
        )

    def attention_back(sums, grad_mid, dnum, dden, end, name):
        third = ((3, tokens, width // 2), BF16)
        extra = [third, third, ((8, width), F32)] if sums else []
        return call(
            functools.partial(attention_back_kernel, bool(sums)),
            (fq, fk, vv, dnum, dden, states, end, cols, seg, x, grad_mid, gain, qkv, *sums),
            [(wide, BF16)] + extra,
            [mask_mem, mask_mem, grad_mem, pltpu.VMEM((3, *wide), BF16)], name, 7.5,
        )

    grad_mid, dnum, dden, moved = ffn_back((own_g,), "ffn_back_first")
    (grad_x,) = attention_back((), grad_mid, dnum, dden, across(moved, 1), "attention_back_first")
    came = across(grad_x, 1, "section")
    activations, token_rms = finish(
        where, after(y, grad_x), after(far_y, grad_x), True, "activations"
    )
    came = after(came, activations)

    share = (width, units // 4)
    keep, send = call(
        down_grad_kernel, (where, own_g, other_g, came, across(came, 1), active, active_two),
        [(share, BF16)] * 2, [turned_mem], "down_grad", 2.2,
    )
    down_keep, down_far = keep, across(send, 2)
    grad_mid, dnum, dden, moved, dup, dup_send, dattn, sums_two = ffn_back(
        (own_g, after(came, send)), "ffn_back_second"
    )
    end = across(moved, 1)
    dattn_other = across(dattn, 1)
    keep, send = call(
        up_grad_kernel, (normed_two, normed_two_other, dup, across(dup_send, 1)),
        [(share, BF16)] * 2, [turned_mem], "up_grad", 1.3,
    )
    up_keep, up_far = keep, across(send, 2)
    down_steps = halving_sum(down_keep, after(down_far, send), where, "down")
    goes = next(down_steps)
    grad_x, dproj, dproj_send, sums = attention_back(
        (sums_two,), grad_mid, dnum, dden, after(end, goes), "attention_back_second"
    )
    goes = next(down_steps)
    late = (4 * width + 64, LANES)
    keep, send = call(
        late_grad_kernel,
        (
            normed, normed_other, dproj, across(dproj_send, 1), o, o_other, dattn, dattn_other,
            after(sums, goes), across(sums, 1),
        ),
        [(late, BF16)] * 2, [turned_mem], "late_grad", 1.3,
    )
    up_steps = halving_sum(up_keep, after(up_far, grad_x), where, "up")
    next(up_steps)
    next(up_steps)

    def late_join(where, *parts):
        results = [
            ((3, width, LANES), F32), ((LANES, width), F32), ((2, width), F32), ((2, width), F32)
        ]
        if len(parts) == 1:
            kernel, operands = unpack_late_kernel, parts
        else:
            kernel, operands = join_late_kernel, (where, *parts)
        return call(kernel, operands, results, [pltpu.VMEM(late, F32)], "join_late", 1.5)

    qkv_total, out_total, gain_total, bias_total = sum_rows(keep, send, where, late_join, "_late")
    down_total, up_total = next(down_steps), next(up_steps)
    own = after(grad_x, send)
    (input_grad,) = finish(where, own, across(own, 2), False, "input_grad")
    return (
        activations[None], input_grad[None], token_rms.reshape(1, -1), qkv_total[None],
        out_total[None], up_total[None], down_total[None], gain_total[None], bias_total[None],
    )


def solution(mesh):
    placed = (
        P("dp", None),
        P("dp", None),
        P("dp"),
        P("dp"),
        P("section", None, None, "head"),
        P("section", "head", None),
        P("section", None, "head"),
        P("section", None, "head"),
        P("section", None, None),
        P("section", None, None),
    )
    return jax.shard_map(
        local,
        mesh=mesh,
        in_specs=placed,
        out_specs=(
            P("section", "dp", None),
            P("section", "dp", None),
            P("section", "dp"),
            P("section", None, None, "head"),
            P("section", "head", None),
            P("section", None, "head"),
            P("section", None, "head"),
            P("section", None, None),
            P("section", None, None),
        ),
        check_vma=False,
    )
```

time: 331 us -> 226 us (0.68)
  waiting for transfers between devices: 148 us -> 85.8 us
  starting transfers between devices: 16.6 us -> 50.4 us
  Pallas kernels: 103 us -> 78.1 us
  other arithmetic: 25.6 us -> 3.13 us
  between operations: 16.5 us -> 1.68 us
  local copies, waits for them, and re-layouts: 19.9 us -> 6.11 us
    psum x1 -> x0, waiting for transfers between devices: 62.4 us -> none  [local(): late_total = lax.psum(late_total, 'dp').astype(F32)]
    ppermute x24 -> x50, starting transfers between devices: 16.1 us -> 50.4 us  [across(): return lax.ppermute(block, axis, [(i, i ^ distance) for i in range(size)])]
    pallas_call x13 -> x28, Pallas kernels: 103 us -> 78.1 us  [call(): pl.pallas_call(kernel, out_shape=near, in_specs=[IN_SMEM if v.dtype == jn...]
    broadcast_in_dim x6 -> x0, other arithmetic: 11 us -> none  [the longest x1 4.22 us: local(): input_grad[None]]
    slice x6 -> x1, local copies, waits for them, and re-layouts: 5.03 us -> 0.21 us  [the longest x1 2.01 us: local(): qkv_total = late_total[:3 * width].reshape(3, width, LANES)]
    select_n x2 -> x0, other arithmetic: 4.31 us -> none  [the longest x1 2.36 us: local(): gy = jnp.where(section == 1, own_g, came.astype(F32))]
    rev x4 -> x0, local copies, waits for them, and re-layouts: 3.86 us -> none  [the longest x2 2.42 us: features(): start = came.reshape(2, 2, LANES, PAIR)[:, ::-1].reshape(state_shape)]
    add x3 -> x0, other arithmetic: 3.5 us -> none  [reduce_shares(): pair_sum = keep.astype(F32) + came.astype(F32)]
  transfers between devices with their start and end apart: 27 -> 50, of which waited for: 11 -> 20; matrix products, arithmetic and copies ran while one was open for 10% -> 3% of each run, Pallas kernels for 24% -> 17%
where the time goes in v2:
time: 226 us; the launch traced here: 225 us
  waiting for transfers between devices  85.8 us (38%)
  Pallas kernels  78.1 us (35%)
  starting transfers between devices  50.4 us (22%)
  local copies, waits for them, and re-layouts  6.11 us (3%)
  other arithmetic  3.13 us (1%)
    ppermute x50, waiting for transfers between devices, across(): return lax.ppermute(block, axis, [(i, i ^ distance) for i in range(size)])  85.8 us
    pallas_call x28, Pallas kernels, call(): pl.pallas_call(kernel, out_shape=near, in_specs=[IN_SMEM if v.dtype == jn...  78.1 us
    ppermute x50, starting transfers between devices, across(): return lax.ppermute(block, axis, [(i, i ^ distance) for i in range(size)])  50.4 us
  transfers between devices with their start and end apart: 50, of which 20 were waited for; matrix products, arithmetic and copies ran while one was open for 3% of the time, Pallas kernels for 17%

profile of v2, /device:TPU:0, one launch (start us, length us, event | category | flops | bytes accessed | tf_op | source)
XLA Modules:
  0.0 225.3 jit_solution(1777192497238888738)
XLA Ops:
  0.7 3.0 %collective-permute-start.1 = (bf16[3,512,128]{2,1,0:T(8,128)(2,1)}, bf16[3,512,128]{2,1,0:T(8,128)(2,1)}, u32[]{:S(2)}, u32[]{:S(2)}) collective-permute-start(bf16[3,512,128]{2,1,0:T(8,128)(2,1)} %bitcast.53), channel_id=1, source_target_pairs={{0,2},{1,3},{2,0},{3,1},{4,6},{5,7},{6,4},{7,5},{8,10},{9,11},{10,... | collective-permute-start | bytes 1179656 | tf_op jit(solution)/shard_map/ppermute | solution.py:587
  3.8 1.9 collective-permute-start.8
  5.7 1.2 reduce-window.6
  8.0 0.8 dynamic-slice_bitcast_fusion
  10.4 0.7 fusion.1
  11.4 2.6 %collective-permute-done.1.rest_5_ = bf16[3,512,128]{2,1,0:T(8,128)(2,1)} collective-permute-done((bf16[3,512,128]{2,1,0:T(8,128)(2,1)}, bf16[3,512,128]{2,1,0:T(8,128)(2,1)}, u32[]{:S(2)}, u32[]{:S(2)}) %collective-permute-start.1) | collective-permute-done | bytes 393248 | tf_op jit(solution)/shard_map/ppermute | solution.py:587
  14.0 1.7 constant_dynamic-slice_fusion
  16.0 1.0 copy-done.4
  17.0 0.7 copy-done.6
  17.7 0.7 copy-done.8
  18.4 3.6 %qkv_first.1 = (bf16[512,512]{1,0:T(8,128)(2,1)S(1)}, bf16[512,512]{1,0:T(8,128)(2,1)S(1)}, bf16[512,512]{1,0:T(8,128)(2,1)S(1)}, bf16[4,128,256]{2,1,0:T(8,128)(2,1)S(1)}, bf16[3,512,512]{2,1,0:T(8,128)(2,1)S(1)}) custom-call(s32[3]{0:T(128)S(1)} %pad_add_fusion.where, bf16[512,512]{1,0:T(8,128)(2,1)S(1)} %constant_dynamic-slice_fusion.2.own.x, ...), custom_call_target="tpu_custom_call" | custom-call | flops 4400000000 | tf_op jit(solution)/shard_map/qkv_first/pallas_call | solution.py:570
  23.1 3.9 %collective-permute-done.8.w2.u2.rest_10_.rest_11_ = bf16[512,512]{1,0:T(8,128)(2,1)S(1)} collective-permute-done((bf16[512,512]{1,0:T(8,128)(2,1)}, bf16[512,512]{1,0:T(8,128)(2,1)S(1)}, u32[]{:S(2)}, u32[]{:S(2)}) %collective-permute-start.8) | collective-permute-done | bytes 524320 | tf_op jit(solution)/shard_map/ppermute | solution.py:587
  27.0 1.7 collective-permute-start.11
  29.3 5.8 %attention_first.1 = (f32[512,512]{1,0:T(8,128)S(1)}, bf16[512,512]{1,0:T(8,128)(2,1)S(1)}, bf16[512,512]{1,0:T(8,128)(2,1)S(1)}) custom-call(bf16[512,512]{1,0:T(8,128)(2,1)S(1)} %get-tuple-element.87.fq, bf16[512,512]{1,0:T(8,128)(2,1)S(1)} %get-tuple-element.88.fk, bf16[512,512]{1,0:T(8,128)(2,1)S(1)} %get-tuple-element.89.vv, ...), custom_call_target="tpu_custom_call" | custom-call | flops 6049999872 | tf_op jit(solution)/shard_map/attention_first/pallas_call | solution.py:570
  35.1 5.1 %collective-permute-done.11.w2.d2.rest_14_.rest_15_ = bf16[512,512]{1,0:T(8,128)(2,1)S(1)} collective-permute-done((bf16[512,512]{1,0:T(8,128)(2,1)S(1)}, bf16[512,512]{1,0:T(8,128)(2,1)S(1)}, u32[]{:S(2)}, u32[]{:S(2)}) %collective-permute-start.11) | collective-permute-done | bytes 524320 | tf_op jit(solution)/shard_map/ppermute | solution.py:587
  40.2 3.2 %up_first.1.active = bf16[512,2048]{1,0:T(8,128)(2,1)S(1)} custom-call(bf16[512,512]{1,0:T(8,128)(2,1)S(1)} %get-tuple-element.93.normed_two, bf16[512,512]{1,0:T(8,128)(2,1)S(1)} %bitcast.43, bf16[512,512]{1,0:T(8,128)(2,1)S(1)} %collective-permute-done.7.w1.u1.rest_9_.rest_10_, bf16[512,512]{1,0:T(8,128)(2,1)S(1)} %collective-permute-done.8.w2.u2.rest_10_.rest_11_, ...), custom_call_target="tpu_custom_call" | custom-call | flops 3520000000 | tf_op jit(solution)/shard_map/up_first/pallas_call | solution.py:570
  43.4 1.5 down_first.1
  44.9 1.5 collective-permute-start.13
  46.4 12.9 %collective-permute-done.13.rest_0_ = bf16[512,512]{1,0:T(8,128)(2,1)S(1)} collective-permute-done((bf16[512,512]{1,0:T(8,128)(2,1)S(1)}, bf16[512,512]{1,0:T(8,128)(2,1)S(1)}, u32[]{:S(2)}, u32[]{:S(2)}) %collective-permute-start.13) | collective-permute-done | bytes 524320 | tf_op jit(solution)/shard_map/ppermute | solution.py:587
  59.3 3.1 %qkv_second.1 = (bf16[512,512]{1,0:T(8,128)(2,1)S(1)}, bf16[512,512]{1,0:T(8,128)(2,1)S(1)}, bf16[512,512]{1,0:T(8,128)(2,1)S(1)}, bf16[4,128,256]{2,1,0:T(8,128...) custom-call(s32[3]{0:T(128)S(1)} %pad_add_fusion.where, ...), custom_call_target="tpu_custom_call" | custom-call | flops 3849999872 | tf_op jit(solution)/shard_map/qkv_second/pallas_call | solution.py:570
  62.5 1.5 collective-permute-done.14.start
  64.0 10.0 %block_second.1 = (bf16[512,512]{1,0:T(8,128)(2,1)S(1)}, f32[512,512]{1,0:T(8,128)S(1)}, bf16[512,512]{1,0:T(8,128)(2,1)S(1)}, bf16[512,256]{1,0:T(8,128)(2,1)S(...) custom-call(bf16[512,512]{1,0:T(8,128)(2,1)S(1)} %get-tuple-element., ...), custom_call_target="tpu_custom_call" | custom-call | flops 11000000512 | tf_op jit(solution)/shard_map/block_second/pallas_call | solution.py:570
  74.1 6.4 %ffn_back_first.1 = (f32[512,512]{1,0:T(8,128)S(1)}, bf16[512,512]{1,0:T(8,128)(2,1)S(1)}, bf16[512,512]{1,0:T(8,128)(2,1)S(1)}, bf16[4,128,256]{2,1,0:T(8,128)(2,1)S(1)}) custom-call(s32[3]{0:T(128)S(1)} %pad_add_fusion.where, f32[512,512]{1,0:T(8,128)S(1)} %get-tuple-element.164.own_g, bf16[512,2048]{1,0:T(8,128)(2,1)S(1)} %get-tuple-element.104.rest_0_.rest_1_, ...), custom_call_target="tpu_custom_call" | custom-call | flops 8249999872 | tf_op jit(solution)/shard_map/ffn_back_first/pallas_call | solution.py:570
  80.7 1.4 collective-permute-start.17
  82.1 7.7 %attention_back_first.1 = bf16[512,512]{1,0:T(8,128)(2,1)S(1)} custom-call(bf16[512,512]{1,0:T(8,128)(2,1)S(1)} %get-tuple-element.97.fq.rest_4_.rest_5_, bf16[512,512]{1,0:T(8,128)(2,1)S(1)} %get-tuple-element.98.fk, bf16[512,512]{1,0:T(8,128)(2,1)S(1)} %get-tuple-element.99.vv, bf16[512,512]{1,0:T(8,128)(2,1)S(1)} %get-tuple-element.108.dnum, ...), custom_call_target="tpu_custom_call" | custom-call | flops 8249999872 | tf_op jit(solution)/shard_map/attention_back_first/pallas_call | solution.py:570
  90.0 4.9 %collective-permute-done.17.p2 = bf16[512,512]{1,0:T(8,128)(2,1)S(1)} collective-permute-done((bf16[512,512]{1,0:T(8,128)(2,1)S(1)}, bf16[512,512]{1,0:T(8,128)(2,1)S(1)}, u32[]{:S(2)}, u32[]{:S(2)}) %collective-permute-start.17) | collective-permute-done | bytes 524320 | tf_op jit(solution)/shard_map/ppermute | solution.py:587
  94.9 1.5 collective-permute-start.19
  96.8 5.6 %activations.1 = (f32[2048,512]{1,0:T(8,128)}, f32[16,128]{1,0:T(8,128)}) custom-call(s32[3]{0:T(128)S(1)} %pad_add_fusion.where, bf16[512,512]{1,0:T(8,128)(2,1)S(1)} %get-tuple-element.113.p0, bf16[512,512]{1,0:T(8,128)(2,1)S(1)} %collective-permute-done.16.p1, bf16[512,512]{1,0:T(8,128)(2,1)S(1)} %collective-permute-done.17.p2, ...), custom_call_target="tpu_custom_call" | custom-call | flops 3300000000 | tf_op jit(solution)/shard_map/activations/pallas_call | solution.py:570
  102.4 6.8 %collective-permute-done.19.came.rest_0_ = bf16[512,512]{1,0:T(8,128)(2,1)S(1)} collective-permute-done((bf16[512,512]{1,0:T(8,128)(2,1)S(1)}, bf16[512,512]{1,0:T(8,128)(2,1)S(1)}, u32[]{:S(2)}, u32[]{:S(2)}) %collective-permute-start.19) | collective-permute-done | bytes 524320 | tf_op jit(solution)/shard_map/ppermute | solution.py:587
  109.2 1.9 collective-permute-done.20.came_two
  111.1 1.9 down_grad.1
  113.0 6.6 %ffn_back_second.1 = (f32[512,512]{1,0:T(8,128)S(1)}, bf16[512,512]{1,0:T(8,128)(2,1)S(1)}, bf16[512,512]{1,0:T(8,128)(2,1)S(1)}, bf16[4,128,256]{2,1,0:T(8,128)...) custom-call(s32[3]{0:T(128)S(1)} %pad_add_fusion.where, ...), custom_call_target="tpu_custom_call" | custom-call | flops 8249999872 | tf_op jit(solution)/shard_map/ffn_back_second/pallas_call | solution.py:570
  120.2 1.4 collective-permute-start.23
  121.6 1.5 collective-permute-done.24.normed_other
  123.1 1.3 up_grad.1
  124.3 9.8 %collective-permute-done.23.came = bf16[512,512]{1,0:T(8,128)(2,1)S(1)} collective-permute-done((bf16[512,512]{1,0:T(8,128)(2,1)S(1)}, bf16[512,512]{1,0:T(8,128)(2,1)S(1)}, u32[]{:S(2)}, u32[]{:S(2)}) %collective-permute-start.23) | collective-permute-done | bytes 524320 | tf_op jit(solution)/shard_map/ppermute | solution.py:587
  134.1 0.7 halve_down.1
  134.8 8.0 %attention_back_second.1 = (bf16[512,512]{1,0:T(8,128)(2,1)S(1)}, bf16[3,512,256]{2,1,0:T(8,128)(2,1)S(1)}, bf16[3,512,256]{2,1,0:T(8,128)(2,1)S(1)}, f32[8,512]{1,0:T(8,128)S(1)}) custom-call(bf16[512,512]{1,0:T(8,128)(2,1)S(1)} %get-tuple-element.97.fq.rest_4_.rest_5_, bf16[512,512]{1,0:T(8,128)(2,1)S(1)} %get-tuple-element.98.fk, ...), custom_call_target="tpu_custom_call" | custom-call | flops 8249999872 | tf_op jit(solution)/shard_map/attention_back_second/pallas_call | solution.py:570
  142.9 1.5 collective-permute-start.42
  144.4 1.6 collective-permute-start.30
  146.5 6.3 %collective-permute-done.30.came = bf16[256,512]{1,0:T(8,128)(2,1)S(1)} collective-permute-done((bf16[256,512]{1,0:T(8,128)(2,1)S(1)}, bf16[256,512]{1,0:T(8,128)(2,1)S(1)}, u32[]{:S(2)}, u32[]{:S(2)}) %collective-permute-start.30) | collective-permute-done | bytes 262176 | tf_op jit(solution)/shard_map/ppermute | solution.py:587
  152.8 0.6 halve_again_down.1
  153.4 3.9 %collective-permute-done.42.came = bf16[512,512]{1,0:T(8,128)(2,1)S(1)} collective-permute-done((bf16[512,512]{1,0:T(8,128)(2,1)S(1)}, bf16[512,512]{1,0:T(8,128)(2,1)S(1)}, u32[]{:S(2)}, u32[]{:S(2)}) %collective-permute-start.42) | collective-permute-done | bytes 524320 | tf_op jit(solution)/shard_map/ppermute | solution.py:587
  157.3 0.7 halve_up.1
  158.0 1.6 collective-permute-start.43
  159.6 1.3 late_grad.1
  160.9 1.6 collective-permute-start.35
  162.4 2.5 %collective-permute-start.47 = (bf16[128,512]{1,0:T(8,128)(2,1)S(1)}, bf16[128,512]{1,0:T(8,128)(2,1)S(1)}, u32[]{:S(2)}, u32[]{:S(2)}) collective-permute-start(bf16[128,512]{1,0:T(8,128)(2,1)S(1)} %get-tuple-element.142), channel_id=1, source_target_pairs={{0,12},{4,8},{8,4},{12,0},{1,13},{5,9},{9,5},{13,1},{2,14},{6,10},... | collective-permute-start | bytes 393224 | tf_op jit(solution)/shard_map/ppermute | solution.py:587
  165.4 1.3 collective-permute-done.43.came
  167.3 6.4 %collective-permute-start.44 = (bf16[128,512]{1,0:T(8,128)(2,1)S(1)}, bf16[128,512]{1,0:T(8,128)(2,1)S(1)}, u32[]{:S(2)}, u32[]{:S(2)}) collective-permute-start(bf16[128,512]{1,0:T(8,128)(2,1)S(1)} %get-tuple-element.159), channel_id=1, source_target_pairs={{0,12},{4,8},{8,4},{12,0},{1,13},{5,9},{9,5},{13,1},{2,14},{6,10},... | collective-permute-start | bytes 393224 | tf_op jit(solution)/shard_map/ppermute | solution.py:587
  173.9 4.0 %collective-permute-done.44.came = bf16[128,512]{1,0:T(8,128)(2,1)S(1)} collective-permute-done((bf16[128,512]{1,0:T(8,128)(2,1)S(1)}, bf16[128,512]{1,0:T(8,128)(2,1)S(1)}, u32[]{:S(2)}, u32[]{:S(2)}) %collective-permute-start.44) | collective-permute-done | bytes 131104 | tf_op jit(solution)/shard_map/ppermute | solution.py:587
  177.9 2.8 %collective-permute-start.45 = (bf16[128,512]{1,0:T(8,128)(2,1)S(1)}, bf16[128,512]{1,0:T(8,128)(2,1)S(1)}, u32[]{:S(2)}, u32[]{:S(2)}) collective-permute-start(bf16[128,512]{1,0:T(8,128)(2,1)S(1)} %sum_up.1.own), channel_id=1, source_target_pairs={{0,12},{4,8},{8,4},{12,0},{1,13},{5,9},{9,5},{13,1},{2,14},{6,10},... | collective-permute-start | bytes 393224 | tf_op jit(solution)/shard_map/ppermute | solution.py:587
  181.6 5.4 %collective-permute-start.49 = (bf16[256,512]{1,0:T(8,128)(2,1)S(1)}, bf16[256,512]{1,0:T(8,128)(2,1)S(1)}, u32[]{:S(2)}, u32[]{:S(2)}) collective-permute-start(bf16[256,512]{1,0:T(8,128)(2,1)S(1)} %pair_down.1.own), channel_id=1, source_target_pairs={{0,4},{4,0},{8,12},{12,8},{1,5},{5,1},{9,13},{13,9},{2,6},{6,2},{1... | collective-permute-start | bytes 786440 | tf_op jit(solution)/shard_map/ppermute | solution.py:587
  187.0 0.7 cut_late.1
  187.8 3.7 %collective-permute-start.37 = (bf16[528,128]{1,0:T(8,128)(2,1)S(1)}, bf16[528,128]{1,0:T(8,128)(2,1)S(1)}, u32[]{:S(2)}, u32[]{:S(2)}) collective-permute-start(bf16[528,128]{1,0:T(8,128)(2,1)S(1)} %get-tuple-element.150), channel_id=1, source_target_pairs={{0,8},{4,12},{8,0},{12,4},{1,9},{5,13},{9,1},{13,5},{2,10},{6,14},... | collective-permute-start | bytes 405512 | tf_op jit(solution)/shard_map/ppermute | solution.py:587
  192.2 1.4 collective-permute-start.38
  193.6 6.4 %collective-permute-done.36.one = bf16[528,128]{1,0:T(8,128)(2,1)S(1)} collective-permute-done((bf16[528,128]{1,0:T(8,128)(2,1)S(1)}, bf16[528,128]{1,0:T(8,128)(2,1)S(1)}, u32[]{:S(2)}, u32[]{:S(2)}) %collective-permute-start.36) | collective-permute-done | bytes 135200 | tf_op jit(solution)/shard_map/ppermute | solution.py:587
  200.5 7.2 %collective-permute-done.38.three = bf16[528,128]{1,0:T(8,128)(2,1)S(1)} collective-permute-done((bf16[528,128]{1,0:T(8,128)(2,1)S(1)}, bf16[528,128]{1,0:T(8,128)(2,1)S(1)}, u32[]{:S(2)}, u32[]{:S(2)}) %collective-permute-start.38) | collective-permute-done | bytes 135200 | tf_op jit(solution)/shard_map/ppermute | solution.py:587
  207.8 4.5 %collective-permute-start.40 = (bf16[528,128]{1,0:T(8,128)(2,1)S(1)}, bf16[528,128]{1,0:T(8,128)(2,1)S(1)}, u32[]{:S(2)}, u32[]{:S(2)}) collective-permute-start(bf16[528,128]{1,0:T(8,128)(2,1)S(1)} %add_late.1.own), channel_id=1, source_target_pairs={{0,8},{4,12},{8,0},{12,4},{1,9},{5,13},{9,1},{13,5},{2,10},{6,14},... | collective-permute-start | bytes 405512 | tf_op jit(solution)/shard_map/ppermute | solution.py:587
  212.4 1.6 whole_down.1
  213.9 1.6 whole_up.1
  215.5 5.2 %collective-permute-done.40.two = bf16[528,128]{1,0:T(8,128)(2,1)S(1)} collective-permute-done((bf16[528,128]{1,0:T(8,128)(2,1)S(1)}, bf16[528,128]{1,0:T(8,128)(2,1)S(1)}, u32[]{:S(2)}, u32[]{:S(2)}) %collective-permute-start.40) | collective-permute-done | bytes 135200 | tf_op jit(solution)/shard_map/ppermute | solution.py:587
  220.7 1.6 join_late.1
  222.4 2.9 %input_grad.1 = f32[2048,512]{1,0:T(8,128)} custom-call(s32[3]{0:T(128)S(1)} %pad_add_fusion.where, bf16[512,512]{1,0:T(8,128)(2,1)S(1)} %get-tuple-element.145.p0, bf16[512,512]{1,0:T(8,128)(2,1)S(1)} %collective-permute-done.32.p1, bf16[512,512]{1,0:T(8,128)(2,1)S(1)} %collective-permute-done.33.p2, bf16[512,512]{1,0:T(8,128)(2,1)S(1)} %collective-permute-done.34.p3), custom_call_target="tpu_custom_call" | custom-call | flops 3300000000 | tf_op jit(solution)/shard_map/input_grad/pallas_call | solution.py:570
  (103 shorter events, 10.1 us)
Async XLA Ops:
  0.6 13.3 %copy-start = (bf16[2048,512]{1,0:T(8,128)(2,1)S(1)}, bf16[2048,512]{1,0:T(8,128)(2,1)}, u32[]{:S(2)}) copy-start(bf16[2048,512]{1,0:T(8,128)(2,1)} %param.10) | copy-start | bytes 6291460
  0.7 13.3 %collective-permute-start.1 = (bf16[3,512,128]{2,1,0:T(8,128)(2,1)}, bf16[3,512,128]{2,1,0:T(8,128)(2,1)}, u32[]{:S(2)}, u32[]{:S(2)}) collective-permute-start(bf16[3,512,128]{2,1,0:T(8,128)(2,1)} %bitcast.53), channel_id=1, source_target_pairs={{0,2},{1,3},{2,0},{3,1},{4,6},{5,7},{6,4},{7,5},{8,10},{9,11},{10,... | collective-permute-start | bytes 1179656 | tf_op jit(solution)/shard_map/ppermute | solution.py:587
  3.7 12.2 %collective-permute-start = (bf16[3,512,128]{2,1,0:T(8,128)(2,1)}, bf16[3,512,128]{2,1,0:T(8,128)(2,1)}, u32[]{:S(2)}, u32[]{:S(2)}) collective-permute-start(bf16[3,512,128]{2,1,0:T(8,128)(2,1)} %bitcast.54), channel_id=1, source_target_pairs={{0,1},{1,0},{2,3},{3,2},{4,5},{5,4},{6,7},{7,6},{8,9},{9,8},{10,11... | collective-permute-start | bytes 1179656 | tf_op jit(solution)/shard_map/ppermute | solution.py:587
  3.7 18.9 %collective-permute-start.5 = (bf16[128,512]{1,0:T(8,128)(2,1)}, bf16[128,512]{1,0:T(8,128)(2,1)S(1)}, u32[]{:S(2)}, u32[]{:S(2)}) collective-permute-start(bf16[128,512]{1,0:T(8,128)(2,1)} %bitcast.56), channel_id=1, source_target_pairs={{0,2},{1,3},{2,0},{3,1},{4,6},{5,7},{6,4},{7,5},{8,10},{9,11},{10,... | collective-permute-start | bytes 393224 | tf_op jit(solution)/shard_map/ppermute | solution.py:587
  3.8 23.2 %collective-permute-start.8 = (bf16[512,512]{1,0:T(8,128)(2,1)}, bf16[512,512]{1,0:T(8,128)(2,1)S(1)}, u32[]{:S(2)}, u32[]{:S(2)}) collective-permute-start(bf16[512,512]{1,0:T(8,128)(2,1)} %bitcast.41), channel_id=1, source_target_pairs={{0,2},{1,3},{2,0},{3,1},{4,6},{5,7},{6,4},{7,5},{8,10},{9,11},{10,... | collective-permute-start | bytes 1572872 | tf_op jit(solution)/shard_map/ppermute | solution.py:587
  8.8 5.2 %copy-start.9 = (f32[512]{0:T(512)}, f32[512]{0:T(512)S(1)}, u32[]{:S(2)}) copy-start(f32[512]{0:T(512)S(1)} %get-tuple-element.170) | copy-start | bytes 6148
  13.9 2.1 collective-permute-start.2
  14.0 1.7 copy-start.10
  16.0 1.0 copy-start.4
  17.0 0.7 copy-start.6
  17.7 0.7 copy-start.8
  18.4 4.0 %copy-start.5 = (bf16[1,128,512]{2,1,0:T(8,128)(2,1)S(1)}, bf16[1,128,512]{2,1,0:T(8,128)(2,1)}, u32[]{:S(2)}) copy-start(bf16[1,128,512]{2,1,0:T(8,128)(2,1)} %param.15) | copy-start | bytes 393220
  18.4 4.5 %copy-start.2 = (bf16[1,512,512]{2,1,0:T(8,128)(2,1)S(1)}, bf16[1,512,512]{2,1,0:T(8,128)(2,1)}, u32[]{:S(2)}) copy-start(bf16[1,512,512]{2,1,0:T(8,128)(2,1)} %param.16) | copy-start | bytes 1572868
  18.4 8.7 %copy-start.3 = (bf16[1,512,512]{2,1,0:T(8,128)(2,1)S(1)}, bf16[1,512,512]{2,1,0:T(8,128)(2,1)}, u32[]{:S(2)}) copy-start(bf16[1,512,512]{2,1,0:T(8,128)(2,1)} %param.17) | copy-start | bytes 1572868
  18.4 10.9 %copy-start.7 = (f32[1,2,512]{2,1,0:T(2,128)S(1)}, f32[1,2,512]{2,1,0:T(2,128)}, u32[]{:S(2)}) copy-start(f32[1,2,512]{2,1,0:T(2,128)} %param.19) | copy-start | bytes 12292
  22.0 7.3 %collective-permute-start.3 = (bf16[4,128,256]{2,1,0:T(8,128)(2,1)S(1)}, bf16[4,128,256]{2,1,0:T(8,128)(2,1)S(1)}, u32[]{:S(2)}, u32[]{:S(2)}) collective-permute-start(bf16[4,128,256]{2,1,0:T(8,128)(2,1)S(1)} %get-tuple-element.90), channel_id=1, source_target_pairs={{0,1},{1,0},{2,3},{3,2},{4,5},{5,4},{6,7},{7,6},{8,9},{9,8},{10,11... | collective-permute-start | bytes 786440 | tf_op jit(solution)/shard_map/ppermute | solution.py:587
  22.4 6.4 %collective-permute-start.4 = (bf16[128,512]{1,0:T(8,128)(2,1)S(1)}, bf16[128,512]{1,0:T(8,128)(2,1)S(1)}, u32[]{:S(2)}, u32[]{:S(2)}) collective-permute-start(bf16[128,512]{1,0:T(8,128)(2,1)S(1)} %bitcast.57), channel_id=1, source_target_pairs={{0,1},{1,0},{2,3},{3,2},{4,5},{5,4},{6,7},{7,6},{8,9},{9,8},{10,11... | collective-permute-start | bytes 393224 | tf_op jit(solution)/shard_map/ppermute | solution.py:587
  22.6 6.2 %collective-permute-start.6 = (bf16[128,512]{1,0:T(8,128)(2,1)S(1)}, bf16[128,512]{1,0:T(8,128)(2,1)S(1)}, u32[]{:S(2)}, u32[]{:S(2)}) collective-permute-start(bf16[128,512]{1,0:T(8,128)(2,1)S(1)} %collective-permute-done.5.w2), channel_id=1, source_target_pairs={{0,1},{1,0},{2,3},{3,2},{4,5},{5,4},{6,7},{7,6},{8,9},{9,8},{10,11... | collective-permute-start | bytes 393224 | tf_op jit(solution)/shard_map/ppermute | solution.py:587
  22.9 17.2 %collective-permute-start.7 = (bf16[512,512]{1,0:T(8,128)(2,1)S(1)}, bf16[512,512]{1,0:T(8,128)(2,1)S(1)}, u32[]{:S(2)}, u32[]{:S(2)}) collective-permute-start(bf16[512,512]{1,0:T(8,128)(2,1)S(1)} %bitcast.42), channel_id=1, source_target_pairs={{0,1},{1,0},{2,3},{3,2},{4,5},{5,4},{6,7},{7,6},{8,9},{9,8},{10,11... | collective-permute-start | bytes 1572872 | tf_op jit(solution)/shard_map/ppermute | solution.py:587
  27.0 13.1 %collective-permute-start.11 = (bf16[512,512]{1,0:T(8,128)(2,1)S(1)}, bf16[512,512]{1,0:T(8,128)(2,1)S(1)}, u32[]{:S(2)}, u32[]{:S(2)}) collective-permute-start(bf16[512,512]{1,0:T(8,128)(2,1)S(1)} %bitcast.47), channel_id=1, source_target_pairs={{0,2},{1,3},{2,0},{3,1},{4,6},{5,7},{6,4},{7,5},{8,10},{9,11},{10,... | collective-permute-start | bytes 1572872 | tf_op jit(solution)/shard_map/ppermute | solution.py:587
  28.8 14.6 %collective-permute-start.10 = (bf16[512,512]{1,0:T(8,128)(2,1)S(1)}, bf16[512,512]{1,0:T(8,128)(2,1)S(1)}, u32[]{:S(2)}, u32[]{:S(2)}) collective-permute-start(bf16[512,512]{1,0:T(8,128)(2,1)S(1)} %bitcast.48), channel_id=1, source_target_pairs={{0,1},{1,0},{2,3},{3,2},{4,5},{5,4},{6,7},{7,6},{8,9},{9,8},{10,11... | collective-permute-start | bytes 1572872 | tf_op jit(solution)/shard_map/ppermute | solution.py:587
  28.8 11.4 %collective-permute-start.9 = (bf16[512,512]{1,0:T(8,128)(2,1)S(1)}, bf16[512,512]{1,0:T(8,128)(2,1)S(1)}, u32[]{:S(2)}, u32[]{:S(2)}) collective-permute-start(bf16[512,512]{1,0:T(8,128)(2,1)S(1)} %collective-permute-done.8.w2.u2.rest_10_.rest_11_), channel_id=1, source_target_pairs={{0,1},{1,0},{2,3},{3,2},{4,5},{5,4},{6,7},{7,6},{8,9},{9,8},{10,11... | collective-permute-start | bytes 1572872 | tf_op jit(solution)/shard_map/ppermute | solution.py:587
  40.1 3.3 %collective-permute-start.12 = (bf16[512,512]{1,0:T(8,128)(2,1)S(1)}, bf16[512,512]{1,0:T(8,128)(2,1)S(1)}, u32[]{:S(2)}, u32[]{:S(2)}) collective-permute-start(bf16[512,512]{1,0:T(8,128)(2,1)S(1)} %collective-permute-done.11.w2.d2.rest_14_.rest_15_), channel_id=1, source_target_pairs={{0,1},{1,0},{2,3},{3,2},{4,5},{5,4},{6,7},{7,6},{8,9},{9,8},{10,11... | collective-permute-start | bytes 1572872 | tf_op jit(solution)/shard_map/ppermute | solution.py:587
  44.9 14.4 %collective-permute-start.13 = (bf16[512,512]{1,0:T(8,128)(2,1)S(1)}, bf16[512,512]{1,0:T(8,128)(2,1)S(1)}, u32[]{:S(2)}, u32[]{:S(2)}) collective-permute-start(bf16[512,512]{1,0:T(8,128)(2,1)S(1)} %down_first.1), channel_id=1, source_target_pairs={{0,16},{16,0},{1,17},{17,1},{2,18},{18,2},{3,19},{19,3},{4,20},{20... | collective-permute-start | bytes 1572872 | tf_op jit(solution)/shard_map/ppermute | solution.py:587
  62.4 1.6 collective-permute-start.14
  80.5 1.6 collective-permute-start.15
  80.7 14.2 %collective-permute-start.17 = (bf16[512,512]{1,0:T(8,128)(2,1)S(1)}, bf16[512,512]{1,0:T(8,128)(2,1)S(1)}, u32[]{:S(2)}, u32[]{:S(2)}) collective-permute-start(bf16[512,512]{1,0:T(8,128)(2,1)S(1)} %get-tuple-element.113.p0), channel_id=1, source_target_pairs={{0,2},{1,3},{2,0},{3,1},{4,6},{5,7},{6,4},{7,5},{8,10},{9,11},{10,... | collective-permute-start | bytes 1572872 | tf_op jit(solution)/shard_map/ppermute | solution.py:587
  89.9 6.7 %collective-permute-start.16 = (bf16[512,512]{1,0:T(8,128)(2,1)S(1)}, bf16[512,512]{1,0:T(8,128)(2,1)S(1)}, u32[]{:S(2)}, u32[]{:S(2)}) collective-permute-start(bf16[512,512]{1,0:T(8,128)(2,1)S(1)} %get-tuple-element.113.p0), channel_id=1, source_target_pairs={{0,1},{1,0},{2,3},{3,2},{4,5},{5,4},{6,7},{7,6},{8,9},{9,8},{10,11... | collective-permute-start | bytes 1572872 | tf_op jit(solution)/shard_map/ppermute | solution.py:587
  94.9 1.9 collective-permute-start.18
  94.9 14.3 %collective-permute-start.19 = (bf16[512,512]{1,0:T(8,128)(2,1)S(1)}, bf16[512,512]{1,0:T(8,128)(2,1)S(1)}, u32[]{:S(2)}, u32[]{:S(2)}) collective-permute-start(bf16[512,512]{1,0:T(8,128)(2,1)S(1)} %attention_back_first.1), channel_id=1, source_target_pairs={{0,16},{16,0},{1,17},{17,1},{2,18},{18,2},{3,19},{19,3},{4,20},{20... | collective-permute-start | bytes 1572872 | tf_op jit(solution)/shard_map/ppermute | solution.py:587
  96.4 12.9 %collective-permute-start.21 = (bf16[512,1024]{1,0:T(8,128)(2,1)S(1)}, bf16[512,1024]{1,0:T(8,128)(2,1)S(1)}, u32[]{:S(2)}, u32[]{:S(2)}) collective-permute-start(bf16[512,1024]{1,0:T(8,128)(2,1)S(1)} %get-tuple-element.118), channel_id=1, source_target_pairs={{0,1},{1,0},{2,3},{3,2},{4,5},{5,4},{6,7},{7,6},{8,9},{9,8},{10,11... | collective-permute-start | bytes 3145736 | tf_op jit(solution)/shard_map/ppermute | solution.py:587
  109.2 1.9 collective-permute-start.20
  119.6 3.5 %collective-permute-start.25 = (bf16[512,1024]{1,0:T(8,128)(2,1)S(1)}, bf16[512,1024]{1,0:T(8,128)(2,1)S(1)}, u32[]{:S(2)}, u32[]{:S(2)}) collective-permute-start(bf16[512,1024]{1,0:T(8,128)(2,1)S(1)} %get-tuple-element.127), channel_id=1, source_target_pairs={{0,1},{1,0},{2,3},{3,2},{4,5},{5,4},{6,7},{7,6},{8,9},{9,8},{10,11... | collective-permute-start | bytes 3145736 | tf_op jit(solution)/shard_map/ppermute | solution.py:587
  119.8 3.3 %collective-permute-start.24 = (bf16[512,512]{1,0:T(8,128)(2,1)S(1)}, bf16[512,512]{1,0:T(8,128)(2,1)S(1)}, u32[]{:S(2)}, u32[]{:S(2)}) collective-permute-start(bf16[512,512]{1,0:T(8,128)(2,1)S(1)} %get-tuple-element.125.normed_own), channel_id=1, source_target_pairs={{0,1},{1,0},{2,3},{3,2},{4,5},{5,4},{6,7},{7,6},{8,9},{9,8},{10,11... | collective-permute-start | bytes 1572872 | tf_op jit(solution)/shard_map/ppermute | solution.py:587
  120.2 14.0 %collective-permute-start.23 = (bf16[512,512]{1,0:T(8,128)(2,1)S(1)}, bf16[512,512]{1,0:T(8,128)(2,1)S(1)}, u32[]{:S(2)}, u32[]{:S(2)}) collective-permute-start(bf16[512,512]{1,0:T(8,128)(2,1)S(1)} %get-tuple-element.119), channel_id=1, source_target_pairs={{0,2},{1,3},{2,0},{3,1},{4,6},{5,7},{6,4},{7,5},{8,10},{9,11},{10,... | collective-permute-start | bytes 1572872 | tf_op jit(solution)/shard_map/ppermute | solution.py:587
  121.6 13.2 %collective-permute-start.22 = (bf16[4,128,256]{2,1,0:T(8,128)(2,1)S(1)}, bf16[4,128,256]{2,1,0:T(8,128)(2,1)S(1)}, u32[]{:S(2)}, u32[]{:S(2)}) collective-permute-start(bf16[4,128,256]{2,1,0:T(8,128)(2,1)S(1)} %get-tuple-element.123), channel_id=1, source_target_pairs={{0,1},{1,0},{2,3},{3,2},{4,5},{5,4},{6,7},{7,6},{8,9},{9,8},{10,11... | collective-permute-start | bytes 786440 | tf_op jit(solution)/shard_map/ppermute | solution.py:587
  142.9 16.7 %collective-permute-start.27 = (bf16[3,512,256]{2,1,0:T(8,128)(2,1)S(1)}, bf16[3,512,256]{2,1,0:T(8,128)(2,1)S(1)}, u32[]{:S(2)}, u32[]{:S(2)}) collective-permute-start(bf16[3,512,256]{2,1,0:T(8,128)(2,1)S(1)} %get-tuple-element.137), channel_id=1, source_target_pairs={{0,1},{1,0},{2,3},{3,2},{4,5},{5,4},{6,7},{7,6},{8,9},{9,8},{10,11... | collective-permute-start | bytes 2359304 | tf_op jit(solution)/shard_map/ppermute | solution.py:587
  142.9 14.3 %collective-permute-start.42 = (bf16[512,512]{1,0:T(8,128)(2,1)S(1)}, bf16[512,512]{1,0:T(8,128)(2,1)S(1)}, u32[]{:S(2)}, u32[]{:S(2)}) collective-permute-start(bf16[512,512]{1,0:T(8,128)(2,1)S(1)} %get-tuple-element.128), channel_id=1, source_target_pairs={{0,2},{1,3},{2,0},{3,1},{4,6},{5,7},{6,4},{7,5},{8,10},{9,11},{10,... | collective-permute-start | bytes 1572872 | tf_op jit(solution)/shard_map/ppermute | solution.py:587
  144.4 8.4 %collective-permute-start.30 = (bf16[256,512]{1,0:T(8,128)(2,1)S(1)}, bf16[256,512]{1,0:T(8,128)(2,1)S(1)}, u32[]{:S(2)}, u32[]{:S(2)}) collective-permute-start(bf16[256,512]{1,0:T(8,128)(2,1)S(1)} %get-tuple-element.130), channel_id=1, source_target_pairs={{0,4},{4,0},{8,12},{12,8},{1,5},{5,1},{9,13},{13,9},{2,6},{6,2},{1... | collective-permute-start | bytes 786440 | tf_op jit(solution)/shard_map/ppermute | solution.py:587
  146.0 13.5 %collective-permute-start.26 = (bf16[512,512]{1,0:T(8,128)(2,1)S(1)}, bf16[512,512]{1,0:T(8,128)(2,1)S(1)}, u32[]{:S(2)}, u32[]{:S(2)}) collective-permute-start(bf16[512,512]{1,0:T(8,128)(2,1)S(1)} %get-tuple-element.135.normed_own), channel_id=1, source_target_pairs={{0,1},{1,0},{2,3},{3,2},{4,5},{5,4},{6,7},{7,6},{8,9},{9,8},{10,11... | collective-permute-start | bytes 1572872 | tf_op jit(solution)/shard_map/ppermute | solution.py:587
  146.0 13.5 %collective-permute-start.29 = (bf16[512,512]{1,0:T(8,128)(2,1)S(1)}, bf16[512,512]{1,0:T(8,128)(2,1)S(1)}, u32[]{:S(2)}, u32[]{:S(2)}) collective-permute-start(bf16[512,512]{1,0:T(8,128)(2,1)S(1)} %get-tuple-element.139.dattn_own), channel_id=1, source_target_pairs={{0,1},{1,0},{2,3},{3,2},{4,5},{5,4},{6,7},{7,6},{8,9},{9,8},{10,11... | collective-permute-start | bytes 1572872 | tf_op jit(solution)/shard_map/ppermute | solution.py:587
  152.8 5.1 %collective-permute-start.28 = (bf16[512,256]{1,0:T(8,128)(2,1)S(1)}, bf16[512,256]{1,0:T(8,128)(2,1)S(1)}, u32[]{:S(2)}, u32[]{:S(2)}) collective-permute-start(bf16[512,256]{1,0:T(8,128)(2,1)S(1)} %get-tuple-element.138), channel_id=1, source_target_pairs={{0,1},{1,0},{2,3},{3,2},{4,5},{5,4},{6,7},{7,6},{8,9},{9,8},{10,11... | collective-permute-start | bytes 786440 | tf_op jit(solution)/shard_map/ppermute | solution.py:587
  157.3 2.3 %collective-permute-start.31 = (f32[8,512]{1,0:T(8,128)S(1)}, f32[8,512]{1,0:T(8,128)S(1)}, u32[]{:S(2)}, u32[]{:S(2)}) collective-permute-start(f32[8,512]{1,0:T(8,128)S(1)} %get-tuple-element.143.sums_own), channel_id=1, source_target_pairs={{0,1},{1,0},{2,3},{3,2},{4,5},{5,4},{6,7},{7,6},{8,9},{9,8},{10,11... | collective-permute-start | bytes 49160 | tf_op jit(solution)/shard_map/ppermute | solution.py:587
  158.0 8.8 %collective-permute-start.43 = (bf16[256,512]{1,0:T(8,128)(2,1)S(1)}, bf16[256,512]{1,0:T(8,128)(2,1)S(1)}, u32[]{:S(2)}, u32[]{:S(2)}) collective-permute-start(bf16[256,512]{1,0:T(8,128)(2,1)S(1)} %get-tuple-element.157), channel_id=1, source_target_pairs={{0,4},{4,0},{8,12},{12,8},{1,5},{5,1},{9,13},{13,9},{2,6},{6,2},{1... | collective-permute-start | bytes 786440 | tf_op jit(solution)/shard_map/ppermute | solution.py:587
  160.9 26.2 %collective-permute-start.35 = (bf16[2112,128]{1,0:T(8,128)(2,1)S(1)}, bf16[2112,128]{1,0:T(8,128)(2,1)S(1)}, u32[]{:S(2)}, u32[]{:S(2)}) collective-permute-start(bf16[2112,128]{1,0:T(8,128)(2,1)S(1)} %get-tuple-element.144), channel_id=1, source_target_pairs={{0,2},{1,3},{2,0},{3,1},{4,6},{5,7},{6,4},{7,5},{8,10},{9,11},{10,... | collective-permute-start | bytes 1622024 | tf_op jit(solution)/shard_map/ppermute | solution.py:587
  162.4 11.3 %collective-permute-start.47 = (bf16[128,512]{1,0:T(8,128)(2,1)S(1)}, bf16[128,512]{1,0:T(8,128)(2,1)S(1)}, u32[]{:S(2)}, u32[]{:S(2)}) collective-permute-start(bf16[128,512]{1,0:T(8,128)(2,1)S(1)} %get-tuple-element.142), channel_id=1, source_target_pairs={{0,12},{4,8},{8,4},{12,0},{1,13},{5,9},{9,5},{13,1},{2,14},{6,10},... | collective-permute-start | bytes 393224 | tf_op jit(solution)/shard_map/ppermute | solution.py:587
  164.9 27.3 %collective-permute-start.33 = (bf16[512,512]{1,0:T(8,128)(2,1)S(1)}, bf16[512,512]{1,0:T(8,128)(2,1)S(1)}, u32[]{:S(2)}, u32[]{:S(2)}) collective-permute-start(bf16[512,512]{1,0:T(8,128)(2,1)S(1)} %get-tuple-element.145.p0), channel_id=1, source_target_pairs={{0,2},{1,3},{2,0},{3,1},{4,6},{5,7},{6,4},{7,5},{8,10},{9,11},{10,... | collective-permute-start | bytes 1572872 | tf_op jit(solution)/shard_map/ppermute | solution.py:587
  167.3 10.5 %collective-permute-start.44 = (bf16[128,512]{1,0:T(8,128)(2,1)S(1)}, bf16[128,512]{1,0:T(8,128)(2,1)S(1)}, u32[]{:S(2)}, u32[]{:S(2)}) collective-permute-start(bf16[128,512]{1,0:T(8,128)(2,1)S(1)} %get-tuple-element.159), channel_id=1, source_target_pairs={{0,12},{4,8},{8,4},{12,0},{1,13},{5,9},{9,5},{13,1},{2,14},{6,10},... | collective-permute-start | bytes 393224 | tf_op jit(solution)/shard_map/ppermute | solution.py:587
  173.8 7.2 %collective-permute-start.48 = (bf16[128,512]{1,0:T(8,128)(2,1)S(1)}, bf16[128,512]{1,0:T(8,128)(2,1)S(1)}, u32[]{:S(2)}, u32[]{:S(2)}) collective-permute-start(bf16[128,512]{1,0:T(8,128)(2,1)S(1)} %sum_down.1.own), channel_id=1, source_target_pairs={{0,12},{4,8},{8,4},{12,0},{1,13},{5,9},{9,5},{13,1},{2,14},{6,10},... | collective-permute-start | bytes 393224 | tf_op jit(solution)/shard_map/ppermute | solution.py:587
  177.9 13.6 %collective-permute-start.45 = (bf16[128,512]{1,0:T(8,128)(2,1)S(1)}, bf16[128,512]{1,0:T(8,128)(2,1)S(1)}, u32[]{:S(2)}, u32[]{:S(2)}) collective-permute-start(bf16[128,512]{1,0:T(8,128)(2,1)S(1)} %sum_up.1.own), channel_id=1, source_target_pairs={{0,12},{4,8},{8,4},{12,0},{1,13},{5,9},{9,5},{13,1},{2,14},{6,10},... | collective-permute-start | bytes 393224 | tf_op jit(solution)/shard_map/ppermute | solution.py:587
  181.6 26.2 %collective-permute-start.49 = (bf16[256,512]{1,0:T(8,128)(2,1)S(1)}, bf16[256,512]{1,0:T(8,128)(2,1)S(1)}, u32[]{:S(2)}, u32[]{:S(2)}) collective-permute-start(bf16[256,512]{1,0:T(8,128)(2,1)S(1)} %pair_down.1.own), channel_id=1, source_target_pairs={{0,4},{4,0},{8,12},{12,8},{1,5},{5,1},{9,13},{13,9},{2,6},{6,2},{1... | collective-permute-start | bytes 786440 | tf_op jit(solution)/shard_map/ppermute | solution.py:587
  187.7 12.3 %collective-permute-start.36 = (bf16[528,128]{1,0:T(8,128)(2,1)S(1)}, bf16[528,128]{1,0:T(8,128)(2,1)S(1)}, u32[]{:S(2)}, u32[]{:S(2)}) collective-permute-start(bf16[528,128]{1,0:T(8,128)(2,1)S(1)} %get-tuple-element.149), channel_id=1, source_target_pairs={{0,4},{4,0},{8,12},{12,8},{1,5},{5,1},{9,13},{13,9},{2,6},{6,2},{1... | collective-permute-start | bytes 405512 | tf_op jit(solution)/shard_map/ppermute | solution.py:587
  187.8 12.2 %collective-permute-start.37 = (bf16[528,128]{1,0:T(8,128)(2,1)S(1)}, bf16[528,128]{1,0:T(8,128)(2,1)S(1)}, u32[]{:S(2)}, u32[]{:S(2)}) collective-permute-start(bf16[528,128]{1,0:T(8,128)(2,1)S(1)} %get-tuple-element.150), channel_id=1, source_target_pairs={{0,8},{4,12},{8,0},{12,4},{1,9},{5,13},{9,1},{13,5},{2,10},{6,14},... | collective-permute-start | bytes 405512 | tf_op jit(solution)/shard_map/ppermute | solution.py:587
  192.0 20.3 %collective-permute-start.46 = (bf16[256,512]{1,0:T(8,128)(2,1)S(1)}, bf16[256,512]{1,0:T(8,128)(2,1)S(1)}, u32[]{:S(2)}, u32[]{:S(2)}) collective-permute-start(bf16[256,512]{1,0:T(8,128)(2,1)S(1)} %pair_up.1.own), channel_id=1, source_target_pairs={{0,4},{4,0},{8,12},{12,8},{1,5},{5,1},{9,13},{13,9},{2,6},{6,2},{1... | collective-permute-start | bytes 786440 | tf_op jit(solution)/shard_map/ppermute | solution.py:587
  192.2 15.5 %collective-permute-start.38 = (bf16[528,128]{1,0:T(8,128)(2,1)S(1)}, bf16[528,128]{1,0:T(8,128)(2,1)S(1)}, u32[]{:S(2)}, u32[]{:S(2)}) collective-permute-start(bf16[528,128]{1,0:T(8,128)(2,1)S(1)} %get-tuple-element.151), channel_id=1, source_target_pairs={{0,12},{4,8},{8,4},{12,0},{1,13},{5,9},{9,5},{13,1},{2,14},{6,10},... | collective-permute-start | bytes 405512 | tf_op jit(solution)/shard_map/ppermute | solution.py:587
  200.0 22.4 %collective-permute-start.32 = (bf16[512,512]{1,0:T(8,128)(2,1)S(1)}, bf16[512,512]{1,0:T(8,128)(2,1)S(1)}, u32[]{:S(2)}, u32[]{:S(2)}) collective-permute-start(bf16[512,512]{1,0:T(8,128)(2,1)S(1)} %get-tuple-element.145.p0), channel_id=1, source_target_pairs={{0,1},{1,0},{2,3},{3,2},{4,5},{5,4},{6,7},{7,6},{8,9},{9,8},{10,11... | collective-permute-start | bytes 1572872 | tf_op jit(solution)/shard_map/ppermute | solution.py:587
  200.0 22.4 %collective-permute-start.34 = (bf16[512,512]{1,0:T(8,128)(2,1)S(1)}, bf16[512,512]{1,0:T(8,128)(2,1)S(1)}, u32[]{:S(2)}, u32[]{:S(2)}) collective-permute-start(bf16[512,512]{1,0:T(8,128)(2,1)S(1)} %collective-permute-done.33.p2), channel_id=1, source_target_pairs={{0,1},{1,0},{2,3},{3,2},{4,5},{5,4},{6,7},{7,6},{8,9},{9,8},{10,11... | collective-permute-start | bytes 1572872 | tf_op jit(solution)/shard_map/ppermute | solution.py:587
  207.7 7.8 %collective-permute-start.39 = (bf16[528,128]{1,0:T(8,128)(2,1)S(1)}, bf16[528,128]{1,0:T(8,128)(2,1)S(1)}, u32[]{:S(2)}, u32[]{:S(2)}) collective-permute-start(bf16[528,128]{1,0:T(8,128)(2,1)S(1)} %add_late.1.own), channel_id=1, source_target_pairs={{0,4},{4,0},{8,12},{12,8},{1,5},{5,1},{9,13},{13,9},{2,6},{6,2},{1... | collective-permute-start | bytes 405512 | tf_op jit(solution)/shard_map/ppermute | solution.py:587
  207.8 12.9 %collective-permute-start.40 = (bf16[528,128]{1,0:T(8,128)(2,1)S(1)}, bf16[528,128]{1,0:T(8,128)(2,1)S(1)}, u32[]{:S(2)}, u32[]{:S(2)}) collective-permute-start(bf16[528,128]{1,0:T(8,128)(2,1)S(1)} %add_late.1.own), channel_id=1, source_target_pairs={{0,8},{4,12},{8,0},{12,4},{1,9},{5,13},{9,1},{13,5},{2,10},{6,14},... | collective-permute-start | bytes 405512 | tf_op jit(solution)/shard_map/ppermute | solution.py:587
  212.4 8.4 %collective-permute-start.41 = (bf16[528,128]{1,0:T(8,128)(2,1)S(1)}, bf16[528,128]{1,0:T(8,128)(2,1)S(1)}, u32[]{:S(2)}, u32[]{:S(2)}) collective-permute-start(bf16[528,128]{1,0:T(8,128)(2,1)S(1)} %add_late.1.own), channel_id=1, source_target_pairs={{0,12},{4,8},{8,4},{12,0},{1,13},{5,9},{9,5},{13,1},{2,14},{6,10},... | collective-permute-start | bytes 405512 | tf_op jit(solution)/shard_map/ppermute | solution.py:587
  222.3 2.9 %copy-start.1 = (bf16[2048,512]{1,0:T(8,128)(2,1)S(1)}, bf16[2048,512]{1,0:T(8,128)(2,1)}, u32[]{:S(2)}) copy-start(bf16[2048,512]{1,0:T(8,128)(2,1)} %param.10) | copy-start | bytes 6291460

commit v3 on v2

--- a/solution.py
+++ b/solution.py
@@ -19,6 +19,7 @@
 GELU_C = 0.7978845608028654
 GELU_A = 0.044715
 SPLIT = 1.0 / 32.0
+LOW = 0.02
 VMEM_LIMIT = 16 * 1024 * 1024
 
 SECTION, PLACE, DEPTH = range(3)
@@ -73,7 +74,7 @@
 
 def row_tiles(total, step=ROWS):
     def decorate(body):
-        pl.loop(0, total // step)(
+        pl.loop(0, total // step, unroll=True)(
             lambda index: body(pl.ds(pl.multiple_of(index * step, step), step))
         )
 
@@ -96,10 +97,10 @@
         span = slice(chunk * CHUNK, (chunk + 1) * CHUNK)
         same = cols_ref[span, SEG : SEG + 1] == seg_ref[0:1, span]
         if mask is not None:
-            lower = (same & (col <= row)).astype(F32)
+            lower = (same & (col <= row)).astype(F32).astype(BF16)
             mask[chunk] = jnp.concatenate([lower, lower], axis=1)
         if mask_t is not None:
-            upper = (same & (row <= col)).astype(F32)
+            upper = (same & (row <= col)).astype(F32).astype(BF16)
             mask_t[chunk] = jnp.concatenate([upper, upper], axis=1)
 
 
@@ -143,13 +144,11 @@
         state[pair] = (diag * tn(tail, side(vv[:, lanes], 1.0))).astype(BF16)
 
 
-def attention_forward(fq, fk, vv, start, cols, seg, o, inv_den, states, mask):
-    chunk_masks(cols, seg, mask, None)
+def attention_forward(fq, fk, vv, start, cols, o, inv_den, states, mask):
     diag = diagonal_blocks()
 
-    @pl.loop(0, start.shape[0])
-    def _(pair):
-        lanes = pl.ds(pl.multiple_of(pair * LANES, LANES), LANES)
+    for pair in range(start.shape[0]):
+        lanes = slice(pair * LANES, (pair + 1) * LANES)
         state = start[pair ^ 1].astype(F32)
         for chunk in range(fq.shape[0] // CHUNK):
             span = slice(chunk * CHUNK, (chunk + 1) * CHUNK)
@@ -159,7 +158,7 @@
             state_low = state.astype(BF16)
             if states is not None:
                 states[pair, chunk] = state_low
-            scores = (nt(query, split_pair(key)) * mask[chunk]).astype(BF16)
+            scores = nt(query, split_pair(key)).astype(BF16) * mask[chunk]
             ones = split_pair(jnp.ones_like(value))
             values = jnp.concatenate([split_pair(value), ones], axis=1)
             both = nn(scores, values) + carried * nn(query, state_low)
@@ -198,7 +197,8 @@
     copies = start_copies(
         (w0, w1, w2, w3), lambda r: w.at[r * LANES : (r + 1) * LANES, :], sems, 0
     )
-    attention_forward(fq, fk, vv, start, cols, seg, o, None, None, mask)
+    chunk_masks(cols, seg, mask, None)
+    attention_forward(fq, fk, vv, start, cols, o, None, None, mask)
     for copy in copies:
         copy.wait()
     out_and_norm(o, x, w, gain, bias, mid, normed_two)
@@ -227,9 +227,10 @@
 
 def block_kernel(
     fq, fk, vv, start, cols, seg, x, gain, bias, out_w, u0, u1, u2, u3, d0, d1, d2, d3,
-    y, mid, o, o_send, inv_den, states, keep, send, slope, normed_two, mask,
+    y, mid, o, o_send, inv_den, states, keep, send, slope, normed_two, mask, mask_t,
 ):
-    attention_forward(fq, fk, vv, start, cols, seg, o, inv_den, states, mask)
+    chunk_masks(cols, seg, mask, mask_t)
+    attention_forward(fq, fk, vv, start, cols, o, inv_den, states, mask)
     for slot, r in enumerate((1, 3)):
         o_send[:, slot * LANES : (slot + 1) * LANES] = o[:, r * LANES : (r + 1) * LANES]
     out_and_norm(o, x, out_w, gain, bias, mid, normed_two)
@@ -250,48 +251,57 @@
         y[rows, :] = total.astype(BF16)
 
 
-def ffn_back_kernel(with_weights, where, own_g, *rest):
-    if with_weights:
+def ffn_rows(rows, gy, slope, up_w, down_w, save):
+    width = up_w[0].shape[1]
+    dffn = gy[rows, :].astype(BF16)
+    grad = jnp.zeros(dffn.shape, F32)
+    for r in range(4):
+        units = slice(r * width, (r + 1) * width)
+        dup = (slope[rows, units].astype(F32) * nn(dffn, down_w[r][...])).astype(BF16)
+        if save is not None:
+            half = slice(r // 2 * width, (r // 2 + 1) * width)
+            save[r % 2][rows, half] = dup
+        grad = grad + nt(dup, up_w[r][...])
+    return grad
+
+
+def ffn_back_kernel(second, where, own_g, *rest):
+    if second:
         came, rest = rest[0], rest[1:]
     slope, mid, o, inv_den, fq, cols, gain, out_w, *rest = rest
     up_w, down_w = rest[0:4], rest[4:8]
-    grad_mid, dnum, dden, grad_state, *rest = rest[8:]
-    if with_weights:
-        dup_keep, dup_send, dattn, sums, gy = rest
-    else:
-        (dattn,) = rest
-        gy = own_g
-    width = up_w[0].shape[1]
-    total = gy.shape[0]
-    if with_weights:
-
-        @row_tiles(total)
+    grad_mid, dnum, dden, grad_state, dattn, *rest = rest[8:]
+    gy, save, sums = own_g, None, None
+    if second:
+        *save, sums, gy = rest
+
+        @row_tiles(gy.shape[0])
         def _(rows):
             gy[rows, :] = jnp.where(
                 where[SECTION] == 1, own_g[rows, :], came[rows, :].astype(F32)
             )
 
-    @row_tiles(total, 256)
-    def _(rows):
-        dffn = gy[rows, :].astype(BF16)
-        grad = jnp.zeros(dffn.shape, F32)
-        for r in range(4):
-            units = slice(r * width, (r + 1) * width)
-            dup = (slope[rows, units].astype(F32) * nn(dffn, down_w[r][...])).astype(BF16)
-            if with_weights:
-                half = slice(r // 2 * width, (r // 2 + 1) * width)
-                (dup_send if r % 2 else dup_keep)[rows, half] = dup
-            grad = grad + nt(dup, up_w[r][...])
-        grad_mid[rows, :] = grad
-
-    if with_weights:
+    @row_tiles(gy.shape[0], 256)
+    def _(rows):
+        grad_mid[rows, :] = ffn_rows(rows, gy, slope, up_w, down_w, save)
+
+    mid_back(
+        gy, mid, o, inv_den, fq, cols, gain, out_w, grad_mid, dnum, dden, grad_state, dattn, sums
+    )
+
+
+def mid_back(
+    gy, mid, o, inv_den, fq, cols, gain, out_w, grad_mid, dnum, dden, grad_state, dattn, sums
+):
+    total = gy.shape[0]
+    if sums is not None:
         sums[...] = jnp.zeros_like(sums)
 
     @row_tiles(total)
     def _(rows):
         unit, scale = normalise(mid[rows, :])
         grad = grad_mid[rows, :]
-        if with_weights:
+        if sums is not None:
             sums[0:1, :] += jnp.sum(grad * unit, axis=0, keepdims=True)
             sums[1:2, :] += jnp.sum(grad, axis=0, keepdims=True)
         grad = gy[rows, :] + norm_backward(grad, unit, scale, gain[1:2, :])
@@ -327,21 +337,19 @@
 
 
 def attention_back_kernel(
-    with_weights, fq, fk, vv, dnum, dden, states, end, cols, seg, x, grad_mid, gain, w, *rest
+    with_weights, fq, fk, vv, dnum, dden, states, end, cols, mask, mask_t, x, grad_mid, gain, w, *rest
 ):
     if with_weights:
         sums_two, grad_x, keep, send, sums, *rest = rest
     else:
         grad_x, *rest = rest
-    mask, mask_t, acc, dproj = rest
-    chunk_masks(cols, seg, mask, mask_t)
+    acc, dproj = rest
     diag = diagonal_blocks()
     lane = lax.broadcasted_iota(jnp.int32, (1, PAIR), 1)
     share = jnp.where(lane < LANES, 1.0, SPLIT)
 
-    @pl.loop(0, end.shape[0])
-    def _(pair):
-        lanes = pl.ds(pl.multiple_of(pair * LANES, LANES), LANES)
+    for pair in range(end.shape[0]):
+        lanes = slice(pair * LANES, (pair + 1) * LANES)
         grad_state = end[pair ^ 1].astype(F32)
         for chunk in reversed(range(fq.shape[0] // CHUNK)):
             span = slice(chunk * CHUNK, (chunk + 1) * CHUNK)
@@ -357,9 +365,9 @@
             share_two = split_pair(jnp.full(value.shape, SPLIT, BF16))
             values_two = jnp.concatenate([split_pair(value), share_two], axis=1)
             values = side(value, SPLIT)
-            scores_t = (nt(key, query_two) * mask_t[chunk]).astype(BF16)
-            dscores = (nt(both, values_two) * mask[chunk]).astype(BF16)
-            dscores_t = (nt(values, both_two) * mask_t[chunk]).astype(BF16)
+            scores_t = nt(key, query_two).astype(BF16) * mask_t[chunk]
+            dscores = nt(both, values_two).astype(BF16) * mask[chunk]
+            dscores_t = nt(values, both_two).astype(BF16) * mask_t[chunk]
             state = (states[pair, chunk].astype(F32) * share).astype(BF16)
             grad_low = grad_state.astype(BF16)
             dfq = nn(dscores, split_pair(key)) + carried * nt(both, state)
@@ -452,27 +460,6 @@
         place[last + small.shape[0] :, :] = jnp.zeros((left, LANES), BF16)
 
 
-def part_rows(where, r, size):
-    return pl.ds(pl.multiple_of((where[DEPTH] ^ r) * size, 16), size)
-
-
-def cut_kernel(where, keep, came, *outs):
-    for r, out in enumerate(outs):
-        rows = part_rows(where, r, out.shape[0])
-        total = keep[rows, :].astype(F32) + came[rows, :].astype(F32)
-        out[...] = total.astype(out.dtype)
-
-
-def add_kernel(own, one, two, three, out):
-    total = own[...] + one[...].astype(F32) + two[...].astype(F32) + three[...].astype(F32)
-    out[...] = total.astype(BF16)
-
-
-def join_kernel(where, own, one, two, three, out):
-    for r, part in enumerate((own, one, two, three)):
-        out[part_rows(where, r, part.shape[0]), :] = part[...].astype(F32)
-
-
 def unpack_late(source, qkv, out, gains, biases):
     width = out.shape[1]
     base = 3 * width
@@ -488,8 +475,8 @@
             place[v % 2 : v % 2 + 1, cols] = source[row : row + 1, :].astype(F32)
 
 
-def join_late_kernel(where, own, one, two, three, qkv, out, gains, biases, whole):
-    join_kernel(where, own, one, two, three, whole)
+def join_late_kernel(where, own, came, qkv, out, gains, biases, whole):
+    whole_kernel(where, own, came, whole)
     unpack_late(whole, qkv, out, gains, biases)
 
 
@@ -498,44 +485,29 @@
     unpack_late(whole, qkv, out, gains, biases)
 
 
-def halves(where):
+def my_half(where):
     depth = where[DEPTH]
-    return (depth ^ (depth >> 1)) & 1, depth >> 1
+    return (depth ^ (depth >> 1)) & 1
 
 
 def rows_at(index, size):
     return pl.ds(pl.multiple_of(index * size, 16), size)
 
 
-def halve_first_kernel(where, keep, came, stays, goes):
-    mine, _ = halves(where)
+def halve_kernel(where, keep, came, stays, goes):
+    mine = my_half(where)
     size = stays.shape[0]
     for index, out in ((mine, stays), (1 - mine, goes)):
         rows = rows_at(index, size)
         out[...] = (keep[rows, :].astype(F32) + came[rows, :].astype(F32)).astype(out.dtype)
 
 
-def halve_second_kernel(where, keep, came, stays, goes):
-    _, mine = halves(where)
-    size = stays.shape[0]
-    for index, out in ((mine, stays), (1 - mine, goes)):
-        rows = rows_at(index, size)
-        out[...] = (keep[rows, :] + came[rows, :].astype(F32)).astype(out.dtype)
-
-
 def sum_kernel(keep, came, out):
-    out[...] = (keep[...] + came[...].astype(F32)).astype(BF16)
-
-
-def pair_kernel(where, own, came, out):
-    _, mine = halves(where)
-    size = own.shape[0]
-    out[rows_at(mine, size), :] = own[...]
-    out[rows_at(1 - mine, size), :] = came[...]
+    out[...] = (keep[...].astype(F32) + came[...].astype(F32)).astype(BF16)
 
 
 def whole_kernel(where, own, came, out):
-    mine, _ = halves(where)
+    mine = my_half(where)
     size = own.shape[0]
     out[rows_at(mine, size), :] = own[...].astype(F32)
     out[rows_at(1 - mine, size), :] = came[...].astype(F32)
@@ -546,7 +518,7 @@
     for r, part in enumerate((p0, p1, p2, p3)):
         begin = where[PLACE] ^ r
 
-        @pl.loop(0, total // LANES)
+        @pl.loop(0, total // LANES, unroll=True)
         def _(tile, part=part, begin=begin):
             block = part[pl.ds(pl.multiple_of(tile * LANES, LANES), LANES), :].astype(F32)
             to = begin * (total // LANES) + tile
@@ -555,9 +527,12 @@
                 square = block * block
                 high = square.astype(BF16)
                 low = (square - high.astype(F32)).astype(BF16)
-                ones = jnp.ones((8, width), BF16)
-                mean = (nt(ones, high) + nt(ones, low)) * (1.0 / width)
-                rms[0][pl.ds(to, 1), :] = jnp.sqrt(mean[0:1, :] + 1e-06)
+                ones = jnp.ones((width, LANES), BF16)
+                mean = (nn(high, ones) + nn(low, ones)) * (1.0 / width)
+                row = lax.broadcasted_iota(jnp.int32, (LANES, LANES), 0)
+                col = lax.broadcasted_iota(jnp.int32, (LANES, LANES), 1)
+                mean = jnp.sum(jnp.where(row == col, mean, 0.0), axis=0, keepdims=True)
+                rms[0][pl.ds(to, 1), :] = jnp.sqrt(mean + 1e-06)
 
 
 IN_VMEM = pl.BlockSpec(memory_space=pltpu.VMEM)
@@ -595,47 +570,22 @@
     return lax.optimization_barrier((value, *others))[0]
 
 
-def sum_rows(keep, send, where, join, name):
-    came = across(send, 2)
-    rows, width = keep.shape
-    depth = lax.axis_size("dp")
-    if depth != 4:
-        total = (keep.astype(F32) + came.astype(F32)).astype(BF16)
-        return join(where, lax.psum(total, "dp"))
-    part = (rows // depth, width)
-    own, *parts = call(
-        cut_kernel, (where, keep, came), [(part, F32)] + [(part, BF16)] * 3, [], "cut" + name, 0.7
-    )
-    parts = [across(v, r + 1, "dp") for r, v in enumerate(parts)]
-    (own,) = call(add_kernel, (own, *parts), [(part, BF16)], [], "add" + name, 0.7)
-    return join(where, own, *[across(own, r, "dp") for r in (1, 2, 3)])
-
-
-def halving_sum(keep, came, where, name):
+def sum_over_dp(keep, came, where, name, join):
     rows, width = keep.shape
     if lax.axis_size("dp") != 4:
         total = (keep.astype(F32) + came.astype(F32)).astype(BF16)
-        yield total
-        yield total
-        yield lax.psum(total, "dp").astype(F32)
-        return
-    half, quarter = (rows // 2, width), (rows // 4, width)
+        return join(lax.psum(total, "dp"))
+    half = (rows // 2, width)
     stays, goes = call(
-        halve_first_kernel, (where, keep, came), [(half, F32), (half, BF16)], [], "halve_" + name, 0.8
-    )
-    came = across(goes, 1, "dp")
-    yield goes
-    stays, goes = call(
-        halve_second_kernel, (where, stays, came), [(quarter, F32), (quarter, BF16)], [],
-        "halve_again_" + name, 0.7,
-    )
-    came = across(goes, 3, "dp")
-    yield goes
-    (own,) = call(sum_kernel, (stays, came), [(quarter, BF16)], [], "sum_" + name, 0.6)
-    came = across(own, 3, "dp")
-    (own,) = call(pair_kernel, (where, own, came), [(half, BF16)], [], "pair_" + name, 0.6)
-    came = across(own, 1, "dp")
-    yield call(whole_kernel, (where, own, came), [((rows, width), F32)], [], "whole_" + name, 1.0)[0]
+        halve_kernel, (where, keep, came), [(half, F32), (half, BF16)], [], "halve_" + name, 0.8
+    )
+    (own,) = call(
+        sum_kernel, (stays, across(goes, 1, "dp")), [(half, BF16)], [], "sum_near_" + name, 0.7
+    )
+    (own,) = call(
+        sum_kernel, (own, across(own, 3, "dp")), [(half, BF16)], [], "sum_far_" + name, 0.7
+    )
+    return join(where, own, across(own, 1, "dp"))
 
 
 def finish(where, own, far, with_rms, name):
@@ -697,7 +647,8 @@
     wide = (tokens, width)
     state_shape = (pairs, LANES, PAIR)
     dma = pltpu.SemaphoreType.DMA
-    mask_mem = pltpu.VMEM((chunks, CHUNK, PAIR), F32)
+    mask_shape = ((chunks, CHUNK, PAIR), BF16)
+    mask_mem = pltpu.VMEM(*mask_shape)
     row_mem = pltpu.VMEM(wide, BF16)
 
     own_g = lax.dynamic_slice(cotangent, (place * tokens, 0), (tokens, width))
@@ -725,7 +676,7 @@
     (active,) = call(
         up_kernel, (normed_two, *up_w), [((tokens, units), BF16)], [], "up_first", 3.2
     )
-    down_w = spread(down_weight[0], after(far_down, normed_two))
+    down_w = spread(down_weight[0], after(far_down, active))
     (y,) = call(down_kernel, (mid, active, *down_w), [(wide, BF16)], [], "down_first", 2.8)
     came = across(y, 1, "section")
 
@@ -734,14 +685,14 @@
         features + [(wide, BF16)] * 2, [], "qkv_second", 3.5,
     )
     start = across(state, 1)
-    y, mid, o, o_send, inv_den, states, active, active_send, slope, normed_two = call(
+    y, mid, o, o_send, inv_den, states, active, active_send, slope, normed_two, *masks = call(
         block_kernel, (fq, fk, vv, start, cols, seg, x, gain, bias, out_w, *up_w, *down_w),
         [
             (wide, BF16), (wide, F32), (wide, BF16), ((tokens, width // 2), BF16), (wide, F32),
             ((pairs, chunks, LANES, PAIR), BF16), (half, BF16), (half, BF16),
-            ((tokens, units), BF16), (wide, BF16),
+            ((tokens, units), BF16), (wide, BF16), mask_shape, mask_shape,
         ],
-        [mask_mem], "block_second", 10.0,
+        [], "block_second", 10.0,
     )
     far_y = across(y, 2)
     active_two = across(active_send, 1)
@@ -749,81 +700,80 @@
     normed_two_other = across(normed_two, 1)
     o_other = across(o_send, 1)
 
-    def ffn_back(grads, name):
-        second = len(grads) > 1
-        extra = [(half, BF16)] * 2 + [(wide, BF16), ((2, width), F32)] if second else []
-        return call(
-            functools.partial(ffn_back_kernel, second),
-            (where, *grads, slope, mid, o, inv_den, fq, cols, gain, out_w, *up_w, *down_w),
-            [(wide, F32), (wide, BF16), (wide, BF16), (state_shape, BF16)] + extra,
-            [grad_mem] if second else [row_mem], name, 7.5,
-        )
-
     def attention_back(sums, grad_mid, dnum, dden, end, name):
         third = ((3, tokens, width // 2), BF16)
         extra = [third, third, ((8, width), F32)] if sums else []
         return call(
             functools.partial(attention_back_kernel, bool(sums)),
-            (fq, fk, vv, dnum, dden, states, end, cols, seg, x, grad_mid, gain, qkv, *sums),
+            (fq, fk, vv, dnum, dden, states, end, cols, *masks, x, grad_mid, gain, qkv, *sums),
             [(wide, BF16)] + extra,
-            [mask_mem, mask_mem, grad_mem, pltpu.VMEM((3, *wide), BF16)], name, 7.5,
+            [grad_mem, pltpu.VMEM((3, *wide), BF16)], name, (LOW if sums else 1.0) * 7.5,
         )
 
-    grad_mid, dnum, dden, moved = ffn_back((own_g,), "ffn_back_first")
+    back_shapes = [(wide, F32), (wide, BF16), (wide, BF16), (state_shape, BF16)]
+    back_operands = (slope, mid, o, inv_den, fq, cols, gain, out_w, *up_w, *down_w)
+    grad_mid, dnum, dden, moved = call(
+        functools.partial(ffn_back_kernel, False), (where, own_g, *back_operands),
+        back_shapes, [row_mem], "ffn_back_first", 4.2,
+    )
     (grad_x,) = attention_back((), grad_mid, dnum, dden, across(moved, 1), "attention_back_first")
     came = across(grad_x, 1, "section")
-    activations, token_rms = finish(
-        where, after(y, grad_x), after(far_y, grad_x), True, "activations"
-    )
-    came = after(came, activations)
+    came = after(came, far_y)
 
     share = (width, units // 4)
     keep, send = call(
         down_grad_kernel, (where, own_g, other_g, came, across(came, 1), active, active_two),
-        [(share, BF16)] * 2, [turned_mem], "down_grad", 2.2,
+        [(share, BF16)] * 2, [turned_mem], "down_grad", LOW * 2.2,
     )
     down_keep, down_far = keep, across(send, 2)
-    grad_mid, dnum, dden, moved, dup, dup_send, dattn, sums_two = ffn_back(
-        (own_g, after(came, send)), "ffn_back_second"
-    )
+    grad_mid, dnum, dden, moved, dattn, dup, dup_send, sums_two = call(
+        functools.partial(ffn_back_kernel, True),
+        (where, own_g, after(came, send), *back_operands),
+        back_shapes + [(wide, BF16), (half, BF16), (half, BF16), ((2, width), F32)],
+        [grad_mem], "ffn_back_second", LOW * 5.0,
+    )
+    dup_other = across(dup_send, 1)
     end = across(moved, 1)
     dattn_other = across(dattn, 1)
+    grad_x, dproj, dproj_send, sums = attention_back(
+        (sums_two,), grad_mid, dnum, dden, end, "attention_back_second"
+    )
+    dproj_other = across(dproj_send, 1)
     keep, send = call(
-        up_grad_kernel, (normed_two, normed_two_other, dup, across(dup_send, 1)),
+        up_grad_kernel,
+        (normed_two, normed_two_other, dup, after(dup_other, grad_x, down_far)),
         [(share, BF16)] * 2, [turned_mem], "up_grad", 1.3,
     )
     up_keep, up_far = keep, across(send, 2)
-    down_steps = halving_sum(down_keep, after(down_far, send), where, "down")
-    goes = next(down_steps)
-    grad_x, dproj, dproj_send, sums = attention_back(
-        (sums_two,), grad_mid, dnum, dden, after(end, goes), "attention_back_second"
-    )
-    goes = next(down_steps)
+    dproj_other = after(dproj_other, send)
     late = (4 * width + 64, LANES)
     keep, send = call(
         late_grad_kernel,
         (
-            normed, normed_other, dproj, across(dproj_send, 1), o, o_other, dattn, dattn_other,
-            after(sums, goes), across(sums, 1),
+            normed, normed_other, dproj, dproj_other, o, o_other, dattn, dattn_other,
+            sums, across(sums, 1),
         ),
         [(late, BF16)] * 2, [turned_mem], "late_grad", 1.3,
     )
-    up_steps = halving_sum(up_keep, after(up_far, grad_x), where, "up")
-    next(up_steps)
-    next(up_steps)
-
-    def late_join(where, *parts):
+    late_far = across(send, 2)
+    def join_plain(*parts):
+        if len(parts) == 1:
+            return parts[0].astype(F32)
+        return call(whole_kernel, parts, [(share, F32)], [], "whole", 1.5)[0]
+
+    def join_late(*parts):
         results = [
             ((3, width, LANES), F32), ((LANES, width), F32), ((2, width), F32), ((2, width), F32)
         ]
-        if len(parts) == 1:
-            kernel, operands = unpack_late_kernel, parts
-        else:
-            kernel, operands = join_late_kernel, (where, *parts)
-        return call(kernel, operands, results, [pltpu.VMEM(late, F32)], "join_late", 1.5)
-
-    qkv_total, out_total, gain_total, bias_total = sum_rows(keep, send, where, late_join, "_late")
-    down_total, up_total = next(down_steps), next(up_steps)
+        kernel = unpack_late_kernel if len(parts) == 1 else join_late_kernel
+        return call(kernel, parts, results, [pltpu.VMEM(late, F32)], "join_late", 1.5)
+
+    down_total = sum_over_dp(down_keep, after(down_far, send), where, "down", join_plain)
+    up_total = sum_over_dp(up_keep, up_far, where, "up", join_plain)
+    qkv_total, out_total, gain_total, bias_total = sum_over_dp(
+        keep, late_far, where, "late", join_late
+    )
+    activations, token_rms = finish(where, after(y, up_total), after(far_y, up_total), True, "activations")
     own = after(grad_x, send)
     (input_grad,) = finish(where, own, across(own, 2), False, "input_grad")
     return (

time: 226 us -> 195 us (0.86); the launches traced: 225 us -> 192 us
  Pallas kernels: 78.1 us -> 60.4 us
  starting transfers between devices: 50.4 us -> 42 us
  waiting for transfers between devices: 85.8 us -> 79.5 us
    pallas_call x28 -> x27, Pallas kernels: 78.1 us -> 60.4 us  [call(): pl.pallas_call(kernel, out_shape=near, in_specs=[IN_SMEM if v.dtype == jn...]
    ppermute x50 -> x45, starting transfers between devices: 50.4 us -> 42 us  [across(): return lax.ppermute(block, axis, [(i, i ^ distance) for i in range(size)])]
    ppermute x50 -> x45, waiting for transfers between devices: 85.8 us -> 79.5 us  [across(): return lax.ppermute(block, axis, [(i, i ^ distance) for i in range(size)])]
  transfers between devices with their start and end apart: 50 -> 45, of which waited for: 20 -> 21; matrix products, arithmetic and copies ran while one was open for 3% -> 4% of each run, Pallas kernels for 17% -> 17%
where the time goes in v3:
time: 195 us; the launch traced here: 192 us
  waiting for transfers between devices  79.5 us (41%)
  Pallas kernels  60.4 us (31%)
  starting transfers between devices  42 us (22%)
  local copies, waits for them, and re-layouts  4.73 us (2%)
  other arithmetic  3.13 us (2%)
    ppermute x45, waiting for transfers between devices, across(): return lax.ppermute(block, axis, [(i, i ^ distance) for i in range(size)])  79.5 us
    pallas_call x27, Pallas kernels, call(): pl.pallas_call(kernel, out_shape=near, in_specs=[IN_SMEM if v.dtype == jn...  60.4 us
    ppermute x45, starting transfers between devices, across(): return lax.ppermute(block, axis, [(i, i ^ distance) for i in range(size)])  42 us
  transfers between devices with their start and end apart: 45, of which 21 were waited for; matrix products, arithmetic and copies ran while one was open for 4% of the time, Pallas kernels for 17%

profile of v3, /device:TPU:0, one launch (start us, length us, event | category | flops | bytes accessed | tf_op | source)
XLA Modules:
  0.0 191.6 jit_solution(2759194619154641268)
XLA Ops:
  0.7 3.0 %collective-permute-start.1 = (bf16[3,512,128]{2,1,0:T(8,128)(2,1)}, bf16[3,512,128]{2,1,0:T(8,128)(2,1)}, u32[]{:S(2)}, u32[]{:S(2)}) collective-permute-start(bf16[3,512,128]{2,1,0:T(8,128)(2,1)} %bitcast.61), channel_id=1, source_target_pairs={{0,2},{1,3},{2,0},{3,1},{4,6},{5,7},{6,4},{7,5},{8,10},{9,11},{10,... | collective-permute-start | bytes 1179656 | tf_op jit(solution)/shard_map/ppermute | solution.py:562
  3.8 1.9 collective-permute-start.8
  5.7 1.2 reduce-window.6
  7.4 0.6 dynamic_slice.23
  8.0 0.8 dynamic-slice_bitcast_fusion
  9.7 0.6 slice.23
  10.4 0.7 fusion.1
  11.4 2.6 %collective-permute-done.1.rest_5_ = bf16[3,512,128]{2,1,0:T(8,128)(2,1)} collective-permute-done((bf16[3,512,128]{2,1,0:T(8,128)(2,1)}, bf16[3,512,128]{2,1,0:T(8,128)(2,1)}, u32[]{:S(2)}, u32[]{:S(2)}) %collective-permute-start.1) | collective-permute-done | bytes 393248 | tf_op jit(solution)/shard_map/ppermute | solution.py:562
  14.0 1.7 constant_dynamic-slice_fusion
  16.0 1.0 copy-done.5
  17.0 3.3 %qkv_first.1 = (bf16[512,512]{1,0:T(8,128)(2,1)S(1)}, bf16[512,512]{1,0:T(8,128)(2,1)S(1)}, bf16[512,512]{1,0:T(8,128)(2,1)S(1)}, bf16[4,128,256]{2,1,0:T(8,128)(2,1)S(1)}, bf16[3,512,512]{2,1,0:T(8,128)(2,1)S(1)}) custom-call(s32[3]{0:T(128)S(1)} %pad_add_fusion.where, bf16[512,512]{1,0:T(8,128)(2,1)S(1)} %constant_dynamic-slice_fusion.2.own.x, ...), custom_call_target="tpu_custom_call" | custom-call | flops 4400000000 | tf_op jit(solution)/shard_map/qkv_first/pallas_call | solution.py:545
  21.4 5.6 %collective-permute-done.8.w2.u2.rest_10_.rest_11_ = bf16[512,512]{1,0:T(8,128)(2,1)S(1)} collective-permute-done((bf16[512,512]{1,0:T(8,128)(2,1)}, bf16[512,512]{1,0:T(8,128)(2,1)S(1)}, u32[]{:S(2)}, u32[]{:S(2)}) %collective-permute-start.8) | collective-permute-done | bytes 524320 | tf_op jit(solution)/shard_map/ppermute | solution.py:562
  27.0 1.7 collective-permute-start.11
  29.3 4.2 %attention_first.1 = (f32[512,512]{1,0:T(8,128)S(1)}, bf16[512,512]{1,0:T(8,128)(2,1)S(1)}, bf16[512,512]{1,0:T(8,128)(2,1)S(1)}) custom-call(bf16[512,512]{1,0:T(8,128)(2,1)S(1)} %get-tuple-element.82.fq, bf16[512,512]{1,0:T(8,128)(2,1)S(1)} %get-tuple-element.83.fk, bf16[512,512]{1,0:T(8,128)(2,1)S(1)} %get-tuple-element.84.vv, ...), custom_call_target="tpu_custom_call" | custom-call | flops 6049999872 | tf_op jit(solution)/shard_map/attention_first/pallas_call | solution.py:545
  33.5 1.6 up_first.1.active
  35.1 5.1 %collective-permute-done.11.w2.d2.rest_14_.rest_15_ = bf16[512,512]{1,0:T(8,128)(2,1)S(1)} collective-permute-done((bf16[512,512]{1,0:T(8,128)(2,1)S(1)}, bf16[512,512]{1,0:T(8,128)(2,1)S(1)}, u32[]{:S(2)}, u32[]{:S(2)}) %collective-permute-start.11) | collective-permute-done | bytes 524320 | tf_op jit(solution)/shard_map/ppermute | solution.py:562
  40.2 1.9 collective-permute-done.12.w3.d3.rest_15_.rest_16_
  42.1 1.3 down_first.1
  43.4 1.5 collective-permute-start.13
  44.9 12.5 %collective-permute-done.13.rest_0_ = bf16[512,512]{1,0:T(8,128)(2,1)S(1)} collective-permute-done((bf16[512,512]{1,0:T(8,128)(2,1)S(1)}, bf16[512,512]{1,0:T(8,128)(2,1)S(1)}, u32[]{:S(2)}, u32[]{:S(2)}) %collective-permute-start.13) | collective-permute-done | bytes 524320 | tf_op jit(solution)/shard_map/ppermute | solution.py:562
  57.4 2.3 %qkv_second.1 = (bf16[512,512]{1,0:T(8,128)(2,1)S(1)}, bf16[512,512]{1,0:T(8,128)(2,1)S(1)}, bf16[512,512]{1,0:T(8,128)(2,1)S(1)}, bf16[4,128,256]{2,1,0:T(8,128...) custom-call(s32[3]{0:T(128)S(1)} %pad_add_fusion.where, ...), custom_call_target="tpu_custom_call" | custom-call | flops 3849999872 | tf_op jit(solution)/shard_map/qkv_second/pallas_call | solution.py:545
  59.8 1.5 collective-permute-done.14.start
  61.3 8.2 %block_second.1 = (bf16[512,512]{1,0:T(8,128)(2,1)S(1)}, f32[512,512]{1,0:T(8,128)S(1)}, bf16[512,512]{1,0:T(8,128)(2,1)S(1)}, bf16[512,256]{1,0:T(8,128)(2,1)S(...) custom-call(bf16[512,512]{1,0:T(8,128)(2,1)S(1)} %get-tuple-element., ...), custom_call_target="tpu_custom_call" | custom-call | flops 11000000512 | tf_op jit(solution)/shard_map/block_second/pallas_call | solution.py:545
  69.5 4.7 %ffn_back_first.1 = (f32[512,512]{1,0:T(8,128)S(1)}, bf16[512,512]{1,0:T(8,128)(2,1)S(1)}, bf16[512,512]{1,0:T(8,128)(2,1)S(1)}, bf16[4,128,256]{2,1,0:T(8,128)(2,1)S(1)}) custom-call(s32[3]{0:T(128)S(1)} %pad_add_fusion.where, f32[512,512]{1,0:T(8,128)S(1)} %get-tuple-element.154.own_g, bf16[512,2048]{1,0:T(8,128)(2,1)S(1)} %get-tuple-element.100.rest_0_.rest_1_, ...), custom_call_target="tpu_custom_call" | custom-call | flops 4620000256 | tf_op jit(solution)/shard_map/ffn_back_first/pallas_call | solution.py:545
  74.4 1.4 collective-permute-start.18
  75.9 5.6 %attention_back_first.1 = bf16[512,512]{1,0:T(8,128)(2,1)S(1)} custom-call(bf16[512,512]{1,0:T(8,128)(2,1)S(1)} %get-tuple-element.92.fq.rest_4_.rest_5_, bf16[512,512]{1,0:T(8,128)(2,1)S(1)} %get-tuple-element.93.fk, bf16[512,512]{1,0:T(8,128)(2,1)S(1)} %get-tuple-element.94.vv, bf16[512,512]{1,0:T(8,128)(2,1)S(1)} %get-tuple-element.104.dnum, ...), custom_call_target="tpu_custom_call" | custom-call | flops 8249999872 | tf_op jit(solution)/shard_map/attention_back_first/pallas_call | solution.py:545
  81.5 1.6 collective-permute-start.17
  83.0 5.6 %collective-permute-done.18.p2 = bf16[512,512]{1,0:T(8,128)(2,1)S(1)} collective-permute-done((bf16[512,512]{1,0:T(8,128)(2,1)S(1)}, bf16[512,512]{1,0:T(8,128)(2,1)S(1)}, u32[]{:S(2)}, u32[]{:S(2)}) %collective-permute-start.18) | collective-permute-done | bytes 524320 | tf_op jit(solution)/shard_map/ppermute | solution.py:562
  88.6 6.8 %collective-permute-done.17.came.rest_0_ = bf16[512,512]{1,0:T(8,128)(2,1)S(1)} collective-permute-done((bf16[512,512]{1,0:T(8,128)(2,1)S(1)}, bf16[512,512]{1,0:T(8,128)(2,1)S(1)}, u32[]{:S(2)}, u32[]{:S(2)}) %collective-permute-start.17) | collective-permute-done | bytes 524320 | tf_op jit(solution)/shard_map/ppermute | solution.py:562
  95.4 1.9 collective-permute-done.19.came_two
  97.4 1.9 down_grad.1
  99.2 5.0 %ffn_back_second.1 = (f32[512,512]{1,0:T(8,128)S(1)}, bf16[512,512]{1,0:T(8,128)(2,1)S(1)}, bf16[512,512]{1,0:T(8,128)(2,1)S(1)}, bf16[4,128,256]{2,1,0:T(8,128)...) custom-call(s32[3]{0:T(128)S(1)} %pad_add_fusion.where, ...), custom_call_target="tpu_custom_call" | custom-call | flops 110000000 | tf_op jit(solution)/shard_map/ffn_back_second/pallas_call | solution.py:545
  104.9 1.4 collective-permute-start.23
  106.3 1.1 collective-permute-done.22.end
  107.4 6.0 %attention_back_second.1 = (bf16[512,512]{1,0:T(8,128)(2,1)S(1)}, bf16[3,512,256]{2,1,0:T(8,128)(2,1)S(1)}, bf16[3,512,256]{2,1,0:T(8,128)(2,1)S(1)}, f32[8,512]{1,0:T(8,128)S(1)}) custom-call(bf16[512,512]{1,0:T(8,128)(2,1)S(1)} %get-tuple-element.92.fq.rest_4_.rest_5_, bf16[512,512]{1,0:T(8,128)(2,1)S(1)} %get-tuple-element.93.fk, ...), custom_call_target="tpu_custom_call" | custom-call | flops 165000000 | tf_op jit(solution)/shard_map/attention_back_second/pallas_call | solution.py:545
  114.0 4.8 %collective-permute-done.23.came = bf16[512,512]{1,0:T(8,128)(2,1)S(1)} collective-permute-done((bf16[512,512]{1,0:T(8,128)(2,1)S(1)}, bf16[512,512]{1,0:T(8,128)(2,1)S(1)}, u32[]{:S(2)}, u32[]{:S(2)}) %collective-permute-start.23) | collective-permute-done | bytes 524320 | tf_op jit(solution)/shard_map/ppermute | solution.py:562
  119.3 1.3 up_grad.1
  120.6 1.5 collective-permute-start.24
  122.1 1.2 collective-permute-done.34.sums_other
  123.3 1.3 late_grad.1
  124.6 0.7 collective-permute-start.38
  125.3 0.7 halve_down.1
  125.9 1.6 collective-permute-start.42
  127.5 7.9 %collective-permute-done.24.came = bf16[512,512]{1,0:T(8,128)(2,1)S(1)} collective-permute-done((bf16[512,512]{1,0:T(8,128)(2,1)S(1)}, bf16[512,512]{1,0:T(8,128)(2,1)S(1)}, u32[]{:S(2)}, u32[]{:S(2)}) %collective-permute-start.24) | collective-permute-done | bytes 524320 | tf_op jit(solution)/shard_map/ppermute | solution.py:562
  135.5 0.7 halve_up.1
  136.1 1.6 collective-permute-start.25
  137.8 1.4 collective-permute-start.36
  139.3 2.5 %collective-permute-start.43 = (bf16[256,512]{1,0:T(8,128)(2,1)S(1)}, bf16[256,512]{1,0:T(8,128)(2,1)S(1)}, u32[]{:S(2)}, u32[]{:S(2)}) collective-permute-start(bf16[256,512]{1,0:T(8,128)(2,1)S(1)} %sum_near_down.1.keep), channel_id=1, source_target_pairs={{0,12},{4,8},{8,4},{12,0},{1,13},{5,9},{9,5},{13,1},{2,14},{6,10},... | collective-permute-start | bytes 786440 | tf_op jit(solution)/shard_map/ppermute | solution.py:562
  141.8 2.0 %collective-permute-done.25.came = bf16[256,512]{1,0:T(8,128)(2,1)S(1)} collective-permute-done((bf16[256,512]{1,0:T(8,128)(2,1)S(1)}, bf16[256,512]{1,0:T(8,128)(2,1)S(1)}, u32[]{:S(2)}, u32[]{:S(2)}) %collective-permute-start.25) | collective-permute-done | bytes 262176 | tf_op jit(solution)/shard_map/ppermute | solution.py:562
  143.9 10.9 %collective-permute-start.26 = (bf16[256,512]{1,0:T(8,128)(2,1)S(1)}, bf16[256,512]{1,0:T(8,128)(2,1)S(1)}, u32[]{:S(2)}, u32[]{:S(2)}) collective-permute-start(bf16[256,512]{1,0:T(8,128)(2,1)S(1)} %sum_near_up.1.keep), channel_id=1, source_target_pairs={{0,12},{4,8},{8,4},{12,0},{1,13},{5,9},{9,5},{13,1},{2,14},{6,10},... | collective-permute-start | bytes 786440 | tf_op jit(solution)/shard_map/ppermute | solution.py:562
  154.8 0.7 halve_late.1
  155.7 2.2 %collective-permute-start.44 = (bf16[256,512]{1,0:T(8,128)(2,1)S(1)}, bf16[256,512]{1,0:T(8,128)(2,1)S(1)}, u32[]{:S(2)}, u32[]{:S(2)}) collective-permute-start(bf16[256,512]{1,0:T(8,128)(2,1)S(1)} %sum_far_down.1.own), channel_id=1, source_target_pairs={{0,4},{4,0},{8,12},{12,8},{1,5},{5,1},{9,13},{13,9},{2,6},{6,2},{1... | collective-permute-start | bytes 786440 | tf_op jit(solution)/shard_map/ppermute | solution.py:562
  158.3 3.6 %collective-permute-done.26.came = bf16[256,512]{1,0:T(8,128)(2,1)S(1)} collective-permute-done((bf16[256,512]{1,0:T(8,128)(2,1)S(1)}, bf16[256,512]{1,0:T(8,128)(2,1)S(1)}, u32[]{:S(2)}, u32[]{:S(2)}) %collective-permute-start.26) | collective-permute-done | bytes 262176 | tf_op jit(solution)/shard_map/ppermute | solution.py:562
  162.0 1.6 collective-permute-start.27
  163.6 2.8 %collective-permute-done.39.came = bf16[1056,128]{1,0:T(8,128)(2,1)S(1)} collective-permute-done((bf16[1056,128]{1,0:T(8,128)(2,1)S(1)}, bf16[1056,128]{1,0:T(8,128)(2,1)S(1)}, u32[]{:S(2)}, u32[]{:S(2)}) %collective-permute-start.39) | collective-permute-done | bytes 270368 | tf_op jit(solution)/shard_map/ppermute | solution.py:562
  167.0 3.1 %collective-permute-done.44.came = bf16[256,512]{1,0:T(8,128)(2,1)S(1)} collective-permute-done((bf16[256,512]{1,0:T(8,128)(2,1)S(1)}, bf16[256,512]{1,0:T(8,128)(2,1)S(1)}, u32[]{:S(2)}, u32[]{:S(2)}) %collective-permute-start.44) | collective-permute-done | bytes 262176 | tf_op jit(solution)/shard_map/ppermute | solution.py:562
  170.1 1.6 whole.3
  171.7 3.7 %collective-permute-done.27.came = bf16[256,512]{1,0:T(8,128)(2,1)S(1)} collective-permute-done((bf16[256,512]{1,0:T(8,128)(2,1)S(1)}, bf16[256,512]{1,0:T(8,128)(2,1)S(1)}, u32[]{:S(2)}, u32[]{:S(2)}) %collective-permute-start.27) | collective-permute-done | bytes 262176 | tf_op jit(solution)/shard_map/ppermute | solution.py:562
  175.4 1.6 whole.2
  177.5 1.6 collective-permute-done.40.came
  179.3 2.8 %input_grad.1 = f32[2048,512]{1,0:T(8,128)} custom-call(s32[3]{0:T(128)S(1)} %pad_add_fusion.where, bf16[512,512]{1,0:T(8,128)(2,1)S(1)} %get-tuple-element.140.p0, bf16[512,512]{1,0:T(8,128)(2,1)S(1)} %collective-permute-done.35.p1, bf16[512,512]{1,0:T(8,128)(2,1)S(1)} %collective-permute-done.36.p2, bf16[512,512]{1,0:T(8,128)(2,1)S(1)} %collective-permute-done.37.p3), custom_call_target="tpu_custom_call" | custom-call | flops 3300000000 | tf_op jit(solution)/shard_map/input_grad/pallas_call | solution.py:545
  182.1 3.9 %collective-permute-done.41.came = bf16[1056,128]{1,0:T(8,128)(2,1)S(1)} collective-permute-done((bf16[1056,128]{1,0:T(8,128)(2,1)S(1)}, bf16[1056,128]{1,0:T(8,128)(2,1)S(1)}, u32[]{:S(2)}, u32[]{:S(2)}) %collective-permute-start.41) | collective-permute-done | bytes 270368 | tf_op jit(solution)/shard_map/ppermute | solution.py:562
  186.0 1.6 join_late.1
  187.6 3.8 %activations.1 = (f32[2048,512]{1,0:T(8,128)}, f32[16,128]{1,0:T(8,128)}) custom-call(s32[3]{0:T(128)S(1)} %pad_add_fusion.where, bf16[512,512]{1,0:T(8,128)(2,1)S(1)} %get-tuple-element.129.p0, bf16[512,512]{1,0:T(8,128)(2,1)S(1)} %collective-permute-done.28.p1, bf16[512,512]{1,0:T(8,128)(2,1)S(1)} %collective-permute-done.18.p2, ...), custom_call_target="tpu_custom_call" | custom-call | flops 3300000000 | tf_op jit(solution)/shard_map/activations/pallas_call | solution.py:545
  (86 shorter events, 7.3 us)
Async XLA Ops:
  0.6 13.3 %copy-start = (bf16[2048,512]{1,0:T(8,128)(2,1)S(1)}, bf16[2048,512]{1,0:T(8,128)(2,1)}, u32[]{:S(2)}) copy-start(bf16[2048,512]{1,0:T(8,128)(2,1)} %param.10) | copy-start | bytes 6291460
  0.7 13.3 %collective-permute-start.1 = (bf16[3,512,128]{2,1,0:T(8,128)(2,1)}, bf16[3,512,128]{2,1,0:T(8,128)(2,1)}, u32[]{:S(2)}, u32[]{:S(2)}) collective-permute-start(bf16[3,512,128]{2,1,0:T(8,128)(2,1)} %bitcast.61), channel_id=1, source_target_pairs={{0,2},{1,3},{2,0},{3,1},{4,6},{5,7},{6,4},{7,5},{8,10},{9,11},{10,... | collective-permute-start | bytes 1179656 | tf_op jit(solution)/shard_map/ppermute | solution.py:562
  3.7 12.2 %collective-permute-start = (bf16[3,512,128]{2,1,0:T(8,128)(2,1)}, bf16[3,512,128]{2,1,0:T(8,128)(2,1)}, u32[]{:S(2)}, u32[]{:S(2)}) collective-permute-start(bf16[3,512,128]{2,1,0:T(8,128)(2,1)} %bitcast.62), channel_id=1, source_target_pairs={{0,1},{1,0},{2,3},{3,2},{4,5},{5,4},{6,7},{7,6},{8,9},{9,8},{10,11... | collective-permute-start | bytes 1179656 | tf_op jit(solution)/shard_map/ppermute | solution.py:562
  3.7 17.3 %collective-permute-start.5 = (bf16[128,512]{1,0:T(8,128)(2,1)}, bf16[128,512]{1,0:T(8,128)(2,1)}, u32[]{:S(2)}, u32[]{:S(2)}) collective-permute-start(bf16[128,512]{1,0:T(8,128)(2,1)} %bitcast.64), channel_id=1, source_target_pairs={{0,2},{1,3},{2,0},{3,1},{4,6},{5,7},{6,4},{7,5},{8,10},{9,11},{10,... | collective-permute-start | bytes 393224 | tf_op jit(solution)/shard_map/ppermute | solution.py:562
  3.8 23.2 %collective-permute-start.8 = (bf16[512,512]{1,0:T(8,128)(2,1)}, bf16[512,512]{1,0:T(8,128)(2,1)S(1)}, u32[]{:S(2)}, u32[]{:S(2)}) collective-permute-start(bf16[512,512]{1,0:T(8,128)(2,1)} %bitcast.41), channel_id=1, source_target_pairs={{0,2},{1,3},{2,0},{3,1},{4,6},{5,7},{6,4},{7,5},{8,10},{9,11},{10,... | collective-permute-start | bytes 1572872 | tf_op jit(solution)/shard_map/ppermute | solution.py:562
  13.9 2.1 %collective-permute-start.2 = (bf16[3,512,128]{2,1,0:T(8,128)(2,1)}, bf16[3,512,128]{2,1,0:T(8,128)(2,1)}, u32[]{:S(2)}, u32[]{:S(2)}) collective-permute-start(bf16[3,512,128]{2,1,0:T(8,128)(2,1)} %collective-permute-done.1.rest_5_), channel_id=1, source_target_pairs={{0,1},{1,0},{2,3},{3,2},{4,5},{5,4},{6,7},{7,6},{8,9},{9,8},{10,11... | collective-permute-start | bytes 1179656 | tf_op jit(solution)/shard_map/ppermute | solution.py:562
  14.0 2.0 %copy-start.4 = (f32[1,2,512]{2,1,0:T(2,128)S(1)}, f32[1,2,512]{2,1,0:T(2,128)}, u32[]{:S(2)}) copy-start(f32[1,2,512]{2,1,0:T(2,128)} %param.18) | copy-start | bytes 12292
  14.0 2.0 %copy-start.7 = (f32[1,2,512]{2,1,0:T(2,128)S(1)}, f32[1,2,512]{2,1,0:T(2,128)}, u32[]{:S(2)}) copy-start(f32[1,2,512]{2,1,0:T(2,128)} %param.19) | copy-start | bytes 12292
  16.0 1.0 copy-start.5
  17.0 3.8 %copy-start.6 = (bf16[1,128,512]{2,1,0:T(8,128)(2,1)S(1)}, bf16[1,128,512]{2,1,0:T(8,128)(2,1)}, u32[]{:S(2)}) copy-start(bf16[1,128,512]{2,1,0:T(8,128)(2,1)} %param.15) | copy-start | bytes 393220
  17.0 4.3 %copy-start.2 = (bf16[1,512,512]{2,1,0:T(8,128)(2,1)S(1)}, bf16[1,512,512]{2,1,0:T(8,128)(2,1)}, u32[]{:S(2)}) copy-start(bf16[1,512,512]{2,1,0:T(8,128)(2,1)} %param.16) | copy-start | bytes 1572868
  17.0 10.0 %copy-start.3 = (bf16[1,512,512]{2,1,0:T(8,128)(2,1)S(1)}, bf16[1,512,512]{2,1,0:T(8,128)(2,1)}, u32[]{:S(2)}) copy-start(bf16[1,512,512]{2,1,0:T(8,128)(2,1)} %param.17) | copy-start | bytes 1572868
  20.3 8.9 %collective-permute-start.3 = (bf16[4,128,256]{2,1,0:T(8,128)(2,1)S(1)}, bf16[4,128,256]{2,1,0:T(8,128)(2,1)S(1)}, u32[]{:S(2)}, u32[]{:S(2)}) collective-permute-start(bf16[4,128,256]{2,1,0:T(8,128)(2,1)S(1)} %get-tuple-element.85), channel_id=1, source_target_pairs={{0,1},{1,0},{2,3},{3,2},{4,5},{5,4},{6,7},{7,6},{8,9},{9,8},{10,11... | collective-permute-start | bytes 786440 | tf_op jit(solution)/shard_map/ppermute | solution.py:562
  20.8 8.0 %collective-permute-start.4 = (bf16[128,512]{1,0:T(8,128)(2,1)S(1)}, bf16[128,512]{1,0:T(8,128)(2,1)S(1)}, u32[]{:S(2)}, u32[]{:S(2)}) collective-permute-start(bf16[128,512]{1,0:T(8,128)(2,1)S(1)} %bitcast.65), channel_id=1, source_target_pairs={{0,1},{1,0},{2,3},{3,2},{4,5},{5,4},{6,7},{7,6},{8,9},{9,8},{10,11... | collective-permute-start | bytes 393224 | tf_op jit(solution)/shard_map/ppermute | solution.py:562
  20.9 7.9 %collective-permute-start.6 = (bf16[128,512]{1,0:T(8,128)(2,1)}, bf16[128,512]{1,0:T(8,128)(2,1)S(1)}, u32[]{:S(2)}, u32[]{:S(2)}) collective-permute-start(bf16[128,512]{1,0:T(8,128)(2,1)} %collective-permute-done.5.w2), channel_id=1, source_target_pairs={{0,1},{1,0},{2,3},{3,2},{4,5},{5,4},{6,7},{7,6},{8,9},{9,8},{10,11... | collective-permute-start | bytes 393224 | tf_op jit(solution)/shard_map/ppermute | solution.py:562
  21.3 12.2 %collective-permute-start.7 = (bf16[512,512]{1,0:T(8,128)(2,1)S(1)}, bf16[512,512]{1,0:T(8,128)(2,1)S(1)}, u32[]{:S(2)}, u32[]{:S(2)}) collective-permute-start(bf16[512,512]{1,0:T(8,128)(2,1)S(1)} %bitcast.42), channel_id=1, source_target_pairs={{0,1},{1,0},{2,3},{3,2},{4,5},{5,4},{6,7},{7,6},{8,9},{9,8},{10,11... | collective-permute-start | bytes 1572872 | tf_op jit(solution)/shard_map/ppermute | solution.py:562
  27.0 13.1 %collective-permute-start.11 = (bf16[512,512]{1,0:T(8,128)(2,1)S(1)}, bf16[512,512]{1,0:T(8,128)(2,1)S(1)}, u32[]{:S(2)}, u32[]{:S(2)}) collective-permute-start(bf16[512,512]{1,0:T(8,128)(2,1)S(1)} %bitcast.47), channel_id=1, source_target_pairs={{0,2},{1,3},{2,0},{3,1},{4,6},{5,7},{6,4},{7,5},{8,10},{9,11},{10,... | collective-permute-start | bytes 1572872 | tf_op jit(solution)/shard_map/ppermute | solution.py:562
  28.8 11.4 %collective-permute-start.10 = (bf16[512,512]{1,0:T(8,128)(2,1)S(1)}, bf16[512,512]{1,0:T(8,128)(2,1)S(1)}, u32[]{:S(2)}, u32[]{:S(2)}) collective-permute-start(bf16[512,512]{1,0:T(8,128)(2,1)S(1)} %bitcast.48), channel_id=1, source_target_pairs={{0,1},{1,0},{2,3},{3,2},{4,5},{5,4},{6,7},{7,6},{8,9},{9,8},{10,11... | collective-permute-start | bytes 1572872 | tf_op jit(solution)/shard_map/ppermute | solution.py:562
  28.8 4.7 %collective-permute-start.9 = (bf16[512,512]{1,0:T(8,128)(2,1)S(1)}, bf16[512,512]{1,0:T(8,128)(2,1)S(1)}, u32[]{:S(2)}, u32[]{:S(2)}) collective-permute-start(bf16[512,512]{1,0:T(8,128)(2,1)S(1)} %collective-permute-done.8.w2.u2.rest_10_.rest_11_), channel_id=1, source_target_pairs={{0,1},{1,0},{2,3},{3,2},{4,5},{5,4},{6,7},{7,6},{8,9},{9,8},{10,11... | collective-permute-start | bytes 1572872 | tf_op jit(solution)/shard_map/ppermute | solution.py:562
  40.1 1.9 collective-permute-start.12
  43.4 14.0 %collective-permute-start.13 = (bf16[512,512]{1,0:T(8,128)(2,1)S(1)}, bf16[512,512]{1,0:T(8,128)(2,1)S(1)}, u32[]{:S(2)}, u32[]{:S(2)}) collective-permute-start(bf16[512,512]{1,0:T(8,128)(2,1)S(1)} %down_first.1), channel_id=1, source_target_pairs={{0,16},{16,0},{1,17},{17,1},{2,18},{18,2},{3,19},{19,3},{4,20},{20... | collective-permute-start | bytes 1572872 | tf_op jit(solution)/shard_map/ppermute | solution.py:562
  59.7 1.6 collective-permute-start.14
  74.2 1.6 collective-permute-start.16
  74.4 14.2 %collective-permute-start.18 = (bf16[512,512]{1,0:T(8,128)(2,1)S(1)}, bf16[512,512]{1,0:T(8,128)(2,1)S(1)}, u32[]{:S(2)}, u32[]{:S(2)}) collective-permute-start(bf16[512,512]{1,0:T(8,128)(2,1)S(1)} %get-tuple-element.129.p0), channel_id=1, source_target_pairs={{0,2},{1,3},{2,0},{3,1},{4,6},{5,7},{6,4},{7,5},{8,10},{9,11},{10,... | collective-permute-start | bytes 1572872 | tf_op jit(solution)/shard_map/ppermute | solution.py:562
  81.5 14.0 %collective-permute-start.17 = (bf16[512,512]{1,0:T(8,128)(2,1)S(1)}, bf16[512,512]{1,0:T(8,128)(2,1)S(1)}, u32[]{:S(2)}, u32[]{:S(2)}) collective-permute-start(bf16[512,512]{1,0:T(8,128)(2,1)S(1)} %attention_back_first.1), channel_id=1, source_target_pairs={{0,16},{16,0},{1,17},{17,1},{2,18},{18,2},{3,19},{19,3},{4,20},{20... | collective-permute-start | bytes 1572872 | tf_op jit(solution)/shard_map/ppermute | solution.py:562
  83.0 12.4 %collective-permute-start.20 = (bf16[512,1024]{1,0:T(8,128)(2,1)S(1)}, bf16[512,1024]{1,0:T(8,128)(2,1)S(1)}, u32[]{:S(2)}, u32[]{:S(2)}) collective-permute-start(bf16[512,1024]{1,0:T(8,128)(2,1)S(1)} %get-tuple-element.113), channel_id=1, source_target_pairs={{0,1},{1,0},{2,3},{3,2},{4,5},{5,4},{6,7},{7,6},{8,9},{9,8},{10,11... | collective-permute-start | bytes 3145736 | tf_op jit(solution)/shard_map/ppermute | solution.py:562
  95.4 1.9 collective-permute-start.19
  104.3 14.5 %collective-permute-start.21 = (bf16[512,1024]{1,0:T(8,128)(2,1)S(1)}, bf16[512,1024]{1,0:T(8,128)(2,1)S(1)}, u32[]{:S(2)}, u32[]{:S(2)}) collective-permute-start(bf16[512,1024]{1,0:T(8,128)(2,1)S(1)} %get-tuple-element.117), channel_id=1, source_target_pairs={{0,1},{1,0},{2,3},{3,2},{4,5},{5,4},{6,7},{7,6},{8,9},{9,8},{10,11... | collective-permute-start | bytes 3145736 | tf_op jit(solution)/shard_map/ppermute | solution.py:562
  104.5 2.9 %collective-permute-start.22 = (bf16[4,128,256]{2,1,0:T(8,128)(2,1)S(1)}, bf16[4,128,256]{2,1,0:T(8,128)(2,1)S(1)}, u32[]{:S(2)}, u32[]{:S(2)}) collective-permute-start(bf16[4,128,256]{2,1,0:T(8,128)(2,1)S(1)} %get-tuple-element.120), channel_id=1, source_target_pairs={{0,1},{1,0},{2,3},{3,2},{4,5},{5,4},{6,7},{7,6},{8,9},{9,8},{10,11... | collective-permute-start | bytes 786440 | tf_op jit(solution)/shard_map/ppermute | solution.py:562
  104.9 14.0 %collective-permute-start.23 = (bf16[512,512]{1,0:T(8,128)(2,1)S(1)}, bf16[512,512]{1,0:T(8,128)(2,1)S(1)}, u32[]{:S(2)}, u32[]{:S(2)}) collective-permute-start(bf16[512,512]{1,0:T(8,128)(2,1)S(1)} %get-tuple-element.114), channel_id=1, source_target_pairs={{0,2},{1,3},{2,0},{3,1},{4,6},{5,7},{6,4},{7,5},{8,10},{9,11},{10,... | collective-permute-start | bytes 1572872 | tf_op jit(solution)/shard_map/ppermute | solution.py:562
  106.3 13.1 %collective-permute-start.15 = (bf16[512,512]{1,0:T(8,128)(2,1)S(1)}, bf16[512,512]{1,0:T(8,128)(2,1)S(1)}, u32[]{:S(2)}, u32[]{:S(2)}) collective-permute-start(bf16[512,512]{1,0:T(8,128)(2,1)S(1)} %get-tuple-element.99.normed_own), channel_id=1, source_target_pairs={{0,1},{1,0},{2,3},{3,2},{4,5},{5,4},{6,7},{7,6},{8,9},{9,8},{10,11... | collective-permute-start | bytes 1572872 | tf_op jit(solution)/shard_map/ppermute | solution.py:562
  113.4 8.7 %collective-permute-start.31 = (bf16[3,512,256]{2,1,0:T(8,128)(2,1)S(1)}, bf16[3,512,256]{2,1,0:T(8,128)(2,1)S(1)}, u32[]{:S(2)}, u32[]{:S(2)}) collective-permute-start(bf16[3,512,256]{2,1,0:T(8,128)(2,1)S(1)} %get-tuple-element.134), channel_id=1, source_target_pairs={{0,1},{1,0},{2,3},{3,2},{4,5},{5,4},{6,7},{7,6},{8,9},{9,8},{10,11... | collective-permute-start | bytes 2359304 | tf_op jit(solution)/shard_map/ppermute | solution.py:562
  113.6 8.5 %collective-permute-start.30 = (bf16[512,512]{1,0:T(8,128)(2,1)S(1)}, bf16[512,512]{1,0:T(8,128)(2,1)S(1)}, u32[]{:S(2)}, u32[]{:S(2)}) collective-permute-start(bf16[512,512]{1,0:T(8,128)(2,1)S(1)} %get-tuple-element.132.normed_own), channel_id=1, source_target_pairs={{0,1},{1,0},{2,3},{3,2},{4,5},{5,4},{6,7},{7,6},{8,9},{9,8},{10,11... | collective-permute-start | bytes 1572872 | tf_op jit(solution)/shard_map/ppermute | solution.py:562
  118.8 4.5 %collective-permute-start.33 = (bf16[512,512]{1,0:T(8,128)(2,1)S(1)}, bf16[512,512]{1,0:T(8,128)(2,1)S(1)}, u32[]{:S(2)}, u32[]{:S(2)}) collective-permute-start(bf16[512,512]{1,0:T(8,128)(2,1)S(1)} %get-tuple-element.137.dattn_own), channel_id=1, source_target_pairs={{0,1},{1,0},{2,3},{3,2},{4,5},{5,4},{6,7},{7,6},{8,9},{9,8},{10,11... | collective-permute-start | bytes 1572872 | tf_op jit(solution)/shard_map/ppermute | solution.py:562
  118.8 3.3 %collective-permute-start.32 = (bf16[512,256]{1,0:T(8,128)(2,1)S(1)}, bf16[512,256]{1,0:T(8,128)(2,1)S(1)}, u32[]{:S(2)}, u32[]{:S(2)}) collective-permute-start(bf16[512,256]{1,0:T(8,128)(2,1)S(1)} %get-tuple-element.136), channel_id=1, source_target_pairs={{0,1},{1,0},{2,3},{3,2},{4,5},{5,4},{6,7},{7,6},{8,9},{9,8},{10,11... | collective-permute-start | bytes 786440 | tf_op jit(solution)/shard_map/ppermute | solution.py:562
  120.6 14.9 %collective-permute-start.24 = (bf16[512,512]{1,0:T(8,128)(2,1)S(1)}, bf16[512,512]{1,0:T(8,128)(2,1)S(1)}, u32[]{:S(2)}, u32[]{:S(2)}) collective-permute-start(bf16[512,512]{1,0:T(8,128)(2,1)S(1)} %get-tuple-element.126), channel_id=1, source_target_pairs={{0,2},{1,3},{2,0},{3,1},{4,6},{5,7},{6,4},{7,5},{8,10},{9,11},{10,... | collective-permute-start | bytes 1572872 | tf_op jit(solution)/shard_map/ppermute | solution.py:562
  122.1 1.2 collective-permute-start.34
  124.6 30.2 %collective-permute-start.38 = (bf16[2112,128]{1,0:T(8,128)(2,1)S(1)}, bf16[2112,128]{1,0:T(8,128)(2,1)S(1)}, u32[]{:S(2)}, u32[]{:S(2)}) collective-permute-start(bf16[2112,128]{1,0:T(8,128)(2,1)S(1)} %get-tuple-element.139), channel_id=1, source_target_pairs={{0,2},{1,3},{2,0},{3,1},{4,6},{5,7},{6,4},{7,5},{8,10},{9,11},{10,... | collective-permute-start | bytes 1622024 | tf_op jit(solution)/shard_map/ppermute | solution.py:562
  125.9 13.3 %collective-permute-start.42 = (bf16[256,512]{1,0:T(8,128)(2,1)S(1)}, bf16[256,512]{1,0:T(8,128)(2,1)S(1)}, u32[]{:S(2)}, u32[]{:S(2)}) collective-permute-start(bf16[256,512]{1,0:T(8,128)(2,1)S(1)} %get-tuple-element.150), channel_id=1, source_target_pairs={{0,4},{4,0},{8,12},{12,8},{1,5},{5,1},{9,13},{13,9},{2,6},{6,2},{1... | collective-permute-start | bytes 786440 | tf_op jit(solution)/shard_map/ppermute | solution.py:562
  136.1 7.7 %collective-permute-start.25 = (bf16[256,512]{1,0:T(8,128)(2,1)S(1)}, bf16[256,512]{1,0:T(8,128)(2,1)S(1)}, u32[]{:S(2)}, u32[]{:S(2)}) collective-permute-start(bf16[256,512]{1,0:T(8,128)(2,1)S(1)} %get-tuple-element.128), channel_id=1, source_target_pairs={{0,4},{4,0},{8,12},{12,8},{1,5},{5,1},{9,13},{13,9},{2,6},{6,2},{1... | collective-permute-start | bytes 786440 | tf_op jit(solution)/shard_map/ppermute | solution.py:562
  137.8 20.1 %collective-permute-start.36 = (bf16[512,512]{1,0:T(8,128)(2,1)S(1)}, bf16[512,512]{1,0:T(8,128)(2,1)S(1)}, u32[]{:S(2)}, u32[]{:S(2)}) collective-permute-start(bf16[512,512]{1,0:T(8,128)(2,1)S(1)} %get-tuple-element.140.p0), channel_id=1, source_target_pairs={{0,2},{1,3},{2,0},{3,1},{4,6},{5,7},{6,4},{7,5},{8,10},{9,11},{10,... | collective-permute-start | bytes 1572872 | tf_op jit(solution)/shard_map/ppermute | solution.py:562
  139.3 16.3 %collective-permute-start.43 = (bf16[256,512]{1,0:T(8,128)(2,1)S(1)}, bf16[256,512]{1,0:T(8,128)(2,1)S(1)}, u32[]{:S(2)}, u32[]{:S(2)}) collective-permute-start(bf16[256,512]{1,0:T(8,128)(2,1)S(1)} %sum_near_down.1.keep), channel_id=1, source_target_pairs={{0,12},{4,8},{8,4},{12,0},{1,13},{5,9},{9,5},{13,1},{2,14},{6,10},... | collective-permute-start | bytes 786440 | tf_op jit(solution)/shard_map/ppermute | solution.py:562
  143.9 18.0 %collective-permute-start.26 = (bf16[256,512]{1,0:T(8,128)(2,1)S(1)}, bf16[256,512]{1,0:T(8,128)(2,1)S(1)}, u32[]{:S(2)}, u32[]{:S(2)}) collective-permute-start(bf16[256,512]{1,0:T(8,128)(2,1)S(1)} %sum_near_up.1.keep), channel_id=1, source_target_pairs={{0,12},{4,8},{8,4},{12,0},{1,13},{5,9},{9,5},{13,1},{2,14},{6,10},... | collective-permute-start | bytes 786440 | tf_op jit(solution)/shard_map/ppermute | solution.py:562
  155.5 10.9 %collective-permute-start.39 = (bf16[1056,128]{1,0:T(8,128)(2,1)S(1)}, bf16[1056,128]{1,0:T(8,128)(2,1)S(1)}, u32[]{:S(2)}, u32[]{:S(2)}) collective-permute-start(bf16[1056,128]{1,0:T(8,128)(2,1)S(1)} %get-tuple-element.144), channel_id=1, source_target_pairs={{0,4},{4,0},{8,12},{12,8},{1,5},{5,1},{9,13},{13,9},{2,6},{6,2},{1... | collective-permute-start | bytes 811016 | tf_op jit(solution)/shard_map/ppermute | solution.py:562
  155.7 14.5 %collective-permute-start.44 = (bf16[256,512]{1,0:T(8,128)(2,1)S(1)}, bf16[256,512]{1,0:T(8,128)(2,1)S(1)}, u32[]{:S(2)}, u32[]{:S(2)}) collective-permute-start(bf16[256,512]{1,0:T(8,128)(2,1)S(1)} %sum_far_down.1.own), channel_id=1, source_target_pairs={{0,4},{4,0},{8,12},{12,8},{1,5},{5,1},{9,13},{13,9},{2,6},{6,2},{1... | collective-permute-start | bytes 786440 | tf_op jit(solution)/shard_map/ppermute | solution.py:562
  157.8 21.4 %collective-permute-start.35 = (bf16[512,512]{1,0:T(8,128)(2,1)S(1)}, bf16[512,512]{1,0:T(8,128)(2,1)S(1)}, u32[]{:S(2)}, u32[]{:S(2)}) collective-permute-start(bf16[512,512]{1,0:T(8,128)(2,1)S(1)} %get-tuple-element.140.p0), channel_id=1, source_target_pairs={{0,1},{1,0},{2,3},{3,2},{4,5},{5,4},{6,7},{7,6},{8,9},{9,8},{10,11... | collective-permute-start | bytes 1572872 | tf_op jit(solution)/shard_map/ppermute | solution.py:562
  157.8 21.4 %collective-permute-start.37 = (bf16[512,512]{1,0:T(8,128)(2,1)S(1)}, bf16[512,512]{1,0:T(8,128)(2,1)S(1)}, u32[]{:S(2)}, u32[]{:S(2)}) collective-permute-start(bf16[512,512]{1,0:T(8,128)(2,1)S(1)} %collective-permute-done.36.p2), channel_id=1, source_target_pairs={{0,1},{1,0},{2,3},{3,2},{4,5},{5,4},{6,7},{7,6},{8,9},{9,8},{10,11... | collective-permute-start | bytes 1572872 | tf_op jit(solution)/shard_map/ppermute | solution.py:562
  162.0 13.4 %collective-permute-start.27 = (bf16[256,512]{1,0:T(8,128)(2,1)S(1)}, bf16[256,512]{1,0:T(8,128)(2,1)S(1)}, u32[]{:S(2)}, u32[]{:S(2)}) collective-permute-start(bf16[256,512]{1,0:T(8,128)(2,1)S(1)} %sum_far_up.1.own), channel_id=1, source_target_pairs={{0,4},{4,0},{8,12},{12,8},{1,5},{5,1},{9,13},{13,9},{2,6},{6,2},{1... | collective-permute-start | bytes 786440 | tf_op jit(solution)/shard_map/ppermute | solution.py:562
  166.5 12.6 %collective-permute-start.40 = (bf16[1056,128]{1,0:T(8,128)(2,1)S(1)}, bf16[1056,128]{1,0:T(8,128)(2,1)S(1)}, u32[]{:S(2)}, u32[]{:S(2)}) collective-permute-start(bf16[1056,128]{1,0:T(8,128)(2,1)S(1)} %sum_near_late.1.keep), channel_id=1, source_target_pairs={{0,12},{4,8},{8,4},{12,0},{1,13},{5,9},{9,5},{13,1},{2,14},{6,10},... | collective-permute-start | bytes 811016 | tf_op jit(solution)/shard_map/ppermute | solution.py:562
  177.0 10.6 %collective-permute-start.29 = (bf16[512,512]{1,0:T(8,128)(2,1)S(1)}, bf16[512,512]{1,0:T(8,128)(2,1)S(1)}, u32[]{:S(2)}, u32[]{:S(2)}) collective-permute-start(bf16[512,512]{1,0:T(8,128)(2,1)S(1)} %collective-permute-done.18.p2), channel_id=1, source_target_pairs={{0,1},{1,0},{2,3},{3,2},{4,5},{5,4},{6,7},{7,6},{8,9},{9,8},{10,11... | collective-permute-start | bytes 1572872 | tf_op jit(solution)/shard_map/ppermute | solution.py:562
  177.0 10.6 %collective-permute-start.28 = (bf16[512,512]{1,0:T(8,128)(2,1)S(1)}, bf16[512,512]{1,0:T(8,128)(2,1)S(1)}, u32[]{:S(2)}, u32[]{:S(2)}) collective-permute-start(bf16[512,512]{1,0:T(8,128)(2,1)S(1)} %get-tuple-element.129.p0), channel_id=1, source_target_pairs={{0,1},{1,0},{2,3},{3,2},{4,5},{5,4},{6,7},{7,6},{8,9},{9,8},{10,11... | collective-permute-start | bytes 1572872 | tf_op jit(solution)/shard_map/ppermute | solution.py:562
  179.2 6.8 %collective-permute-start.41 = (bf16[1056,128]{1,0:T(8,128)(2,1)S(1)}, bf16[1056,128]{1,0:T(8,128)(2,1)S(1)}, u32[]{:S(2)}, u32[]{:S(2)}) collective-permute-start(bf16[1056,128]{1,0:T(8,128)(2,1)S(1)} %sum_far_late.1.own), channel_id=1, source_target_pairs={{0,4},{4,0},{8,12},{12,8},{1,5},{5,1},{9,13},{13,9},{2,6},{6,2},{1... | collective-permute-start | bytes 811016 | tf_op jit(solution)/shard_map/ppermute | solution.py:562
  187.6 3.8 %copy-start.1 = (bf16[2048,512]{1,0:T(8,128)(2,1)S(1)}, bf16[2048,512]{1,0:T(8,128)(2,1)}, u32[]{:S(2)}) copy-start(bf16[2048,512]{1,0:T(8,128)(2,1)} %param.10) | copy-start | bytes 6291460

commit v4 on v3

--- a/solution.py
+++ b/solution.py
@@ -11,7 +11,7 @@
 SEQ = 1024
 LANES = 128
 PAIR = 2 * LANES
-CHUNK = 128
+CHUNK = 256
 EPS = 1e-05
 F32 = jnp.float32
 BF16 = jnp.bfloat16
@@ -182,13 +182,13 @@
 
 
 def gelu_parts(up, with_slope):
-    square = up * up
-    inner = jnp.tanh(GELU_C * up * (1.0 + GELU_A * square))
-    half = 0.5 * (1.0 + inner)
+    half = 0.5 + 0.5 * jnp.tanh(up * (GELU_C + GELU_C * GELU_A * (up * up)))
+    half, up = half.astype(BF16), up.astype(BF16)
+    value = up * half
     if not with_slope:
-        return up * half, None
-    slope = half + up * (0.5 * GELU_C) * (1.0 - inner * inner) * (1.0 + 3.0 * GELU_A * square)
-    return up * half, slope
+        return value, None
+    slope = 2 * GELU_C + 6 * GELU_C * GELU_A * (up * up)
+    return value, half + value * (1.0 - half) * slope
 
 
 def attention_kernel(
@@ -211,7 +211,7 @@
         @row_tiles(normed_two.shape[0], 256)
         def _(rows, r=r, w=w):
             up = nn(normed_two[rows, :], w[...])
-            active[rows, r * width : (r + 1) * width] = gelu_parts(up, False)[0].astype(BF16)
+            active[rows, r * width : (r + 1) * width] = gelu_parts(up, False)[0]
 
 
 def down_kernel(mid, active, w0, w1, w2, w3, y):
@@ -243,10 +243,9 @@
         for r in range(4):
             units = slice(r * width, (r + 1) * width)
             value, steep = gelu_parts(nn(normed_two[rows, :], up_w[r][...]), True)
-            value = value.astype(BF16)
             half = slice(r // 2 * width, (r // 2 + 1) * width)
             (send if r % 2 else keep)[rows, half] = value
-            slope[rows, units] = steep.astype(BF16)
+            slope[rows, units] = steep
             total = total + nt(value, down_w[r][...])
         y[rows, :] = total.astype(BF16)
 
@@ -257,7 +256,7 @@
     grad = jnp.zeros(dffn.shape, F32)
     for r in range(4):
         units = slice(r * width, (r + 1) * width)
-        dup = (slope[rows, units].astype(F32) * nn(dffn, down_w[r][...])).astype(BF16)
+        dup = slope[rows, units] * nn(dffn, down_w[r][...]).astype(BF16)
         if save is not None:
             half = slice(r // 2 * width, (r // 2 + 1) * width)
             save[r % 2][rows, half] = dup
@@ -513,26 +512,48 @@
     out[rows_at(1 - mine, size), :] = came[...].astype(F32)
 
 
-def finish_kernel(with_rms, where, p0, p1, p2, p3, out, *rms):
-    total, width = p0.shape
+def put_rows(place, part, out, rms, row_of):
+    total, width = part.shape
+    begin = place * (total // LANES)
+
+    @pl.loop(0, total // LANES, unroll=True)
+    def _(tile):
+        block = part[pl.ds(pl.multiple_of(tile * LANES, LANES), LANES), :].astype(F32)
+        out[pl.ds(pl.multiple_of((row_of + tile) * LANES, LANES), LANES), :] = block
+        if rms is not None:
+            square = block * block
+            high = square.astype(BF16)
+            low = (square - high.astype(F32)).astype(BF16)
+            ones = jnp.ones((width, LANES), BF16)
+            mean = (nn(high, ones) + nn(low, ones)) * (1.0 / width)
+            row = lax.broadcasted_iota(jnp.int32, (LANES, LANES), 0)
+            col = lax.broadcasted_iota(jnp.int32, (LANES, LANES), 1)
+            mean = jnp.sum(jnp.where(row == col, mean, 0.0), axis=0, keepdims=True)
+            rms[pl.ds(begin + tile, 1), :] = jnp.sqrt(mean + 1e-06)
+
+
+def finish_kernel(where, p0, p1, p2, p3, out):
     for r, part in enumerate((p0, p1, p2, p3)):
-        begin = where[PLACE] ^ r
-
-        @pl.loop(0, total // LANES, unroll=True)
-        def _(tile, part=part, begin=begin):
-            block = part[pl.ds(pl.multiple_of(tile * LANES, LANES), LANES), :].astype(F32)
-            to = begin * (total // LANES) + tile
-            out[pl.ds(pl.multiple_of(to * LANES, LANES), LANES), :] = block
-            if with_rms:
-                square = block * block
-                high = square.astype(BF16)
-                low = (square - high.astype(F32)).astype(BF16)
-                ones = jnp.ones((width, LANES), BF16)
-                mean = (nn(high, ones) + nn(low, ones)) * (1.0 / width)
-                row = lax.broadcasted_iota(jnp.int32, (LANES, LANES), 0)
-                col = lax.broadcasted_iota(jnp.int32, (LANES, LANES), 1)
-                mean = jnp.sum(jnp.where(row == col, mean, 0.0), axis=0, keepdims=True)
-                rms[0][pl.ds(to, 1), :] = jnp.sqrt(mean + 1e-06)
+        place = where[PLACE] ^ r
+        put_rows(place, part, out, None, place * (part.shape[0] // LANES))
+
+
+def most_kernel(where, p0, p1, p2, out, rms):
+    for r, part in enumerate((p0, p1, p2)):
+        place = where[PLACE] ^ r
+        put_rows(place, part, out, rms, place * (part.shape[0] // LANES))
+
+
+def rest_kernel(where, p3, rms_most, most, out, rms, block, sem):
+    del most
+    rms[...] = rms_most[...]
+    total = p3.shape[0]
+    place = where[PLACE] ^ 3
+    put_rows(place, p3, block, rms, 0)
+    to = out.at[pl.ds(pl.multiple_of(place * total, total), total), :]
+    copy = pltpu.make_async_copy(block, to, sem)
+    copy.start()
+    copy.wait()
 
 
 IN_VMEM = pl.BlockSpec(memory_space=pltpu.VMEM)
@@ -540,14 +561,15 @@
 ANYWHERE = pl.BlockSpec(memory_space=pl.ANY)
 
 
-def call(kernel, operands, outputs, scratch, name, us, far=()):
+def call(kernel, operands, outputs, scratch, name, us, far=(), in_place=False):
     near = [jax.ShapeDtypeStruct(shape, dtype) for shape, dtype in outputs]
     return pl.pallas_call(
         kernel,
         out_shape=near,
         in_specs=[IN_SMEM if v.dtype == jnp.int32 else IN_VMEM for v in operands]
         + [ANYWHERE] * len(far),
-        out_specs=[IN_VMEM] * len(near),
+        out_specs=[ANYWHERE] * in_place + [IN_VMEM] * (len(near) - in_place),
+        input_output_aliases={len(operands): 0} if in_place else {},
         scratch_shapes=scratch,
         compiler_params=pltpu.CompilerParams(vmem_limit_bytes=VMEM_LIMIT),
         cost_estimate=pl.CostEstimate(
@@ -588,13 +610,10 @@
     return join(where, own, across(own, 1, "dp"))
 
 
-def finish(where, own, far, with_rms, name):
-    rows, width = own.shape[0] * 4, own.shape[1]
-    outputs = [((rows, width), F32)] + [((rows // LANES, LANES), F32)] * with_rms
-    return call(
-        functools.partial(finish_kernel, with_rms),
-        (where, own, across(own, 1), far, across(far, 1)), outputs, [], name, 3.0,
-    )
+def finish(where, own, far, name):
+    shape = (own.shape[0] * 4, own.shape[1])
+    operands = (where, own, across(own, 1), far, across(far, 1))
+    return call(finish_kernel, operands, [(shape, F32)], [], name, 3.0)[0]
 
 
 def token_table(segment_start, pad_mask, place, tokens, parts):
@@ -647,7 +666,7 @@
     wide = (tokens, width)
     state_shape = (pairs, LANES, PAIR)
     dma = pltpu.SemaphoreType.DMA
-    mask_shape = ((chunks, CHUNK, PAIR), BF16)
+    mask_shape = ((chunks, CHUNK, 2 * CHUNK), BF16)
     mask_mem = pltpu.VMEM(*mask_shape)
     row_mem = pltpu.VMEM(wide, BF16)
 
@@ -718,25 +737,32 @@
     )
     (grad_x,) = attention_back((), grad_mid, dnum, dden, across(moved, 1), "attention_back_first")
     came = across(grad_x, 1, "section")
-    came = after(came, far_y)
+    rows = block_input.shape[0]
+    whole_outputs = [((rows, width), F32), ((rows // LANES, LANES), F32)]
+    most, rms_most = call(
+        most_kernel, (where, after(y, grad_x), across(y, 1), far_y), whole_outputs, [],
+        "activations_most", 2.8,
+    )
+    came = after(came, most)
 
     share = (width, units // 4)
-    keep, send = call(
-        down_grad_kernel, (where, own_g, other_g, came, across(came, 1), active, active_two),
-        [(share, BF16)] * 2, [turned_mem], "down_grad", LOW * 2.2,
-    )
-    down_keep, down_far = keep, across(send, 2)
     grad_mid, dnum, dden, moved, dattn, dup, dup_send, sums_two = call(
         functools.partial(ffn_back_kernel, True),
-        (where, own_g, after(came, send), *back_operands),
+        (where, own_g, came, *back_operands),
         back_shapes + [(wide, BF16), (half, BF16), (half, BF16), ((2, width), F32)],
         [grad_mem], "ffn_back_second", LOW * 5.0,
     )
     dup_other = across(dup_send, 1)
+    came_two = across(came, 1)
     end = across(moved, 1)
+    keep, send = call(
+        down_grad_kernel, (where, own_g, other_g, came, after(came_two, moved), active, active_two),
+        [(share, BF16)] * 2, [turned_mem], "down_grad", LOW * 2.2,
+    )
+    down_keep, down_far = keep, across(send, 2)
     dattn_other = across(dattn, 1)
     grad_x, dproj, dproj_send, sums = attention_back(
-        (sums_two,), grad_mid, dnum, dden, end, "attention_back_second"
+        (sums_two,), grad_mid, dnum, dden, after(end, send), "attention_back_second"
     )
     dproj_other = across(dproj_send, 1)
     keep, send = call(
@@ -773,9 +799,12 @@
     qkv_total, out_total, gain_total, bias_total = sum_over_dp(
         keep, late_far, where, "late", join_late
     )
-    activations, token_rms = finish(where, after(y, up_total), after(far_y, up_total), True, "activations")
+    activations, token_rms = call(
+        rest_kernel, (where, after(across(far_y, 1), down_total), rms_most), whole_outputs,
+        [grad_mem, dma(())], "activations_rest", 1.0, far=(most,), in_place=True,
+    )
     own = after(grad_x, send)
-    (input_grad,) = finish(where, own, across(own, 2), False, "input_grad")
+    input_grad = finish(where, own, across(own, 2), "input_grad")
     return (
         activations[None], input_grad[None], token_rms.reshape(1, -1), qkv_total[None],
         out_total[None], up_total[None], down_total[None], gain_total[None], bias_total[None],

time: 195 us -> 189 us (0.969)
  starting transfers between devices: 42 us -> 35.5 us
    ppermute x45, starting transfers between devices: 42 us -> 35.5 us  [across(): return lax.ppermute(block, axis, [(i, i ^ distance) for i in range(size)])]
    pallas_call x27 -> x28, Pallas kernels: 60.4 us -> 61.2 us  [call(): pl.pallas_call(kernel, out_shape=near, in_specs=[IN_SMEM if v.dtype == jn...]
  transfers between devices with their start and end apart: 45 -> 45, of which waited for: 21 -> 19; matrix products, arithmetic and copies ran while one was open for 4% -> 4% of each run, Pallas kernels for 17% -> 24%
where the time goes in v4:
time: 189 us; the launch traced here: 186 us
  waiting for transfers between devices  78.6 us (42%)
  Pallas kernels  61.2 us (32%)
  starting transfers between devices  35.5 us (19%)
  local copies, waits for them, and re-layouts  4.71 us (2%)
  other arithmetic  3.79 us (2%)
    ppermute x45, waiting for transfers between devices, across(): return lax.ppermute(block, axis, [(i, i ^ distance) for i in range(size)])  78.6 us
    pallas_call x28, Pallas kernels, call(): pl.pallas_call(kernel, out_shape=near, in_specs=[IN_SMEM if v.dtype == jn...  61.2 us
    ppermute x45, starting transfers between devices, across(): return lax.ppermute(block, axis, [(i, i ^ distance) for i in range(size)])  35.5 us
  transfers between devices with their start and end apart: 45, of which 19 were waited for; matrix products, arithmetic and copies ran while one was open for 4% of the time, Pallas kernels for 24%

profile of v4, /device:TPU:0, one launch (start us, length us, event | category | flops | bytes accessed | tf_op | source)
XLA Modules:
  0.0 185.5 jit_solution(6144470914269284750)
XLA Ops:
  0.7 3.0 %collective-permute-start.1 = (bf16[3,512,128]{2,1,0:T(8,128)(2,1)}, bf16[3,512,128]{2,1,0:T(8,128)(2,1)}, u32[]{:S(2)}, u32[]{:S(2)}) collective-permute-start(bf16[3,512,128]{2,1,0:T(8,128)(2,1)} %bitcast.58), channel_id=1, source_target_pairs={{0,2},{1,3},{2,0},{3,1},{4,6},{5,7},{6,4},{7,5},{8,10},{9,11},{10,... | collective-permute-start | bytes 1179656 | tf_op jit(solution)/shard_map/ppermute | solution.py:584
  3.8 1.9 %collective-permute-start.8 = (bf16[512,512]{1,0:T(8,128)(2,1)}, bf16[512,512]{1,0:T(8,128)(2,1)S(1)}, u32[]{:S(2)}, u32[]{:S(2)}) collective-permute-start(bf16[512,512]{1,0:T(8,128)(2,1)} %bitcast.38), channel_id=1, source_target_pairs={{0,2},{1,3},{2,0},{3,1},{4,6},{5,7},{6,4},{7,5},{8,10},{9,11},{10,... | collective-permute-start | bytes 1572872 | tf_op jit(solution)/shard_map/ppermute | solution.py:584
  5.7 1.2 reduce-window.6
  9.4 0.7 pad_add_fusion.1
  10.4 1.7 constant_dynamic-slice_fusion
  12.2 1.8 collective-permute-done.1.rest_5_
  13.9 0.8 dynamic-slice_convert_fusion
  14.7 0.7 compare_convert_fusion
  16.0 1.0 copy-done.5
  17.0 3.4 %qkv_first.1 = (bf16[512,512]{1,0:T(8,128)(2,1)S(1)}, bf16[512,512]{1,0:T(8,128)(2,1)S(1)}, bf16[512,512]{1,0:T(8,128)(2,1)S(1)}, bf16[4,128,256]{2,1,0:T(8,128)(2,1)S(1)}, bf16[3,512,512]{2,1,0:T(8,128)(2,1)S(1)}) custom-call(s32[3]{0:T(128)S(1)} %pad_add_fusion.where, bf16[512,512]{1,0:T(8,128)(2,1)S(1)} %constant_dynamic-slice_fusion.2.own.x, ...), custom_call_target="tpu_custom_call" | custom-call | flops 4400000000 | tf_op jit(solution)/shard_map/qkv_first/pallas_call | solution.py:566
  21.5 5.5 %collective-permute-done.8.w2.u2.rest_10_.rest_11_ = bf16[512,512]{1,0:T(8,128)(2,1)S(1)} collective-permute-done((bf16[512,512]{1,0:T(8,128)(2,1)}, bf16[512,512]{1,0:T(8,128)(2,1)S(1)}, u32[]{:S(2)}, u32[]{:S(2)}) %collective-permute-start.8) | collective-permute-done | bytes 524320 | tf_op jit(solution)/shard_map/ppermute | solution.py:584
  27.1 1.7 collective-permute-start.11
  29.3 3.3 %attention_first.1 = (f32[512,512]{1,0:T(8,128)S(1)}, bf16[512,512]{1,0:T(8,128)(2,1)S(1)}, bf16[512,512]{1,0:T(8,128)(2,1)S(1)}) custom-call(bf16[512,512]{1,0:T(8,128)(2,1)S(1)} %get-tuple-element.85.fq, bf16[512,512]{1,0:T(8,128)(2,1)S(1)} %get-tuple-element.86.fk, bf16[512,512]{1,0:T(8,128)(2,1)S(1)} %get-tuple-element.87.vv, ...), custom_call_target="tpu_custom_call" | custom-call | flops 6049999872 | tf_op jit(solution)/shard_map/attention_first/pallas_call | solution.py:566
  32.6 1.6 up_first.1.active
  34.3 5.9 %collective-permute-done.11.w2.d2.rest_14_.rest_15_ = bf16[512,512]{1,0:T(8,128)(2,1)S(1)} collective-permute-done((bf16[512,512]{1,0:T(8,128)(2,1)S(1)}, bf16[512,512]{1,0:T(8,128)(2,1)S(1)}, u32[]{:S(2)}, u32[]{:S(2)}) %collective-permute-start.11) | collective-permute-done | bytes 524320 | tf_op jit(solution)/shard_map/ppermute | solution.py:584
  40.2 1.9 %collective-permute-done.12.w3.d3.rest_15_.rest_16_ = bf16[512,512]{1,0:T(8,128)(2,1)S(1)} collective-permute-done((bf16[512,512]{1,0:T(8,128)(2,1)S(1)}, bf16[512,512]{1,0:T(8,128)(2,1)S(1)}, u32[]{:S(2)}, u32[]{:S(2)}) %collective-permute-start.12) | collective-permute-done | bytes 524320 | tf_op jit(solution)/shard_map/ppermute | solution.py:584
  42.1 1.3 down_first.1
  43.4 1.5 collective-permute-start.13
  44.9 12.5 %collective-permute-done.13.rest_0_ = bf16[512,512]{1,0:T(8,128)(2,1)S(1)} collective-permute-done((bf16[512,512]{1,0:T(8,128)(2,1)S(1)}, bf16[512,512]{1,0:T(8,128)(2,1)S(1)}, u32[]{:S(2)}, u32[]{:S(2)}) %collective-permute-start.13) | collective-permute-done | bytes 524320 | tf_op jit(solution)/shard_map/ppermute | solution.py:584
  57.4 2.4 %qkv_second.1 = (bf16[512,512]{1,0:T(8,128)(2,1)S(1)}, bf16[512,512]{1,0:T(8,128)(2,1)S(1)}, bf16[512,512]{1,0:T(8,128)(2,1)S(1)}, bf16[4,128,256]{2,1,0:T(8,128...) custom-call(s32[3]{0:T(128)S(1)} %pad_add_fusion.where, ...), custom_call_target="tpu_custom_call" | custom-call | flops 3849999872 | tf_op jit(solution)/shard_map/qkv_second/pallas_call | solution.py:566
  59.9 1.5 collective-permute-done.14.start
  61.4 6.4 %block_second.1 = (bf16[512,512]{1,0:T(8,128)(2,1)S(1)}, f32[512,512]{1,0:T(8,128)S(1)}, bf16[512,512]{1,0:T(8,128)(2,1)S(1)}, bf16[512,256]{1,0:T(8,128)(2,1)S(...) custom-call(bf16[512,512]{1,0:T(8,128)(2,1)S(1)} %get-tuple-element., ...), custom_call_target="tpu_custom_call" | custom-call | flops 11000000512 | tf_op jit(solution)/shard_map/block_second/pallas_call | solution.py:566
  67.9 5.2 %ffn_back_first.1 = (f32[512,512]{1,0:T(8,128)S(1)}, bf16[512,512]{1,0:T(8,128)(2,1)S(1)}, bf16[512,512]{1,0:T(8,128)(2,1)S(1)}, bf16[4,128,256]{2,1,0:T(8,128)(2,1)S(1)}) custom-call(s32[3]{0:T(128)S(1)} %pad_add_fusion.where, f32[512,512]{1,0:T(8,128)S(1)} %get-tuple-element.162.own_g, bf16[512,2048]{1,0:T(8,128)(2,1)S(1)} %get-tuple-element.102.rest_0_.rest_1_, ...), custom_call_target="tpu_custom_call" | custom-call | flops 4620000256 | tf_op jit(solution)/shard_map/ffn_back_first/pallas_call | solution.py:566
  73.3 1.4 collective-permute-start.15
  74.8 5.9 %attention_back_first.1 = bf16[512,512]{1,0:T(8,128)(2,1)S(1)} custom-call(bf16[512,512]{1,0:T(8,128)(2,1)S(1)} %get-tuple-element.95.fq.rest_4_.rest_5_, bf16[512,512]{1,0:T(8,128)(2,1)S(1)} %get-tuple-element.96.fk, bf16[512,512]{1,0:T(8,128)(2,1)S(1)} %get-tuple-element.97.vv, bf16[512,512]{1,0:T(8,128)(2,1)S(1)} %get-tuple-element.106.dnum, ...), custom_call_target="tpu_custom_call" | custom-call | flops 8249999872 | tf_op jit(solution)/shard_map/attention_back_first/pallas_call | solution.py:566
  80.7 1.6 collective-permute-start.18
  82.5 5.0 %collective-permute-done.15.p2 = bf16[512,512]{1,0:T(8,128)(2,1)S(1)} collective-permute-done((bf16[512,512]{1,0:T(8,128)(2,1)S(1)}, bf16[512,512]{1,0:T(8,128)(2,1)S(1)}, u32[]{:S(2)}, u32[]{:S(2)}) %collective-permute-start.15) | collective-permute-done | bytes 524320 | tf_op jit(solution)/shard_map/ppermute | solution.py:584
  87.5 3.4 %activations_most.1 = (f32[2048,512]{1,0:T(8,128)}, f32[16,128]{1,0:T(8,128)S(1)}) custom-call(s32[3]{0:T(128)S(1)} %pad_add_fusion.where, bf16[512,512]{1,0:T(8,128)(2,1)S(1)} %get-tuple-element.113.p0, bf16[512,512]{1,0:T(8,128)(2,1)S(1)} %collective-permute-done.19.p1, bf16[512,512]{1,0:T(8,128)(2,1)S(1)} %collective-permute-done.15.p2), custom_call_target="tpu_custom_call" | custom-call | flops 3080000000 | tf_op jit(solution)/shard_map/activations_most/pallas_call | solution.py:566
  90.9 4.1 %collective-permute-done.18.rest_0_.came = bf16[512,512]{1,0:T(8,128)(2,1)S(1)} collective-permute-done((bf16[512,512]{1,0:T(8,128)(2,1)S(1)}, bf16[512,512]{1,0:T(8,128)(2,1)S(1)}, u32[]{:S(2)}, u32[]{:S(2)}) %collective-permute-start.18) | collective-permute-done | bytes 524320 | tf_op jit(solution)/shard_map/ppermute | solution.py:584
  95.0 5.1 %ffn_back_second.1 = (f32[512,512]{1,0:T(8,128)S(1)}, bf16[512,512]{1,0:T(8,128)(2,1)S(1)}, bf16[512,512]{1,0:T(8,128)(2,1)S(1)}, bf16[4,128,256]{2,1,0:T(8,128)...) custom-call(s32[3]{0:T(128)S(1)} %pad_add_fusion.where, ...), custom_call_target="tpu_custom_call" | custom-call | flops 110000000 | tf_op jit(solution)/shard_map/ffn_back_second/pallas_call | solution.py:566
  100.8 1.9 %down_grad.1 = (bf16[512,512]{1,0:T(8,128)(2,1)S(1)}, bf16[512,512]{1,0:T(8,128)(2,1)S(1)}) custom-call(s32[3]{0:T(128)S(1)} %pad_add_fusion.where, f32[512,512]{1,0:T(8,128)S(1)} %get-tuple-element.162.own_g, f32[512,512]{1,0:T(8,128)S(1)} %get-tuple-element.161.other_g, bf16[512,512]{1,0:T(8,128)(2,1)S(1)} %collective-permute-done.18.rest_0_.came, ...), custom_call_target="tpu_custom_call" | custom-call | flops 48400000 | tf_op jit(solution)/shard_map/down_grad/pallas_call | solution.py:566
  102.7 1.1 collective-permute-start.22
  103.8 6.4 %attention_back_second.1 = (bf16[512,512]{1,0:T(8,128)(2,1)S(1)}, bf16[3,512,256]{2,1,0:T(8,128)(2,1)S(1)}, bf16[3,512,256]{2,1,0:T(8,128)(2,1)S(1)}, f32[8,512]{1,0:T(8,128)S(1)}) custom-call(bf16[512,512]{1,0:T(8,128)(2,1)S(1)} %get-tuple-element.95.fq.rest_4_.rest_5_, bf16[512,512]{1,0:T(8,128)(2,1)S(1)} %get-tuple-element.96.fk, ...), custom_call_target="tpu_custom_call" | custom-call | flops 165000000 | tf_op jit(solution)/shard_map/attention_back_second/pallas_call | solution.py:566
  110.9 6.1 %collective-permute-done.22.came = bf16[512,512]{1,0:T(8,128)(2,1)S(1)} collective-permute-done((bf16[512,512]{1,0:T(8,128)(2,1)S(1)}, bf16[512,512]{1,0:T(8,128)(2,1)S(1)}, u32[]{:S(2)}, u32[]{:S(2)}) %collective-permute-start.22) | collective-permute-done | bytes 524320 | tf_op jit(solution)/shard_map/ppermute | solution.py:584
  117.5 1.3 up_grad.1
  118.8 1.1 collective-permute-start.41
  119.9 1.2 collective-permute-done.30.sums_other
  121.1 1.3 late_grad.1
  122.4 1.1 collective-permute-start.37
  123.5 0.7 halve_down.1
  124.2 1.6 collective-permute-start.31
  125.8 1.0 collective-permute-start.35
  126.8 6.9 %collective-permute-done.41.came = bf16[512,512]{1,0:T(8,128)(2,1)S(1)} collective-permute-done((bf16[512,512]{1,0:T(8,128)(2,1)S(1)}, bf16[512,512]{1,0:T(8,128)(2,1)S(1)}, u32[]{:S(2)}, u32[]{:S(2)}) %collective-permute-start.41) | collective-permute-done | bytes 524320 | tf_op jit(solution)/shard_map/ppermute | solution.py:584
  133.7 0.7 halve_up.1
  134.4 1.6 collective-permute-start.42
  136.1 2.5 %collective-permute-start.32 = (bf16[256,512]{1,0:T(8,128)(2,1)S(1)}, bf16[256,512]{1,0:T(8,128)(2,1)S(1)}, u32[]{:S(2)}, u32[]{:S(2)}) collective-permute-start(bf16[256,512]{1,0:T(8,128)(2,1)S(1)} %sum_near_down.1.keep), channel_id=1, source_target_pairs={{0,12},{4,8},{8,4},{12,0},{1,13},{5,9},{9,5},{13,1},{2,14},{6,10},... | collective-permute-start | bytes 786440 | tf_op jit(solution)/shard_map/ppermute | solution.py:584
  138.6 6.7 %collective-permute-done.37.came = bf16[2112,128]{1,0:T(8,128)(2,1)S(1)} collective-permute-done((bf16[2112,128]{1,0:T(8,128)(2,1)S(1)}, bf16[2112,128]{1,0:T(8,128)(2,1)S(1)}, u32[]{:S(2)}, u32[]{:S(2)}) %collective-permute-start.37) | collective-permute-done | bytes 540704 | tf_op jit(solution)/shard_map/ppermute | solution.py:584
  145.3 0.7 halve_late.1
  146.0 1.6 collective-permute-start.38
  147.7 2.5 %collective-permute-start.43 = (bf16[256,512]{1,0:T(8,128)(2,1)S(1)}, bf16[256,512]{1,0:T(8,128)(2,1)S(1)}, u32[]{:S(2)}, u32[]{:S(2)}) collective-permute-start(bf16[256,512]{1,0:T(8,128)(2,1)S(1)} %sum_near_up.1.keep), channel_id=1, source_target_pairs={{0,12},{4,8},{8,4},{12,0},{1,13},{5,9},{9,5},{13,1},{2,14},{6,10},... | collective-permute-start | bytes 786440 | tf_op jit(solution)/shard_map/ppermute | solution.py:584
  150.3 0.7 collective-permute-start.33
  151.0 4.5 %collective-permute-done.35.p2 = bf16[512,512]{1,0:T(8,128)(2,1)S(1)} collective-permute-done((bf16[512,512]{1,0:T(8,128)(2,1)S(1)}, bf16[512,512]{1,0:T(8,128)(2,1)S(1)}, u32[]{:S(2)}, u32[]{:S(2)}) %collective-permute-start.35) | collective-permute-done | bytes 524320 | tf_op jit(solution)/shard_map/ppermute | solution.py:584
  155.6 4.3 %collective-permute-done.38.came = bf16[1056,128]{1,0:T(8,128)(2,1)S(1)} collective-permute-done((bf16[1056,128]{1,0:T(8,128)(2,1)S(1)}, bf16[1056,128]{1,0:T(8,128)(2,1)S(1)}, u32[]{:S(2)}, u32[]{:S(2)}) %collective-permute-start.38) | collective-permute-done | bytes 270368 | tf_op jit(solution)/shard_map/ppermute | solution.py:584
  159.9 2.4 %collective-permute-done.43.came = bf16[256,512]{1,0:T(8,128)(2,1)S(1)} collective-permute-done((bf16[256,512]{1,0:T(8,128)(2,1)S(1)}, bf16[256,512]{1,0:T(8,128)(2,1)S(1)}, u32[]{:S(2)}, u32[]{:S(2)}) %collective-permute-start.43) | collective-permute-done | bytes 262176 | tf_op jit(solution)/shard_map/ppermute | solution.py:584
  162.3 1.3 collective-permute-start.39
  163.7 2.4 %collective-permute-done.33.came = bf16[256,512]{1,0:T(8,128)(2,1)S(1)} collective-permute-done((bf16[256,512]{1,0:T(8,128)(2,1)S(1)}, bf16[256,512]{1,0:T(8,128)(2,1)S(1)}, u32[]{:S(2)}, u32[]{:S(2)}) %collective-permute-start.33) | collective-permute-done | bytes 262176 | tf_op jit(solution)/shard_map/ppermute | solution.py:584
  166.1 1.6 whole.2
  167.7 2.4 %activations_rest.1 = (f32[2048,512]{1,0:T(8,128)}, f32[16,128]{1,0:T(8,128)}) custom-call(s32[3]{0:T(128)S(1)} %pad_add_fusion.where, bf16[512,512]{1,0:T(8,128)(2,1)S(1)} %collective-permute-done.16.p3, f32[16,128]{1,0:T(8,128)S(1)} %get-tuple-element.145.rms_most, f32[2048,512]{1,0:T(8,128)} %get-tuple-element.114.most), custom_call_target="tpu_custom_call", output_to_operand_aliasing={{0}: (3, {})} | custom-call | flops 1100000000 | tf_op jit(solution)/shard_map/activations_rest/pallas_call | solution.py:566
  170.1 3.5 %collective-permute-done.39.came = bf16[1056,128]{1,0:T(8,128)(2,1)S(1)} collective-permute-done((bf16[1056,128]{1,0:T(8,128)(2,1)S(1)}, bf16[1056,128]{1,0:T(8,128)(2,1)S(1)}, u32[]{:S(2)}, u32[]{:S(2)}) %collective-permute-start.39) | collective-permute-done | bytes 270368 | tf_op jit(solution)/shard_map/ppermute | solution.py:584
  173.7 3.9 %collective-permute-start.40 = (bf16[1056,128]{1,0:T(8,128)(2,1)S(1)}, bf16[1056,128]{1,0:T(8,128)(2,1)S(1)}, u32[]{:S(2)}, u32[]{:S(2)}) collective-permute-start(bf16[1056,128]{1,0:T(8,128)(2,1)S(1)} %sum_far_late.1.own), channel_id=1, source_target_pairs={{0,4},{4,0},{8,12},{12,8},{1,5},{5,1},{9,13},{13,9},{2,6},{6,2},{1... | collective-permute-start | bytes 811016 | tf_op jit(solution)/shard_map/ppermute | solution.py:584
  177.5 2.8 %input_grad.1 = f32[2048,512]{1,0:T(8,128)} custom-call(s32[3]{0:T(128)S(1)} %pad_add_fusion.where, bf16[512,512]{1,0:T(8,128)(2,1)S(1)} %get-tuple-element.147.p0, bf16[512,512]{1,0:T(8,128)(2,1)S(1)} %collective-permute-done.34.p1, bf16[512,512]{1,0:T(8,128)(2,1)S(1)} %collective-permute-done.35.p2, bf16[512,512]{1,0:T(8,128)(2,1)S(1)} %collective-permute-done.36.p3), custom_call_target="tpu_custom_call" | custom-call | flops 3300000000 | tf_op jit(solution)/shard_map/input_grad/pallas_call | solution.py:566
  180.4 1.6 whole.3
  181.9 1.8 collective-permute-done.40.came
  183.8 1.6 join_late.1
  (93 shorter events, 7.4 us)
Async XLA Ops:
  0.6 8.1 %copy-start = (bf16[2048,512]{1,0:T(8,128)(2,1)S(1)}, bf16[2048,512]{1,0:T(8,128)(2,1)}, u32[]{:S(2)}) copy-start(bf16[2048,512]{1,0:T(8,128)(2,1)} %param.10) | copy-start | bytes 6291460
  0.7 15.4 %copy-start.4 = (f32[1,2,512]{2,1,0:T(2,128)S(1)}, f32[1,2,512]{2,1,0:T(2,128)}, u32[]{:S(2)}) copy-start(f32[1,2,512]{2,1,0:T(2,128)} %param.18) | copy-start | bytes 12292
  0.7 15.3 %copy-start.7 = (f32[1,2,512]{2,1,0:T(2,128)S(1)}, f32[1,2,512]{2,1,0:T(2,128)}, u32[]{:S(2)}) copy-start(f32[1,2,512]{2,1,0:T(2,128)} %param.19) | copy-start | bytes 12292
  0.7 13.3 %collective-permute-start.1 = (bf16[3,512,128]{2,1,0:T(8,128)(2,1)}, bf16[3,512,128]{2,1,0:T(8,128)(2,1)}, u32[]{:S(2)}, u32[]{:S(2)}) collective-permute-start(bf16[3,512,128]{2,1,0:T(8,128)(2,1)} %bitcast.58), channel_id=1, source_target_pairs={{0,2},{1,3},{2,0},{3,1},{4,6},{5,7},{6,4},{7,5},{8,10},{9,11},{10,... | collective-permute-start | bytes 1179656 | tf_op jit(solution)/shard_map/ppermute | solution.py:584
  3.7 12.0 %collective-permute-start = (bf16[3,512,128]{2,1,0:T(8,128)(2,1)}, bf16[3,512,128]{2,1,0:T(8,128)(2,1)}, u32[]{:S(2)}, u32[]{:S(2)}) collective-permute-start(bf16[3,512,128]{2,1,0:T(8,128)(2,1)} %bitcast.59), channel_id=1, source_target_pairs={{0,1},{1,0},{2,3},{3,2},{4,5},{5,4},{6,7},{7,6},{8,9},{9,8},{10,11... | collective-permute-start | bytes 1179656 | tf_op jit(solution)/shard_map/ppermute | solution.py:584
  3.7 17.3 %collective-permute-start.5 = (bf16[128,512]{1,0:T(8,128)(2,1)}, bf16[128,512]{1,0:T(8,128)(2,1)}, u32[]{:S(2)}, u32[]{:S(2)}) collective-permute-start(bf16[128,512]{1,0:T(8,128)(2,1)} %bitcast.61), channel_id=1, source_target_pairs={{0,2},{1,3},{2,0},{3,1},{4,6},{5,7},{6,4},{7,5},{8,10},{9,11},{10,... | collective-permute-start | bytes 393224 | tf_op jit(solution)/shard_map/ppermute | solution.py:584
  3.8 23.2 %collective-permute-start.8 = (bf16[512,512]{1,0:T(8,128)(2,1)}, bf16[512,512]{1,0:T(8,128)(2,1)S(1)}, u32[]{:S(2)}, u32[]{:S(2)}) collective-permute-start(bf16[512,512]{1,0:T(8,128)(2,1)} %bitcast.38), channel_id=1, source_target_pairs={{0,2},{1,3},{2,0},{3,1},{4,6},{5,7},{6,4},{7,5},{8,10},{9,11},{10,... | collective-permute-start | bytes 1572872 | tf_op jit(solution)/shard_map/ppermute | solution.py:584
  13.9 2.1 %collective-permute-start.2 = (bf16[3,512,128]{2,1,0:T(8,128)(2,1)}, bf16[3,512,128]{2,1,0:T(8,128)(2,1)}, u32[]{:S(2)}, u32[]{:S(2)}) collective-permute-start(bf16[3,512,128]{2,1,0:T(8,128)(2,1)} %collective-permute-done.1.rest_5_), channel_id=1, source_target_pairs={{0,1},{1,0},{2,3},{3,2},{4,5},{5,4},{6,7},{7,6},{8,9},{9,8},{10,11... | collective-permute-start | bytes 1179656 | tf_op jit(solution)/shard_map/ppermute | solution.py:584
  16.0 1.0 copy-start.5
  17.0 3.6 %copy-start.6 = (bf16[1,128,512]{2,1,0:T(8,128)(2,1)S(1)}, bf16[1,128,512]{2,1,0:T(8,128)(2,1)}, u32[]{:S(2)}) copy-start(bf16[1,128,512]{2,1,0:T(8,128)(2,1)} %param.15) | copy-start | bytes 393220
  17.0 4.2 %copy-start.2 = (bf16[1,512,512]{2,1,0:T(8,128)(2,1)S(1)}, bf16[1,512,512]{2,1,0:T(8,128)(2,1)}, u32[]{:S(2)}) copy-start(bf16[1,512,512]{2,1,0:T(8,128)(2,1)} %param.16) | copy-start | bytes 1572868
  17.0 10.0 %copy-start.3 = (bf16[1,512,512]{2,1,0:T(8,128)(2,1)S(1)}, bf16[1,512,512]{2,1,0:T(8,128)(2,1)}, u32[]{:S(2)}) copy-start(bf16[1,512,512]{2,1,0:T(8,128)(2,1)} %param.17) | copy-start | bytes 1572868
  20.4 8.9 %collective-permute-start.3 = (bf16[4,128,256]{2,1,0:T(8,128)(2,1)S(1)}, bf16[4,128,256]{2,1,0:T(8,128)(2,1)S(1)}, u32[]{:S(2)}, u32[]{:S(2)}) collective-permute-start(bf16[4,128,256]{2,1,0:T(8,128)(2,1)S(1)} %get-tuple-element.88), channel_id=1, source_target_pairs={{0,1},{1,0},{2,3},{3,2},{4,5},{5,4},{6,7},{7,6},{8,9},{9,8},{10,11... | collective-permute-start | bytes 786440 | tf_op jit(solution)/shard_map/ppermute | solution.py:584
  20.7 8.1 %collective-permute-start.4 = (bf16[128,512]{1,0:T(8,128)(2,1)S(1)}, bf16[128,512]{1,0:T(8,128)(2,1)S(1)}, u32[]{:S(2)}, u32[]{:S(2)}) collective-permute-start(bf16[128,512]{1,0:T(8,128)(2,1)S(1)} %bitcast.62), channel_id=1, source_target_pairs={{0,1},{1,0},{2,3},{3,2},{4,5},{5,4},{6,7},{7,6},{8,9},{9,8},{10,11... | collective-permute-start | bytes 393224 | tf_op jit(solution)/shard_map/ppermute | solution.py:584
  21.0 7.8 %collective-permute-start.6 = (bf16[128,512]{1,0:T(8,128)(2,1)}, bf16[128,512]{1,0:T(8,128)(2,1)S(1)}, u32[]{:S(2)}, u32[]{:S(2)}) collective-permute-start(bf16[128,512]{1,0:T(8,128)(2,1)} %collective-permute-done.5.w2), channel_id=1, source_target_pairs={{0,1},{1,0},{2,3},{3,2},{4,5},{5,4},{6,7},{7,6},{8,9},{9,8},{10,11... | collective-permute-start | bytes 393224 | tf_op jit(solution)/shard_map/ppermute | solution.py:584
  21.2 11.4 %collective-permute-start.7 = (bf16[512,512]{1,0:T(8,128)(2,1)S(1)}, bf16[512,512]{1,0:T(8,128)(2,1)S(1)}, u32[]{:S(2)}, u32[]{:S(2)}) collective-permute-start(bf16[512,512]{1,0:T(8,128)(2,1)S(1)} %bitcast.39), channel_id=1, source_target_pairs={{0,1},{1,0},{2,3},{3,2},{4,5},{5,4},{6,7},{7,6},{8,9},{9,8},{10,11... | collective-permute-start | bytes 1572872 | tf_op jit(solution)/shard_map/ppermute | solution.py:584
  27.1 13.1 %collective-permute-start.11 = (bf16[512,512]{1,0:T(8,128)(2,1)S(1)}, bf16[512,512]{1,0:T(8,128)(2,1)S(1)}, u32[]{:S(2)}, u32[]{:S(2)}) collective-permute-start(bf16[512,512]{1,0:T(8,128)(2,1)S(1)} %bitcast.44), channel_id=1, source_target_pairs={{0,2},{1,3},{2,0},{3,1},{4,6},{5,7},{6,4},{7,5},{8,10},{9,11},{10,... | collective-permute-start | bytes 1572872 | tf_op jit(solution)/shard_map/ppermute | solution.py:584
  28.8 11.4 %collective-permute-start.10 = (bf16[512,512]{1,0:T(8,128)(2,1)S(1)}, bf16[512,512]{1,0:T(8,128)(2,1)S(1)}, u32[]{:S(2)}, u32[]{:S(2)}) collective-permute-start(bf16[512,512]{1,0:T(8,128)(2,1)S(1)} %bitcast.45), channel_id=1, source_target_pairs={{0,1},{1,0},{2,3},{3,2},{4,5},{5,4},{6,7},{7,6},{8,9},{9,8},{10,11... | collective-permute-start | bytes 1572872 | tf_op jit(solution)/shard_map/ppermute | solution.py:584
  28.8 3.8 %collective-permute-start.9 = (bf16[512,512]{1,0:T(8,128)(2,1)S(1)}, bf16[512,512]{1,0:T(8,128)(2,1)S(1)}, u32[]{:S(2)}, u32[]{:S(2)}) collective-permute-start(bf16[512,512]{1,0:T(8,128)(2,1)S(1)} %collective-permute-done.8.w2.u2.rest_10_.rest_11_), channel_id=1, source_target_pairs={{0,1},{1,0},{2,3},{3,2},{4,5},{5,4},{6,7},{7,6},{8,9},{9,8},{10,11... | collective-permute-start | bytes 1572872 | tf_op jit(solution)/shard_map/ppermute | solution.py:584
  40.2 1.9 %collective-permute-start.12 = (bf16[512,512]{1,0:T(8,128)(2,1)S(1)}, bf16[512,512]{1,0:T(8,128)(2,1)S(1)}, u32[]{:S(2)}, u32[]{:S(2)}) collective-permute-start(bf16[512,512]{1,0:T(8,128)(2,1)S(1)} %collective-permute-done.11.w2.d2.rest_14_.rest_15_), channel_id=1, source_target_pairs={{0,1},{1,0},{2,3},{3,2},{4,5},{5,4},{6,7},{7,6},{8,9},{9,8},{10,11... | collective-permute-start | bytes 1572872 | tf_op jit(solution)/shard_map/ppermute | solution.py:584
  43.4 14.0 %collective-permute-start.13 = (bf16[512,512]{1,0:T(8,128)(2,1)S(1)}, bf16[512,512]{1,0:T(8,128)(2,1)S(1)}, u32[]{:S(2)}, u32[]{:S(2)}) collective-permute-start(bf16[512,512]{1,0:T(8,128)(2,1)S(1)} %down_first.1), channel_id=1, source_target_pairs={{0,16},{16,0},{1,17},{17,1},{2,18},{18,2},{3,19},{19,3},{4,20},{20... | collective-permute-start | bytes 1572872 | tf_op jit(solution)/shard_map/ppermute | solution.py:584
  59.8 1.6 collective-permute-start.14
  73.1 1.7 collective-permute-start.17
  73.3 14.2 %collective-permute-start.15 = (bf16[512,512]{1,0:T(8,128)(2,1)S(1)}, bf16[512,512]{1,0:T(8,128)(2,1)S(1)}, u32[]{:S(2)}, u32[]{:S(2)}) collective-permute-start(bf16[512,512]{1,0:T(8,128)(2,1)S(1)} %get-tuple-element.113.p0), channel_id=1, source_target_pairs={{0,2},{1,3},{2,0},{3,1},{4,6},{5,7},{6,4},{7,5},{8,10},{9,11},{10,... | collective-permute-start | bytes 1572872 | tf_op jit(solution)/shard_map/ppermute | solution.py:584
  74.7 12.8 %collective-permute-start.19 = (bf16[512,512]{1,0:T(8,128)(2,1)S(1)}, bf16[512,512]{1,0:T(8,128)(2,1)S(1)}, u32[]{:S(2)}, u32[]{:S(2)}) collective-permute-start(bf16[512,512]{1,0:T(8,128)(2,1)S(1)} %get-tuple-element.113.p0), channel_id=1, source_target_pairs={{0,1},{1,0},{2,3},{3,2},{4,5},{5,4},{6,7},{7,6},{8,9},{9,8},{10,11... | collective-permute-start | bytes 1572872 | tf_op jit(solution)/shard_map/ppermute | solution.py:584
  80.7 14.3 %collective-permute-start.18 = (bf16[512,512]{1,0:T(8,128)(2,1)S(1)}, bf16[512,512]{1,0:T(8,128)(2,1)S(1)}, u32[]{:S(2)}, u32[]{:S(2)}) collective-permute-start(bf16[512,512]{1,0:T(8,128)(2,1)S(1)} %attention_back_first.1), channel_id=1, source_target_pairs={{0,16},{16,0},{1,17},{17,1},{2,18},{18,2},{3,19},{19,3},{4,20},{20... | collective-permute-start | bytes 1572872 | tf_op jit(solution)/shard_map/ppermute | solution.py:584
  82.3 18.5 %collective-permute-start.21 = (bf16[512,1024]{1,0:T(8,128)(2,1)S(1)}, bf16[512,1024]{1,0:T(8,128)(2,1)S(1)}, u32[]{:S(2)}, u32[]{:S(2)}) collective-permute-start(bf16[512,1024]{1,0:T(8,128)(2,1)S(1)} %get-tuple-element.119), channel_id=1, source_target_pairs={{0,1},{1,0},{2,3},{3,2},{4,5},{5,4},{6,7},{7,6},{8,9},{9,8},{10,11... | collective-permute-start | bytes 3145736 | tf_op jit(solution)/shard_map/ppermute | solution.py:584
  95.0 5.7 %collective-permute-start.20 = (bf16[512,512]{1,0:T(8,128)(2,1)S(1)}, bf16[512,512]{1,0:T(8,128)(2,1)S(1)}, u32[]{:S(2)}, u32[]{:S(2)}) collective-permute-start(bf16[512,512]{1,0:T(8,128)(2,1)S(1)} %collective-permute-done.18.rest_0_.came), channel_id=1, source_target_pairs={{0,1},{1,0},{2,3},{3,2},{4,5},{5,4},{6,7},{7,6},{8,9},{9,8},{10,11... | collective-permute-start | bytes 1572872 | tf_op jit(solution)/shard_map/ppermute | solution.py:584
  100.1 16.9 %collective-permute-start.27 = (bf16[512,1024]{1,0:T(8,128)(2,1)S(1)}, bf16[512,1024]{1,0:T(8,128)(2,1)S(1)}, u32[]{:S(2)}, u32[]{:S(2)}) collective-permute-start(bf16[512,1024]{1,0:T(8,128)(2,1)S(1)} %get-tuple-element.132), channel_id=1, source_target_pairs={{0,1},{1,0},{2,3},{3,2},{4,5},{5,4},{6,7},{7,6},{8,9},{9,8},{10,11... | collective-permute-start | bytes 3145736 | tf_op jit(solution)/shard_map/ppermute | solution.py:584
  100.7 3.0 %collective-permute-start.24 = (bf16[4,128,256]{2,1,0:T(8,128)(2,1)S(1)}, bf16[4,128,256]{2,1,0:T(8,128)(2,1)S(1)}, u32[]{:S(2)}, u32[]{:S(2)}) collective-permute-start(bf16[4,128,256]{2,1,0:T(8,128)(2,1)S(1)} %get-tuple-element.116), channel_id=1, source_target_pairs={{0,1},{1,0},{2,3},{3,2},{4,5},{5,4},{6,7},{7,6},{8,9},{9,8},{10,11... | collective-permute-start | bytes 786440 | tf_op jit(solution)/shard_map/ppermute | solution.py:584
  102.7 14.3 %collective-permute-start.22 = (bf16[512,512]{1,0:T(8,128)(2,1)S(1)}, bf16[512,512]{1,0:T(8,128)(2,1)S(1)}, u32[]{:S(2)}, u32[]{:S(2)}) collective-permute-start(bf16[512,512]{1,0:T(8,128)(2,1)S(1)} %get-tuple-element.121), channel_id=1, source_target_pairs={{0,2},{1,3},{2,0},{3,1},{4,6},{5,7},{6,4},{7,5},{8,10},{9,11},{10,... | collective-permute-start | bytes 1572872 | tf_op jit(solution)/shard_map/ppermute | solution.py:584
  110.2 9.8 %collective-permute-start.25 = (bf16[3,512,256]{2,1,0:T(8,128)(2,1)S(1)}, bf16[3,512,256]{2,1,0:T(8,128)(2,1)S(1)}, u32[]{:S(2)}, u32[]{:S(2)}) collective-permute-start(bf16[3,512,256]{2,1,0:T(8,128)(2,1)S(1)} %get-tuple-element.129), channel_id=1, source_target_pairs={{0,1},{1,0},{2,3},{3,2},{4,5},{5,4},{6,7},{7,6},{8,9},{9,8},{10,11... | collective-permute-start | bytes 2359304 | tf_op jit(solution)/shard_map/ppermute | solution.py:584
  110.4 7.2 %collective-permute-start.26 = (bf16[512,512]{1,0:T(8,128)(2,1)S(1)}, bf16[512,512]{1,0:T(8,128)(2,1)S(1)}, u32[]{:S(2)}, u32[]{:S(2)}) collective-permute-start(bf16[512,512]{1,0:T(8,128)(2,1)S(1)} %get-tuple-element.130.normed_own), channel_id=1, source_target_pairs={{0,1},{1,0},{2,3},{3,2},{4,5},{5,4},{6,7},{7,6},{8,9},{9,8},{10,11... | collective-permute-start | bytes 1572872 | tf_op jit(solution)/shard_map/ppermute | solution.py:584
  110.7 9.2 %collective-permute-start.23 = (bf16[512,512]{1,0:T(8,128)(2,1)S(1)}, bf16[512,512]{1,0:T(8,128)(2,1)S(1)}, u32[]{:S(2)}, u32[]{:S(2)}) collective-permute-start(bf16[512,512]{1,0:T(8,128)(2,1)S(1)} %get-tuple-element.122.normed_own), channel_id=1, source_target_pairs={{0,1},{1,0},{2,3},{3,2},{4,5},{5,4},{6,7},{7,6},{8,9},{9,8},{10,11... | collective-permute-start | bytes 1572872 | tf_op jit(solution)/shard_map/ppermute | solution.py:584
  117.0 2.9 %collective-permute-start.29 = (bf16[512,512]{1,0:T(8,128)(2,1)S(1)}, bf16[512,512]{1,0:T(8,128)(2,1)S(1)}, u32[]{:S(2)}, u32[]{:S(2)}) collective-permute-start(bf16[512,512]{1,0:T(8,128)(2,1)S(1)} %get-tuple-element.138.dattn_own), channel_id=1, source_target_pairs={{0,1},{1,0},{2,3},{3,2},{4,5},{5,4},{6,7},{7,6},{8,9},{9,8},{10,11... | collective-permute-start | bytes 1572872 | tf_op jit(solution)/shard_map/ppermute | solution.py:584
  117.0 2.9 %collective-permute-start.28 = (bf16[512,256]{1,0:T(8,128)(2,1)S(1)}, bf16[512,256]{1,0:T(8,128)(2,1)S(1)}, u32[]{:S(2)}, u32[]{:S(2)}) collective-permute-start(bf16[512,256]{1,0:T(8,128)(2,1)S(1)} %get-tuple-element.137), channel_id=1, source_target_pairs={{0,1},{1,0},{2,3},{3,2},{4,5},{5,4},{6,7},{7,6},{8,9},{9,8},{10,11... | collective-permute-start | bytes 786440 | tf_op jit(solution)/shard_map/ppermute | solution.py:584
  118.8 14.9 %collective-permute-start.41 = (bf16[512,512]{1,0:T(8,128)(2,1)S(1)}, bf16[512,512]{1,0:T(8,128)(2,1)S(1)}, u32[]{:S(2)}, u32[]{:S(2)}) collective-permute-start(bf16[512,512]{1,0:T(8,128)(2,1)S(1)} %get-tuple-element.135), channel_id=1, source_target_pairs={{0,2},{1,3},{2,0},{3,1},{4,6},{5,7},{6,4},{7,5},{8,10},{9,11},{10,... | collective-permute-start | bytes 1572872 | tf_op jit(solution)/shard_map/ppermute | solution.py:584
  119.9 1.2 collective-permute-start.30
  122.4 22.9 %collective-permute-start.37 = (bf16[2112,128]{1,0:T(8,128)(2,1)S(1)}, bf16[2112,128]{1,0:T(8,128)(2,1)S(1)}, u32[]{:S(2)}, u32[]{:S(2)}) collective-permute-start(bf16[2112,128]{1,0:T(8,128)(2,1)S(1)} %get-tuple-element.140), channel_id=1, source_target_pairs={{0,2},{1,3},{2,0},{3,1},{4,6},{5,7},{6,4},{7,5},{8,10},{9,11},{10,... | collective-permute-start | bytes 1622024 | tf_op jit(solution)/shard_map/ppermute | solution.py:584
  124.2 11.9 %collective-permute-start.31 = (bf16[256,512]{1,0:T(8,128)(2,1)S(1)}, bf16[256,512]{1,0:T(8,128)(2,1)S(1)}, u32[]{:S(2)}, u32[]{:S(2)}) collective-permute-start(bf16[256,512]{1,0:T(8,128)(2,1)S(1)} %get-tuple-element.143), channel_id=1, source_target_pairs={{0,4},{4,0},{8,12},{12,8},{1,5},{5,1},{9,13},{13,9},{2,6},{6,2},{1... | collective-permute-start | bytes 786440 | tf_op jit(solution)/shard_map/ppermute | solution.py:584
  125.8 29.8 %collective-permute-start.35 = (bf16[512,512]{1,0:T(8,128)(2,1)S(1)}, bf16[512,512]{1,0:T(8,128)(2,1)S(1)}, u32[]{:S(2)}, u32[]{:S(2)}) collective-permute-start(bf16[512,512]{1,0:T(8,128)(2,1)S(1)} %get-tuple-element.147.p0), channel_id=1, source_target_pairs={{0,2},{1,3},{2,0},{3,1},{4,6},{5,7},{6,4},{7,5},{8,10},{9,11},{10,... | collective-permute-start | bytes 1572872 | tf_op jit(solution)/shard_map/ppermute | solution.py:584
  134.4 13.2 %collective-permute-start.42 = (bf16[256,512]{1,0:T(8,128)(2,1)S(1)}, bf16[256,512]{1,0:T(8,128)(2,1)S(1)}, u32[]{:S(2)}, u32[]{:S(2)}) collective-permute-start(bf16[256,512]{1,0:T(8,128)(2,1)S(1)} %get-tuple-element.156), channel_id=1, source_target_pairs={{0,4},{4,0},{8,12},{12,8},{1,5},{5,1},{9,13},{13,9},{2,6},{6,2},{1... | collective-permute-start | bytes 786440 | tf_op jit(solution)/shard_map/ppermute | solution.py:584
  136.1 14.2 %collective-permute-start.32 = (bf16[256,512]{1,0:T(8,128)(2,1)S(1)}, bf16[256,512]{1,0:T(8,128)(2,1)S(1)}, u32[]{:S(2)}, u32[]{:S(2)}) collective-permute-start(bf16[256,512]{1,0:T(8,128)(2,1)S(1)} %sum_near_down.1.keep), channel_id=1, source_target_pairs={{0,12},{4,8},{8,4},{12,0},{1,13},{5,9},{9,5},{13,1},{2,14},{6,10},... | collective-permute-start | bytes 786440 | tf_op jit(solution)/shard_map/ppermute | solution.py:584
  146.0 13.9 %collective-permute-start.38 = (bf16[1056,128]{1,0:T(8,128)(2,1)S(1)}, bf16[1056,128]{1,0:T(8,128)(2,1)S(1)}, u32[]{:S(2)}, u32[]{:S(2)}) collective-permute-start(bf16[1056,128]{1,0:T(8,128)(2,1)S(1)} %get-tuple-element.151), channel_id=1, source_target_pairs={{0,4},{4,0},{8,12},{12,8},{1,5},{5,1},{9,13},{13,9},{2,6},{6,2},{1... | collective-permute-start | bytes 811016 | tf_op jit(solution)/shard_map/ppermute | solution.py:584
  147.6 20.1 %collective-permute-start.16 = (bf16[512,512]{1,0:T(8,128)(2,1)S(1)}, bf16[512,512]{1,0:T(8,128)(2,1)S(1)}, u32[]{:S(2)}, u32[]{:S(2)}) collective-permute-start(bf16[512,512]{1,0:T(8,128)(2,1)S(1)} %collective-permute-done.15.p2), channel_id=1, source_target_pairs={{0,1},{1,0},{2,3},{3,2},{4,5},{5,4},{6,7},{7,6},{8,9},{9,8},{10,11... | collective-permute-start | bytes 1572872 | tf_op jit(solution)/shard_map/ppermute | solution.py:584
  147.7 14.6 %collective-permute-start.43 = (bf16[256,512]{1,0:T(8,128)(2,1)S(1)}, bf16[256,512]{1,0:T(8,128)(2,1)S(1)}, u32[]{:S(2)}, u32[]{:S(2)}) collective-permute-start(bf16[256,512]{1,0:T(8,128)(2,1)S(1)} %sum_near_up.1.keep), channel_id=1, source_target_pairs={{0,12},{4,8},{8,4},{12,0},{1,13},{5,9},{9,5},{13,1},{2,14},{6,10},... | collective-permute-start | bytes 786440 | tf_op jit(solution)/shard_map/ppermute | solution.py:584
  150.3 15.8 %collective-permute-start.33 = (bf16[256,512]{1,0:T(8,128)(2,1)S(1)}, bf16[256,512]{1,0:T(8,128)(2,1)S(1)}, u32[]{:S(2)}, u32[]{:S(2)}) collective-permute-start(bf16[256,512]{1,0:T(8,128)(2,1)S(1)} %sum_far_down.1.own), channel_id=1, source_target_pairs={{0,4},{4,0},{8,12},{12,8},{1,5},{5,1},{9,13},{13,9},{2,6},{6,2},{1... | collective-permute-start | bytes 786440 | tf_op jit(solution)/shard_map/ppermute | solution.py:584
  155.6 22.0 %collective-permute-start.34 = (bf16[512,512]{1,0:T(8,128)(2,1)S(1)}, bf16[512,512]{1,0:T(8,128)(2,1)S(1)}, u32[]{:S(2)}, u32[]{:S(2)}) collective-permute-start(bf16[512,512]{1,0:T(8,128)(2,1)S(1)} %get-tuple-element.147.p0), channel_id=1, source_target_pairs={{0,1},{1,0},{2,3},{3,2},{4,5},{5,4},{6,7},{7,6},{8,9},{9,8},{10,11... | collective-permute-start | bytes 1572872 | tf_op jit(solution)/shard_map/ppermute | solution.py:584
  159.8 17.7 %collective-permute-start.36 = (bf16[512,512]{1,0:T(8,128)(2,1)S(1)}, bf16[512,512]{1,0:T(8,128)(2,1)S(1)}, u32[]{:S(2)}, u32[]{:S(2)}) collective-permute-start(bf16[512,512]{1,0:T(8,128)(2,1)S(1)} %collective-permute-done.35.p2), channel_id=1, source_target_pairs={{0,1},{1,0},{2,3},{3,2},{4,5},{5,4},{6,7},{7,6},{8,9},{9,8},{10,11... | collective-permute-start | bytes 1572872 | tf_op jit(solution)/shard_map/ppermute | solution.py:584
  162.3 11.3 %collective-permute-start.39 = (bf16[1056,128]{1,0:T(8,128)(2,1)S(1)}, bf16[1056,128]{1,0:T(8,128)(2,1)S(1)}, u32[]{:S(2)}, u32[]{:S(2)}) collective-permute-start(bf16[1056,128]{1,0:T(8,128)(2,1)S(1)} %sum_near_late.1.keep), channel_id=1, source_target_pairs={{0,12},{4,8},{8,4},{12,0},{1,13},{5,9},{9,5},{13,1},{2,14},{6,10},... | collective-permute-start | bytes 811016 | tf_op jit(solution)/shard_map/ppermute | solution.py:584
  166.1 14.3 %collective-permute-start.44 = (bf16[256,512]{1,0:T(8,128)(2,1)S(1)}, bf16[256,512]{1,0:T(8,128)(2,1)S(1)}, u32[]{:S(2)}, u32[]{:S(2)}) collective-permute-start(bf16[256,512]{1,0:T(8,128)(2,1)S(1)} %sum_far_up.1.own), channel_id=1, source_target_pairs={{0,4},{4,0},{8,12},{12,8},{1,5},{5,1},{9,13},{13,9},{2,6},{6,2},{1... | collective-permute-start | bytes 786440 | tf_op jit(solution)/shard_map/ppermute | solution.py:584
  173.7 10.1 %collective-permute-start.40 = (bf16[1056,128]{1,0:T(8,128)(2,1)S(1)}, bf16[1056,128]{1,0:T(8,128)(2,1)S(1)}, u32[]{:S(2)}, u32[]{:S(2)}) collective-permute-start(bf16[1056,128]{1,0:T(8,128)(2,1)S(1)} %sum_far_late.1.own), channel_id=1, source_target_pairs={{0,4},{4,0},{8,12},{12,8},{1,5},{5,1},{9,13},{13,9},{2,6},{6,2},{1... | collective-permute-start | bytes 811016 | tf_op jit(solution)/shard_map/ppermute | solution.py:584
  180.4 5.0 %copy-start.1 = (bf16[2048,512]{1,0:T(8,128)(2,1)S(1)}, bf16[2048,512]{1,0:T(8,128)(2,1)}, u32[]{:S(2)}) copy-start(bf16[2048,512]{1,0:T(8,128)(2,1)} %param.10) | copy-start | bytes 6291460

commit v5 on v4

--- a/solution.py
+++ b/solution.py
@@ -237,7 +237,7 @@
     up_w, down_w = (u0, u1, u2, u3), (d0, d1, d2, d3)
     width = u0.shape[1]
 
-    @row_tiles(x.shape[0], 256)
+    @row_tiles(x.shape[0], 512)
     def _(rows):
         total = mid[rows, :]
         for r in range(4):
@@ -280,7 +280,7 @@
                 where[SECTION] == 1, own_g[rows, :], came[rows, :].astype(F32)
             )
 
-    @row_tiles(gy.shape[0], 256)
+    @row_tiles(gy.shape[0], 512)
     def _(rows):
         grad_mid[rows, :] = ffn_rows(rows, gy, slope, up_w, down_w, save)
 
@@ -309,9 +309,9 @@
 
     row_a = lax.broadcasted_iota(jnp.int32, (LANES, LANES), 0) < E
     spread = (row_a == first_head((LANES, LANES))).astype(BF16)
-    use_low = lax.broadcasted_iota(jnp.int32, (256, LANES), 1) % E >= E // 2
-
-    @row_tiles(total, 256)
+    use_low = lax.broadcasted_iota(jnp.int32, (512, LANES), 1) % E >= E // 2
+
+    @row_tiles(total, 512)
     def _(rows):
         grad_heads = nt(dattn[rows, :], out_w[...])
         scaled = grad_heads * inv_den[rows, :]

time: 189 us -> 187 us (0.989)
  no operation moved by 1% of the time
where the time goes in v5:
time: 187 us; the launch traced here: 184 us
  waiting for transfers between devices  78.6 us (42%)
  Pallas kernels  59.4 us (32%)
  starting transfers between devices  35.5 us (19%)
  local copies, waits for them, and re-layouts  4.71 us (3%)
  other arithmetic  3.79 us (2%)
  between operations  2.04 us (1%)
    ppermute x45, waiting for transfers between devices, across(): return lax.ppermute(block, axis, [(i, i ^ distance) for i in range(size)])  78.6 us
    pallas_call x28, Pallas kernels, call(): pl.pallas_call(kernel, out_shape=near, in_specs=[IN_SMEM if v.dtype == jn...  59.4 us
    ppermute x45, starting transfers between devices, across(): return lax.ppermute(block, axis, [(i, i ^ distance) for i in range(size)])  35.5 us
  transfers between devices with their start and end apart: 45, of which 19 were waited for; matrix products, arithmetic and copies ran while one was open for 4% of the time, Pallas kernels for 24%

profile of v5, /device:TPU:0, one launch (start us, length us, event | category | flops | bytes accessed | tf_op | source)
XLA Modules:
  0.0 184.0 jit_solution(7521159709778766779)
XLA Ops:
  0.7 3.0 %collective-permute-start.1 = (bf16[3,512,128]{2,1,0:T(8,128)(2,1)}, bf16[3,512,128]{2,1,0:T(8,128)(2,1)}, u32[]{:S(2)}, u32[]{:S(2)}) collective-permute-start(bf16[3,512,128]{2,1,0:T(8,128)(2,1)} %bitcast.58), channel_id=1, source_target_pairs={{0,2},{1,3},{2,0},{3,1},{4,6},{5,7},{6,4},{7,5},{8,10},{9,11},{10,... | collective-permute-start | bytes 1179656 | tf_op jit(solution)/shard_map/ppermute | solution.py:584
  3.8 1.9 %collective-permute-start.8 = (bf16[512,512]{1,0:T(8,128)(2,1)}, bf16[512,512]{1,0:T(8,128)(2,1)S(1)}, u32[]{:S(2)}, u32[]{:S(2)}) collective-permute-start(bf16[512,512]{1,0:T(8,128)(2,1)} %bitcast.38), channel_id=1, source_target_pairs={{0,2},{1,3},{2,0},{3,1},{4,6},{5,7},{6,4},{7,5},{8,10},{9,11},{10,... | collective-permute-start | bytes 1572872 | tf_op jit(solution)/shard_map/ppermute | solution.py:584
  5.7 1.2 reduce-window.6
  9.4 0.7 pad_add_fusion.1
  10.4 1.7 constant_dynamic-slice_fusion
  12.2 1.8 collective-permute-done.1.rest_5_
  13.9 0.8 dynamic-slice_convert_fusion
  14.7 0.7 compare_convert_fusion
  16.0 1.0 copy-done.5
  17.0 3.4 %qkv_first.1 = (bf16[512,512]{1,0:T(8,128)(2,1)S(1)}, bf16[512,512]{1,0:T(8,128)(2,1)S(1)}, bf16[512,512]{1,0:T(8,128)(2,1)S(1)}, bf16[4,128,256]{2,1,0:T(8,128)(2,1)S(1)}, bf16[3,512,512]{2,1,0:T(8,128)(2,1)S(1)}) custom-call(s32[3]{0:T(128)S(1)} %pad_add_fusion.where, bf16[512,512]{1,0:T(8,128)(2,1)S(1)} %constant_dynamic-slice_fusion.2.own.x, ...), custom_call_target="tpu_custom_call" | custom-call | flops 4400000000 | tf_op jit(solution)/shard_map/qkv_first/pallas_call | solution.py:566
  21.5 5.5 %collective-permute-done.8.w2.u2.rest_10_.rest_11_ = bf16[512,512]{1,0:T(8,128)(2,1)S(1)} collective-permute-done((bf16[512,512]{1,0:T(8,128)(2,1)}, bf16[512,512]{1,0:T(8,128)(2,1)S(1)}, u32[]{:S(2)}, u32[]{:S(2)}) %collective-permute-start.8) | collective-permute-done | bytes 524320 | tf_op jit(solution)/shard_map/ppermute | solution.py:584
  27.1 1.7 collective-permute-start.11
  29.3 3.3 %attention_first.1 = (f32[512,512]{1,0:T(8,128)S(1)}, bf16[512,512]{1,0:T(8,128)(2,1)S(1)}, bf16[512,512]{1,0:T(8,128)(2,1)S(1)}) custom-call(bf16[512,512]{1,0:T(8,128)(2,1)S(1)} %get-tuple-element.85.fq, bf16[512,512]{1,0:T(8,128)(2,1)S(1)} %get-tuple-element.86.fk, bf16[512,512]{1,0:T(8,128)(2,1)S(1)} %get-tuple-element.87.vv, ...), custom_call_target="tpu_custom_call" | custom-call | flops 6049999872 | tf_op jit(solution)/shard_map/attention_first/pallas_call | solution.py:566
  32.6 1.6 up_first.1.active
  34.3 5.9 %collective-permute-done.11.w2.d2.rest_14_.rest_15_ = bf16[512,512]{1,0:T(8,128)(2,1)S(1)} collective-permute-done((bf16[512,512]{1,0:T(8,128)(2,1)S(1)}, bf16[512,512]{1,0:T(8,128)(2,1)S(1)}, u32[]{:S(2)}, u32[]{:S(2)}) %collective-permute-start.11) | collective-permute-done | bytes 524320 | tf_op jit(solution)/shard_map/ppermute | solution.py:584
  40.2 1.9 %collective-permute-done.12.w3.d3.rest_15_.rest_16_ = bf16[512,512]{1,0:T(8,128)(2,1)S(1)} collective-permute-done((bf16[512,512]{1,0:T(8,128)(2,1)S(1)}, bf16[512,512]{1,0:T(8,128)(2,1)S(1)}, u32[]{:S(2)}, u32[]{:S(2)}) %collective-permute-start.12) | collective-permute-done | bytes 524320 | tf_op jit(solution)/shard_map/ppermute | solution.py:584
  42.1 1.3 down_first.1
  43.4 1.5 collective-permute-start.13
  44.9 12.5 %collective-permute-done.13.rest_0_ = bf16[512,512]{1,0:T(8,128)(2,1)S(1)} collective-permute-done((bf16[512,512]{1,0:T(8,128)(2,1)S(1)}, bf16[512,512]{1,0:T(8,128)(2,1)S(1)}, u32[]{:S(2)}, u32[]{:S(2)}) %collective-permute-start.13) | collective-permute-done | bytes 524320 | tf_op jit(solution)/shard_map/ppermute | solution.py:584
  57.4 2.4 %qkv_second.1 = (bf16[512,512]{1,0:T(8,128)(2,1)S(1)}, bf16[512,512]{1,0:T(8,128)(2,1)S(1)}, bf16[512,512]{1,0:T(8,128)(2,1)S(1)}, bf16[4,128,256]{2,1,0:T(8,128...) custom-call(s32[3]{0:T(128)S(1)} %pad_add_fusion.where, ...), custom_call_target="tpu_custom_call" | custom-call | flops 3849999872 | tf_op jit(solution)/shard_map/qkv_second/pallas_call | solution.py:566
  59.9 1.5 collective-permute-done.14.start
  61.4 6.0 %block_second.1 = (bf16[512,512]{1,0:T(8,128)(2,1)S(1)}, f32[512,512]{1,0:T(8,128)S(1)}, bf16[512,512]{1,0:T(8,128)(2,1)S(1)}, bf16[512,256]{1,0:T(8,128)(2,1)S(...) custom-call(bf16[512,512]{1,0:T(8,128)(2,1)S(1)} %get-tuple-element., ...), custom_call_target="tpu_custom_call" | custom-call | flops 11000000512 | tf_op jit(solution)/shard_map/block_second/pallas_call | solution.py:566
  67.4 4.4 %ffn_back_first.1 = (f32[512,512]{1,0:T(8,128)S(1)}, bf16[512,512]{1,0:T(8,128)(2,1)S(1)}, bf16[512,512]{1,0:T(8,128)(2,1)S(1)}, bf16[4,128,256]{2,1,0:T(8,128)(2,1)S(1)}) custom-call(s32[3]{0:T(128)S(1)} %pad_add_fusion.where, f32[512,512]{1,0:T(8,128)S(1)} %get-tuple-element.162.own_g, bf16[512,2048]{1,0:T(8,128)(2,1)S(1)} %get-tuple-element.102.rest_0_.rest_1_, ...), custom_call_target="tpu_custom_call" | custom-call | flops 4620000256 | tf_op jit(solution)/shard_map/ffn_back_first/pallas_call | solution.py:566
  72.0 1.4 collective-permute-start.15
  73.5 5.9 %attention_back_first.1 = bf16[512,512]{1,0:T(8,128)(2,1)S(1)} custom-call(bf16[512,512]{1,0:T(8,128)(2,1)S(1)} %get-tuple-element.95.fq.rest_4_.rest_5_, bf16[512,512]{1,0:T(8,128)(2,1)S(1)} %get-tuple-element.96.fk, bf16[512,512]{1,0:T(8,128)(2,1)S(1)} %get-tuple-element.97.vv, bf16[512,512]{1,0:T(8,128)(2,1)S(1)} %get-tuple-element.106.dnum, ...), custom_call_target="tpu_custom_call" | custom-call | flops 8249999872 | tf_op jit(solution)/shard_map/attention_back_first/pallas_call | solution.py:566
  79.4 1.6 collective-permute-start.18
  81.2 5.0 %collective-permute-done.15.p2 = bf16[512,512]{1,0:T(8,128)(2,1)S(1)} collective-permute-done((bf16[512,512]{1,0:T(8,128)(2,1)S(1)}, bf16[512,512]{1,0:T(8,128)(2,1)S(1)}, u32[]{:S(2)}, u32[]{:S(2)}) %collective-permute-start.15) | collective-permute-done | bytes 524320 | tf_op jit(solution)/shard_map/ppermute | solution.py:584
  86.2 3.4 %activations_most.1 = (f32[2048,512]{1,0:T(8,128)}, f32[16,128]{1,0:T(8,128)S(1)}) custom-call(s32[3]{0:T(128)S(1)} %pad_add_fusion.where, bf16[512,512]{1,0:T(8,128)(2,1)S(1)} %get-tuple-element.113.p0, bf16[512,512]{1,0:T(8,128)(2,1)S(1)} %collective-permute-done.19.p1, bf16[512,512]{1,0:T(8,128)(2,1)S(1)} %collective-permute-done.15.p2), custom_call_target="tpu_custom_call" | custom-call | flops 3080000000 | tf_op jit(solution)/shard_map/activations_most/pallas_call | solution.py:566
  89.7 4.1 %collective-permute-done.18.rest_0_.came = bf16[512,512]{1,0:T(8,128)(2,1)S(1)} collective-permute-done((bf16[512,512]{1,0:T(8,128)(2,1)S(1)}, bf16[512,512]{1,0:T(8,128)(2,1)S(1)}, u32[]{:S(2)}, u32[]{:S(2)}) %collective-permute-start.18) | collective-permute-done | bytes 524320 | tf_op jit(solution)/shard_map/ppermute | solution.py:584
  93.8 4.3 %ffn_back_second.1 = (f32[512,512]{1,0:T(8,128)S(1)}, bf16[512,512]{1,0:T(8,128)(2,1)S(1)}, bf16[512,512]{1,0:T(8,128)(2,1)S(1)}, bf16[4,128,256]{2,1,0:T(8,128)...) custom-call(s32[3]{0:T(128)S(1)} %pad_add_fusion.where, ...), custom_call_target="tpu_custom_call" | custom-call | flops 110000000 | tf_op jit(solution)/shard_map/ffn_back_second/pallas_call | solution.py:566
  98.8 2.1 %down_grad.1 = (bf16[512,512]{1,0:T(8,128)(2,1)S(1)}, bf16[512,512]{1,0:T(8,128)(2,1)S(1)}) custom-call(s32[3]{0:T(128)S(1)} %pad_add_fusion.where, f32[512,512]{1,0:T(8,128)S(1)} %get-tuple-element.162.own_g, f32[512,512]{1,0:T(8,128)S(1)} %get-tuple-element.161.other_g, bf16[512,512]{1,0:T(8,128)(2,1)S(1)} %collective-permute-done.18.rest_0_.came, ...), custom_call_target="tpu_custom_call" | custom-call | flops 48400000 | tf_op jit(solution)/shard_map/down_grad/pallas_call | solution.py:566
  100.9 1.1 collective-permute-start.22
  102.0 6.4 %attention_back_second.1 = (bf16[512,512]{1,0:T(8,128)(2,1)S(1)}, bf16[3,512,256]{2,1,0:T(8,128)(2,1)S(1)}, bf16[3,512,256]{2,1,0:T(8,128)(2,1)S(1)}, f32[8,512]{1,0:T(8,128)S(1)}) custom-call(bf16[512,512]{1,0:T(8,128)(2,1)S(1)} %get-tuple-element.95.fq.rest_4_.rest_5_, bf16[512,512]{1,0:T(8,128)(2,1)S(1)} %get-tuple-element.96.fk, ...), custom_call_target="tpu_custom_call" | custom-call | flops 165000000 | tf_op jit(solution)/shard_map/attention_back_second/pallas_call | solution.py:566
  109.1 6.1 %collective-permute-done.22.came = bf16[512,512]{1,0:T(8,128)(2,1)S(1)} collective-permute-done((bf16[512,512]{1,0:T(8,128)(2,1)S(1)}, bf16[512,512]{1,0:T(8,128)(2,1)S(1)}, u32[]{:S(2)}, u32[]{:S(2)}) %collective-permute-start.22) | collective-permute-done | bytes 524320 | tf_op jit(solution)/shard_map/ppermute | solution.py:584
  115.8 1.3 up_grad.1
  117.1 1.1 collective-permute-start.41
  118.2 1.2 collective-permute-done.30.sums_other
  119.3 1.3 late_grad.1
  120.6 1.1 collective-permute-start.37
  121.7 0.7 halve_down.1
  122.4 1.6 collective-permute-start.31
  124.0 1.0 collective-permute-start.35
  125.0 6.9 %collective-permute-done.41.came = bf16[512,512]{1,0:T(8,128)(2,1)S(1)} collective-permute-done((bf16[512,512]{1,0:T(8,128)(2,1)S(1)}, bf16[512,512]{1,0:T(8,128)(2,1)S(1)}, u32[]{:S(2)}, u32[]{:S(2)}) %collective-permute-start.41) | collective-permute-done | bytes 524320 | tf_op jit(solution)/shard_map/ppermute | solution.py:584
  131.9 0.7 halve_up.1
  132.6 1.6 collective-permute-start.42
  134.3 2.5 %collective-permute-start.32 = (bf16[256,512]{1,0:T(8,128)(2,1)S(1)}, bf16[256,512]{1,0:T(8,128)(2,1)S(1)}, u32[]{:S(2)}, u32[]{:S(2)}) collective-permute-start(bf16[256,512]{1,0:T(8,128)(2,1)S(1)} %sum_near_down.1.keep), channel_id=1, source_target_pairs={{0,12},{4,8},{8,4},{12,0},{1,13},{5,9},{9,5},{13,1},{2,14},{6,10},... | collective-permute-start | bytes 786440 | tf_op jit(solution)/shard_map/ppermute | solution.py:584
  136.8 6.7 %collective-permute-done.37.came = bf16[2112,128]{1,0:T(8,128)(2,1)S(1)} collective-permute-done((bf16[2112,128]{1,0:T(8,128)(2,1)S(1)}, bf16[2112,128]{1,0:T(8,128)(2,1)S(1)}, u32[]{:S(2)}, u32[]{:S(2)}) %collective-permute-start.37) | collective-permute-done | bytes 540704 | tf_op jit(solution)/shard_map/ppermute | solution.py:584
  143.5 0.7 halve_late.1
  144.2 1.6 collective-permute-start.38
  145.9 2.5 %collective-permute-start.43 = (bf16[256,512]{1,0:T(8,128)(2,1)S(1)}, bf16[256,512]{1,0:T(8,128)(2,1)S(1)}, u32[]{:S(2)}, u32[]{:S(2)}) collective-permute-start(bf16[256,512]{1,0:T(8,128)(2,1)S(1)} %sum_near_up.1.keep), channel_id=1, source_target_pairs={{0,12},{4,8},{8,4},{12,0},{1,13},{5,9},{9,5},{13,1},{2,14},{6,10},... | collective-permute-start | bytes 786440 | tf_op jit(solution)/shard_map/ppermute | solution.py:584
  148.5 0.7 collective-permute-start.33
  149.3 4.5 %collective-permute-done.35.p2 = bf16[512,512]{1,0:T(8,128)(2,1)S(1)} collective-permute-done((bf16[512,512]{1,0:T(8,128)(2,1)S(1)}, bf16[512,512]{1,0:T(8,128)(2,1)S(1)}, u32[]{:S(2)}, u32[]{:S(2)}) %collective-permute-start.35) | collective-permute-done | bytes 524320 | tf_op jit(solution)/shard_map/ppermute | solution.py:584
  153.8 4.3 %collective-permute-done.38.came = bf16[1056,128]{1,0:T(8,128)(2,1)S(1)} collective-permute-done((bf16[1056,128]{1,0:T(8,128)(2,1)S(1)}, bf16[1056,128]{1,0:T(8,128)(2,1)S(1)}, u32[]{:S(2)}, u32[]{:S(2)}) %collective-permute-start.38) | collective-permute-done | bytes 270368 | tf_op jit(solution)/shard_map/ppermute | solution.py:584
  158.1 2.4 %collective-permute-done.43.came = bf16[256,512]{1,0:T(8,128)(2,1)S(1)} collective-permute-done((bf16[256,512]{1,0:T(8,128)(2,1)S(1)}, bf16[256,512]{1,0:T(8,128)(2,1)S(1)}, u32[]{:S(2)}, u32[]{:S(2)}) %collective-permute-start.43) | collective-permute-done | bytes 262176 | tf_op jit(solution)/shard_map/ppermute | solution.py:584
  160.5 1.3 collective-permute-start.39
  161.9 2.4 %collective-permute-done.33.came = bf16[256,512]{1,0:T(8,128)(2,1)S(1)} collective-permute-done((bf16[256,512]{1,0:T(8,128)(2,1)S(1)}, bf16[256,512]{1,0:T(8,128)(2,1)S(1)}, u32[]{:S(2)}, u32[]{:S(2)}) %collective-permute-start.33) | collective-permute-done | bytes 262176 | tf_op jit(solution)/shard_map/ppermute | solution.py:584
  164.3 1.6 whole.2
  165.9 2.4 %activations_rest.1 = (f32[2048,512]{1,0:T(8,128)}, f32[16,128]{1,0:T(8,128)}) custom-call(s32[3]{0:T(128)S(1)} %pad_add_fusion.where, bf16[512,512]{1,0:T(8,128)(2,1)S(1)} %collective-permute-done.16.p3, f32[16,128]{1,0:T(8,128)S(1)} %get-tuple-element.145.rms_most, f32[2048,512]{1,0:T(8,128)} %get-tuple-element.114.most), custom_call_target="tpu_custom_call", output_to_operand_aliasing={{0}: (3, {})} | custom-call | flops 1100000000 | tf_op jit(solution)/shard_map/activations_rest/pallas_call | solution.py:566
  168.3 3.5 %collective-permute-done.39.came = bf16[1056,128]{1,0:T(8,128)(2,1)S(1)} collective-permute-done((bf16[1056,128]{1,0:T(8,128)(2,1)S(1)}, bf16[1056,128]{1,0:T(8,128)(2,1)S(1)}, u32[]{:S(2)}, u32[]{:S(2)}) %collective-permute-start.39) | collective-permute-done | bytes 270368 | tf_op jit(solution)/shard_map/ppermute | solution.py:584
  171.9 3.9 %collective-permute-start.40 = (bf16[1056,128]{1,0:T(8,128)(2,1)S(1)}, bf16[1056,128]{1,0:T(8,128)(2,1)S(1)}, u32[]{:S(2)}, u32[]{:S(2)}) collective-permute-start(bf16[1056,128]{1,0:T(8,128)(2,1)S(1)} %sum_far_late.1.own), channel_id=1, source_target_pairs={{0,4},{4,0},{8,12},{12,8},{1,5},{5,1},{9,13},{13,9},{2,6},{6,2},{1... | collective-permute-start | bytes 811016 | tf_op jit(solution)/shard_map/ppermute | solution.py:584
  175.7 2.8 %input_grad.1 = f32[2048,512]{1,0:T(8,128)} custom-call(s32[3]{0:T(128)S(1)} %pad_add_fusion.where, bf16[512,512]{1,0:T(8,128)(2,1)S(1)} %get-tuple-element.147.p0, bf16[512,512]{1,0:T(8,128)(2,1)S(1)} %collective-permute-done.34.p1, bf16[512,512]{1,0:T(8,128)(2,1)S(1)} %collective-permute-done.35.p2, bf16[512,512]{1,0:T(8,128)(2,1)S(1)} %collective-permute-done.36.p3), custom_call_target="tpu_custom_call" | custom-call | flops 3300000000 | tf_op jit(solution)/shard_map/input_grad/pallas_call | solution.py:566
  178.6 1.6 whole.3
  180.2 1.8 collective-permute-done.40.came
  182.0 1.6 join_late.1
  (93 shorter events, 7.4 us)
Async XLA Ops:
  0.6 8.1 %copy-start = (bf16[2048,512]{1,0:T(8,128)(2,1)S(1)}, bf16[2048,512]{1,0:T(8,128)(2,1)}, u32[]{:S(2)}) copy-start(bf16[2048,512]{1,0:T(8,128)(2,1)} %param.10) | copy-start | bytes 6291460
  0.7 15.4 %copy-start.4 = (f32[1,2,512]{2,1,0:T(2,128)S(1)}, f32[1,2,512]{2,1,0:T(2,128)}, u32[]{:S(2)}) copy-start(f32[1,2,512]{2,1,0:T(2,128)} %param.18) | copy-start | bytes 12292
  0.7 15.3 %copy-start.7 = (f32[1,2,512]{2,1,0:T(2,128)S(1)}, f32[1,2,512]{2,1,0:T(2,128)}, u32[]{:S(2)}) copy-start(f32[1,2,512]{2,1,0:T(2,128)} %param.19) | copy-start | bytes 12292
  0.7 13.3 %collective-permute-start.1 = (bf16[3,512,128]{2,1,0:T(8,128)(2,1)}, bf16[3,512,128]{2,1,0:T(8,128)(2,1)}, u32[]{:S(2)}, u32[]{:S(2)}) collective-permute-start(bf16[3,512,128]{2,1,0:T(8,128)(2,1)} %bitcast.58), channel_id=1, source_target_pairs={{0,2},{1,3},{2,0},{3,1},{4,6},{5,7},{6,4},{7,5},{8,10},{9,11},{10,... | collective-permute-start | bytes 1179656 | tf_op jit(solution)/shard_map/ppermute | solution.py:584
  3.7 12.0 %collective-permute-start = (bf16[3,512,128]{2,1,0:T(8,128)(2,1)}, bf16[3,512,128]{2,1,0:T(8,128)(2,1)}, u32[]{:S(2)}, u32[]{:S(2)}) collective-permute-start(bf16[3,512,128]{2,1,0:T(8,128)(2,1)} %bitcast.59), channel_id=1, source_target_pairs={{0,1},{1,0},{2,3},{3,2},{4,5},{5,4},{6,7},{7,6},{8,9},{9,8},{10,11... | collective-permute-start | bytes 1179656 | tf_op jit(solution)/shard_map/ppermute | solution.py:584
  3.7 17.3 %collective-permute-start.5 = (bf16[128,512]{1,0:T(8,128)(2,1)}, bf16[128,512]{1,0:T(8,128)(2,1)}, u32[]{:S(2)}, u32[]{:S(2)}) collective-permute-start(bf16[128,512]{1,0:T(8,128)(2,1)} %bitcast.61), channel_id=1, source_target_pairs={{0,2},{1,3},{2,0},{3,1},{4,6},{5,7},{6,4},{7,5},{8,10},{9,11},{10,... | collective-permute-start | bytes 393224 | tf_op jit(solution)/shard_map/ppermute | solution.py:584
  3.8 23.2 %collective-permute-start.8 = (bf16[512,512]{1,0:T(8,128)(2,1)}, bf16[512,512]{1,0:T(8,128)(2,1)S(1)}, u32[]{:S(2)}, u32[]{:S(2)}) collective-permute-start(bf16[512,512]{1,0:T(8,128)(2,1)} %bitcast.38), channel_id=1, source_target_pairs={{0,2},{1,3},{2,0},{3,1},{4,6},{5,7},{6,4},{7,5},{8,10},{9,11},{10,... | collective-permute-start | bytes 1572872 | tf_op jit(solution)/shard_map/ppermute | solution.py:584
  13.9 2.1 %collective-permute-start.2 = (bf16[3,512,128]{2,1,0:T(8,128)(2,1)}, bf16[3,512,128]{2,1,0:T(8,128)(2,1)}, u32[]{:S(2)}, u32[]{:S(2)}) collective-permute-start(bf16[3,512,128]{2,1,0:T(8,128)(2,1)} %collective-permute-done.1.rest_5_), channel_id=1, source_target_pairs={{0,1},{1,0},{2,3},{3,2},{4,5},{5,4},{6,7},{7,6},{8,9},{9,8},{10,11... | collective-permute-start | bytes 1179656 | tf_op jit(solution)/shard_map/ppermute | solution.py:584
  16.0 1.0 copy-start.5
  17.0 3.6 %copy-start.6 = (bf16[1,128,512]{2,1,0:T(8,128)(2,1)S(1)}, bf16[1,128,512]{2,1,0:T(8,128)(2,1)}, u32[]{:S(2)}) copy-start(bf16[1,128,512]{2,1,0:T(8,128)(2,1)} %param.15) | copy-start | bytes 393220
  17.0 4.2 %copy-start.2 = (bf16[1,512,512]{2,1,0:T(8,128)(2,1)S(1)}, bf16[1,512,512]{2,1,0:T(8,128)(2,1)}, u32[]{:S(2)}) copy-start(bf16[1,512,512]{2,1,0:T(8,128)(2,1)} %param.16) | copy-start | bytes 1572868
  17.0 10.0 %copy-start.3 = (bf16[1,512,512]{2,1,0:T(8,128)(2,1)S(1)}, bf16[1,512,512]{2,1,0:T(8,128)(2,1)}, u32[]{:S(2)}) copy-start(bf16[1,512,512]{2,1,0:T(8,128)(2,1)} %param.17) | copy-start | bytes 1572868
  20.4 8.9 %collective-permute-start.3 = (bf16[4,128,256]{2,1,0:T(8,128)(2,1)S(1)}, bf16[4,128,256]{2,1,0:T(8,128)(2,1)S(1)}, u32[]{:S(2)}, u32[]{:S(2)}) collective-permute-start(bf16[4,128,256]{2,1,0:T(8,128)(2,1)S(1)} %get-tuple-element.88), channel_id=1, source_target_pairs={{0,1},{1,0},{2,3},{3,2},{4,5},{5,4},{6,7},{7,6},{8,9},{9,8},{10,11... | collective-permute-start | bytes 786440 | tf_op jit(solution)/shard_map/ppermute | solution.py:584
  20.7 8.1 %collective-permute-start.4 = (bf16[128,512]{1,0:T(8,128)(2,1)S(1)}, bf16[128,512]{1,0:T(8,128)(2,1)S(1)}, u32[]{:S(2)}, u32[]{:S(2)}) collective-permute-start(bf16[128,512]{1,0:T(8,128)(2,1)S(1)} %bitcast.62), channel_id=1, source_target_pairs={{0,1},{1,0},{2,3},{3,2},{4,5},{5,4},{6,7},{7,6},{8,9},{9,8},{10,11... | collective-permute-start | bytes 393224 | tf_op jit(solution)/shard_map/ppermute | solution.py:584
  21.0 7.8 %collective-permute-start.6 = (bf16[128,512]{1,0:T(8,128)(2,1)}, bf16[128,512]{1,0:T(8,128)(2,1)S(1)}, u32[]{:S(2)}, u32[]{:S(2)}) collective-permute-start(bf16[128,512]{1,0:T(8,128)(2,1)} %collective-permute-done.5.w2), channel_id=1, source_target_pairs={{0,1},{1,0},{2,3},{3,2},{4,5},{5,4},{6,7},{7,6},{8,9},{9,8},{10,11... | collective-permute-start | bytes 393224 | tf_op jit(solution)/shard_map/ppermute | solution.py:584
  21.2 11.4 %collective-permute-start.7 = (bf16[512,512]{1,0:T(8,128)(2,1)S(1)}, bf16[512,512]{1,0:T(8,128)(2,1)S(1)}, u32[]{:S(2)}, u32[]{:S(2)}) collective-permute-start(bf16[512,512]{1,0:T(8,128)(2,1)S(1)} %bitcast.39), channel_id=1, source_target_pairs={{0,1},{1,0},{2,3},{3,2},{4,5},{5,4},{6,7},{7,6},{8,9},{9,8},{10,11... | collective-permute-start | bytes 1572872 | tf_op jit(solution)/shard_map/ppermute | solution.py:584
  27.1 13.1 %collective-permute-start.11 = (bf16[512,512]{1,0:T(8,128)(2,1)S(1)}, bf16[512,512]{1,0:T(8,128)(2,1)S(1)}, u32[]{:S(2)}, u32[]{:S(2)}) collective-permute-start(bf16[512,512]{1,0:T(8,128)(2,1)S(1)} %bitcast.44), channel_id=1, source_target_pairs={{0,2},{1,3},{2,0},{3,1},{4,6},{5,7},{6,4},{7,5},{8,10},{9,11},{10,... | collective-permute-start | bytes 1572872 | tf_op jit(solution)/shard_map/ppermute | solution.py:584
  28.8 11.4 %collective-permute-start.10 = (bf16[512,512]{1,0:T(8,128)(2,1)S(1)}, bf16[512,512]{1,0:T(8,128)(2,1)S(1)}, u32[]{:S(2)}, u32[]{:S(2)}) collective-permute-start(bf16[512,512]{1,0:T(8,128)(2,1)S(1)} %bitcast.45), channel_id=1, source_target_pairs={{0,1},{1,0},{2,3},{3,2},{4,5},{5,4},{6,7},{7,6},{8,9},{9,8},{10,11... | collective-permute-start | bytes 1572872 | tf_op jit(solution)/shard_map/ppermute | solution.py:584
  28.8 3.8 %collective-permute-start.9 = (bf16[512,512]{1,0:T(8,128)(2,1)S(1)}, bf16[512,512]{1,0:T(8,128)(2,1)S(1)}, u32[]{:S(2)}, u32[]{:S(2)}) collective-permute-start(bf16[512,512]{1,0:T(8,128)(2,1)S(1)} %collective-permute-done.8.w2.u2.rest_10_.rest_11_), channel_id=1, source_target_pairs={{0,1},{1,0},{2,3},{3,2},{4,5},{5,4},{6,7},{7,6},{8,9},{9,8},{10,11... | collective-permute-start | bytes 1572872 | tf_op jit(solution)/shard_map/ppermute | solution.py:584
  40.2 1.9 %collective-permute-start.12 = (bf16[512,512]{1,0:T(8,128)(2,1)S(1)}, bf16[512,512]{1,0:T(8,128)(2,1)S(1)}, u32[]{:S(2)}, u32[]{:S(2)}) collective-permute-start(bf16[512,512]{1,0:T(8,128)(2,1)S(1)} %collective-permute-done.11.w2.d2.rest_14_.rest_15_), channel_id=1, source_target_pairs={{0,1},{1,0},{2,3},{3,2},{4,5},{5,4},{6,7},{7,6},{8,9},{9,8},{10,11... | collective-permute-start | bytes 1572872 | tf_op jit(solution)/shard_map/ppermute | solution.py:584
  43.4 14.0 %collective-permute-start.13 = (bf16[512,512]{1,0:T(8,128)(2,1)S(1)}, bf16[512,512]{1,0:T(8,128)(2,1)S(1)}, u32[]{:S(2)}, u32[]{:S(2)}) collective-permute-start(bf16[512,512]{1,0:T(8,128)(2,1)S(1)} %down_first.1), channel_id=1, source_target_pairs={{0,16},{16,0},{1,17},{17,1},{2,18},{18,2},{3,19},{19,3},{4,20},{20... | collective-permute-start | bytes 1572872 | tf_op jit(solution)/shard_map/ppermute | solution.py:584
  59.8 1.6 collective-permute-start.14
  71.8 1.7 collective-permute-start.17
  72.0 14.2 %collective-permute-start.15 = (bf16[512,512]{1,0:T(8,128)(2,1)S(1)}, bf16[512,512]{1,0:T(8,128)(2,1)S(1)}, u32[]{:S(2)}, u32[]{:S(2)}) collective-permute-start(bf16[512,512]{1,0:T(8,128)(2,1)S(1)} %get-tuple-element.113.p0), channel_id=1, source_target_pairs={{0,2},{1,3},{2,0},{3,1},{4,6},{5,7},{6,4},{7,5},{8,10},{9,11},{10,... | collective-permute-start | bytes 1572872 | tf_op jit(solution)/shard_map/ppermute | solution.py:584
  73.5 12.8 %collective-permute-start.19 = (bf16[512,512]{1,0:T(8,128)(2,1)S(1)}, bf16[512,512]{1,0:T(8,128)(2,1)S(1)}, u32[]{:S(2)}, u32[]{:S(2)}) collective-permute-start(bf16[512,512]{1,0:T(8,128)(2,1)S(1)} %get-tuple-element.113.p0), channel_id=1, source_target_pairs={{0,1},{1,0},{2,3},{3,2},{4,5},{5,4},{6,7},{7,6},{8,9},{9,8},{10,11... | collective-permute-start | bytes 1572872 | tf_op jit(solution)/shard_map/ppermute | solution.py:584
  79.4 14.3 %collective-permute-start.18 = (bf16[512,512]{1,0:T(8,128)(2,1)S(1)}, bf16[512,512]{1,0:T(8,128)(2,1)S(1)}, u32[]{:S(2)}, u32[]{:S(2)}) collective-permute-start(bf16[512,512]{1,0:T(8,128)(2,1)S(1)} %attention_back_first.1), channel_id=1, source_target_pairs={{0,16},{16,0},{1,17},{17,1},{2,18},{18,2},{3,19},{19,3},{4,20},{20... | collective-permute-start | bytes 1572872 | tf_op jit(solution)/shard_map/ppermute | solution.py:584
  81.0 17.8 %collective-permute-start.21 = (bf16[512,1024]{1,0:T(8,128)(2,1)S(1)}, bf16[512,1024]{1,0:T(8,128)(2,1)S(1)}, u32[]{:S(2)}, u32[]{:S(2)}) collective-permute-start(bf16[512,1024]{1,0:T(8,128)(2,1)S(1)} %get-tuple-element.119), channel_id=1, source_target_pairs={{0,1},{1,0},{2,3},{3,2},{4,5},{5,4},{6,7},{7,6},{8,9},{9,8},{10,11... | collective-permute-start | bytes 3145736 | tf_op jit(solution)/shard_map/ppermute | solution.py:584
  93.8 5.0 %collective-permute-start.20 = (bf16[512,512]{1,0:T(8,128)(2,1)S(1)}, bf16[512,512]{1,0:T(8,128)(2,1)S(1)}, u32[]{:S(2)}, u32[]{:S(2)}) collective-permute-start(bf16[512,512]{1,0:T(8,128)(2,1)S(1)} %collective-permute-done.18.rest_0_.came), channel_id=1, source_target_pairs={{0,1},{1,0},{2,3},{3,2},{4,5},{5,4},{6,7},{7,6},{8,9},{9,8},{10,11... | collective-permute-start | bytes 1572872 | tf_op jit(solution)/shard_map/ppermute | solution.py:584
  98.1 17.1 %collective-permute-start.27 = (bf16[512,1024]{1,0:T(8,128)(2,1)S(1)}, bf16[512,1024]{1,0:T(8,128)(2,1)S(1)}, u32[]{:S(2)}, u32[]{:S(2)}) collective-permute-start(bf16[512,1024]{1,0:T(8,128)(2,1)S(1)} %get-tuple-element.132), channel_id=1, source_target_pairs={{0,1},{1,0},{2,3},{3,2},{4,5},{5,4},{6,7},{7,6},{8,9},{9,8},{10,11... | collective-permute-start | bytes 3145736 | tf_op jit(solution)/shard_map/ppermute | solution.py:584
  98.7 3.3 %collective-permute-start.24 = (bf16[4,128,256]{2,1,0:T(8,128)(2,1)S(1)}, bf16[4,128,256]{2,1,0:T(8,128)(2,1)S(1)}, u32[]{:S(2)}, u32[]{:S(2)}) collective-permute-start(bf16[4,128,256]{2,1,0:T(8,128)(2,1)S(1)} %get-tuple-element.116), channel_id=1, source_target_pairs={{0,1},{1,0},{2,3},{3,2},{4,5},{5,4},{6,7},{7,6},{8,9},{9,8},{10,11... | collective-permute-start | bytes 786440 | tf_op jit(solution)/shard_map/ppermute | solution.py:584
  100.9 14.3 %collective-permute-start.22 = (bf16[512,512]{1,0:T(8,128)(2,1)S(1)}, bf16[512,512]{1,0:T(8,128)(2,1)S(1)}, u32[]{:S(2)}, u32[]{:S(2)}) collective-permute-start(bf16[512,512]{1,0:T(8,128)(2,1)S(1)} %get-tuple-element.121), channel_id=1, source_target_pairs={{0,2},{1,3},{2,0},{3,1},{4,6},{5,7},{6,4},{7,5},{8,10},{9,11},{10,... | collective-permute-start | bytes 1572872 | tf_op jit(solution)/shard_map/ppermute | solution.py:584
  108.4 9.7 %collective-permute-start.25 = (bf16[3,512,256]{2,1,0:T(8,128)(2,1)S(1)}, bf16[3,512,256]{2,1,0:T(8,128)(2,1)S(1)}, u32[]{:S(2)}, u32[]{:S(2)}) collective-permute-start(bf16[3,512,256]{2,1,0:T(8,128)(2,1)S(1)} %get-tuple-element.129), channel_id=1, source_target_pairs={{0,1},{1,0},{2,3},{3,2},{4,5},{5,4},{6,7},{7,6},{8,9},{9,8},{10,11... | collective-permute-start | bytes 2359304 | tf_op jit(solution)/shard_map/ppermute | solution.py:584
  108.6 7.2 %collective-permute-start.26 = (bf16[512,512]{1,0:T(8,128)(2,1)S(1)}, bf16[512,512]{1,0:T(8,128)(2,1)S(1)}, u32[]{:S(2)}, u32[]{:S(2)}) collective-permute-start(bf16[512,512]{1,0:T(8,128)(2,1)S(1)} %get-tuple-element.130.normed_own), channel_id=1, source_target_pairs={{0,1},{1,0},{2,3},{3,2},{4,5},{5,4},{6,7},{7,6},{8,9},{9,8},{10,11... | collective-permute-start | bytes 1572872 | tf_op jit(solution)/shard_map/ppermute | solution.py:584
  109.0 9.2 %collective-permute-start.23 = (bf16[512,512]{1,0:T(8,128)(2,1)S(1)}, bf16[512,512]{1,0:T(8,128)(2,1)S(1)}, u32[]{:S(2)}, u32[]{:S(2)}) collective-permute-start(bf16[512,512]{1,0:T(8,128)(2,1)S(1)} %get-tuple-element.122.normed_own), channel_id=1, source_target_pairs={{0,1},{1,0},{2,3},{3,2},{4,5},{5,4},{6,7},{7,6},{8,9},{9,8},{10,11... | collective-permute-start | bytes 1572872 | tf_op jit(solution)/shard_map/ppermute | solution.py:584
  115.2 2.9 %collective-permute-start.29 = (bf16[512,512]{1,0:T(8,128)(2,1)S(1)}, bf16[512,512]{1,0:T(8,128)(2,1)S(1)}, u32[]{:S(2)}, u32[]{:S(2)}) collective-permute-start(bf16[512,512]{1,0:T(8,128)(2,1)S(1)} %get-tuple-element.138.dattn_own), channel_id=1, source_target_pairs={{0,1},{1,0},{2,3},{3,2},{4,5},{5,4},{6,7},{7,6},{8,9},{9,8},{10,11... | collective-permute-start | bytes 1572872 | tf_op jit(solution)/shard_map/ppermute | solution.py:584
  115.3 2.9 %collective-permute-start.28 = (bf16[512,256]{1,0:T(8,128)(2,1)S(1)}, bf16[512,256]{1,0:T(8,128)(2,1)S(1)}, u32[]{:S(2)}, u32[]{:S(2)}) collective-permute-start(bf16[512,256]{1,0:T(8,128)(2,1)S(1)} %get-tuple-element.137), channel_id=1, source_target_pairs={{0,1},{1,0},{2,3},{3,2},{4,5},{5,4},{6,7},{7,6},{8,9},{9,8},{10,11... | collective-permute-start | bytes 786440 | tf_op jit(solution)/shard_map/ppermute | solution.py:584
  117.1 14.9 %collective-permute-start.41 = (bf16[512,512]{1,0:T(8,128)(2,1)S(1)}, bf16[512,512]{1,0:T(8,128)(2,1)S(1)}, u32[]{:S(2)}, u32[]{:S(2)}) collective-permute-start(bf16[512,512]{1,0:T(8,128)(2,1)S(1)} %get-tuple-element.135), channel_id=1, source_target_pairs={{0,2},{1,3},{2,0},{3,1},{4,6},{5,7},{6,4},{7,5},{8,10},{9,11},{10,... | collective-permute-start | bytes 1572872 | tf_op jit(solution)/shard_map/ppermute | solution.py:584
  118.1 1.2 collective-permute-start.30
  120.6 22.9 %collective-permute-start.37 = (bf16[2112,128]{1,0:T(8,128)(2,1)S(1)}, bf16[2112,128]{1,0:T(8,128)(2,1)S(1)}, u32[]{:S(2)}, u32[]{:S(2)}) collective-permute-start(bf16[2112,128]{1,0:T(8,128)(2,1)S(1)} %get-tuple-element.140), channel_id=1, source_target_pairs={{0,2},{1,3},{2,0},{3,1},{4,6},{5,7},{6,4},{7,5},{8,10},{9,11},{10,... | collective-permute-start | bytes 1622024 | tf_op jit(solution)/shard_map/ppermute | solution.py:584
  122.4 11.9 %collective-permute-start.31 = (bf16[256,512]{1,0:T(8,128)(2,1)S(1)}, bf16[256,512]{1,0:T(8,128)(2,1)S(1)}, u32[]{:S(2)}, u32[]{:S(2)}) collective-permute-start(bf16[256,512]{1,0:T(8,128)(2,1)S(1)} %get-tuple-element.143), channel_id=1, source_target_pairs={{0,4},{4,0},{8,12},{12,8},{1,5},{5,1},{9,13},{13,9},{2,6},{6,2},{1... | collective-permute-start | bytes 786440 | tf_op jit(solution)/shard_map/ppermute | solution.py:584
  124.0 29.8 %collective-permute-start.35 = (bf16[512,512]{1,0:T(8,128)(2,1)S(1)}, bf16[512,512]{1,0:T(8,128)(2,1)S(1)}, u32[]{:S(2)}, u32[]{:S(2)}) collective-permute-start(bf16[512,512]{1,0:T(8,128)(2,1)S(1)} %get-tuple-element.147.p0), channel_id=1, source_target_pairs={{0,2},{1,3},{2,0},{3,1},{4,6},{5,7},{6,4},{7,5},{8,10},{9,11},{10,... | collective-permute-start | bytes 1572872 | tf_op jit(solution)/shard_map/ppermute | solution.py:584
  132.6 13.2 %collective-permute-start.42 = (bf16[256,512]{1,0:T(8,128)(2,1)S(1)}, bf16[256,512]{1,0:T(8,128)(2,1)S(1)}, u32[]{:S(2)}, u32[]{:S(2)}) collective-permute-start(bf16[256,512]{1,0:T(8,128)(2,1)S(1)} %get-tuple-element.156), channel_id=1, source_target_pairs={{0,4},{4,0},{8,12},{12,8},{1,5},{5,1},{9,13},{13,9},{2,6},{6,2},{1... | collective-permute-start | bytes 786440 | tf_op jit(solution)/shard_map/ppermute | solution.py:584
  134.3 14.2 %collective-permute-start.32 = (bf16[256,512]{1,0:T(8,128)(2,1)S(1)}, bf16[256,512]{1,0:T(8,128)(2,1)S(1)}, u32[]{:S(2)}, u32[]{:S(2)}) collective-permute-start(bf16[256,512]{1,0:T(8,128)(2,1)S(1)} %sum_near_down.1.keep), channel_id=1, source_target_pairs={{0,12},{4,8},{8,4},{12,0},{1,13},{5,9},{9,5},{13,1},{2,14},{6,10},... | collective-permute-start | bytes 786440 | tf_op jit(solution)/shard_map/ppermute | solution.py:584
  144.2 13.9 %collective-permute-start.38 = (bf16[1056,128]{1,0:T(8,128)(2,1)S(1)}, bf16[1056,128]{1,0:T(8,128)(2,1)S(1)}, u32[]{:S(2)}, u32[]{:S(2)}) collective-permute-start(bf16[1056,128]{1,0:T(8,128)(2,1)S(1)} %get-tuple-element.151), channel_id=1, source_target_pairs={{0,4},{4,0},{8,12},{12,8},{1,5},{5,1},{9,13},{13,9},{2,6},{6,2},{1... | collective-permute-start | bytes 811016 | tf_op jit(solution)/shard_map/ppermute | solution.py:584
  145.8 20.1 %collective-permute-start.16 = (bf16[512,512]{1,0:T(8,128)(2,1)S(1)}, bf16[512,512]{1,0:T(8,128)(2,1)S(1)}, u32[]{:S(2)}, u32[]{:S(2)}) collective-permute-start(bf16[512,512]{1,0:T(8,128)(2,1)S(1)} %collective-permute-done.15.p2), channel_id=1, source_target_pairs={{0,1},{1,0},{2,3},{3,2},{4,5},{5,4},{6,7},{7,6},{8,9},{9,8},{10,11... | collective-permute-start | bytes 1572872 | tf_op jit(solution)/shard_map/ppermute | solution.py:584
  145.9 14.6 %collective-permute-start.43 = (bf16[256,512]{1,0:T(8,128)(2,1)S(1)}, bf16[256,512]{1,0:T(8,128)(2,1)S(1)}, u32[]{:S(2)}, u32[]{:S(2)}) collective-permute-start(bf16[256,512]{1,0:T(8,128)(2,1)S(1)} %sum_near_up.1.keep), channel_id=1, source_target_pairs={{0,12},{4,8},{8,4},{12,0},{1,13},{5,9},{9,5},{13,1},{2,14},{6,10},... | collective-permute-start | bytes 786440 | tf_op jit(solution)/shard_map/ppermute | solution.py:584
  148.5 15.8 %collective-permute-start.33 = (bf16[256,512]{1,0:T(8,128)(2,1)S(1)}, bf16[256,512]{1,0:T(8,128)(2,1)S(1)}, u32[]{:S(2)}, u32[]{:S(2)}) collective-permute-start(bf16[256,512]{1,0:T(8,128)(2,1)S(1)} %sum_far_down.1.own), channel_id=1, source_target_pairs={{0,4},{4,0},{8,12},{12,8},{1,5},{5,1},{9,13},{13,9},{2,6},{6,2},{1... | collective-permute-start | bytes 786440 | tf_op jit(solution)/shard_map/ppermute | solution.py:584
  153.8 22.0 %collective-permute-start.34 = (bf16[512,512]{1,0:T(8,128)(2,1)S(1)}, bf16[512,512]{1,0:T(8,128)(2,1)S(1)}, u32[]{:S(2)}, u32[]{:S(2)}) collective-permute-start(bf16[512,512]{1,0:T(8,128)(2,1)S(1)} %get-tuple-element.147.p0), channel_id=1, source_target_pairs={{0,1},{1,0},{2,3},{3,2},{4,5},{5,4},{6,7},{7,6},{8,9},{9,8},{10,11... | collective-permute-start | bytes 1572872 | tf_op jit(solution)/shard_map/ppermute | solution.py:584
  158.1 17.7 %collective-permute-start.36 = (bf16[512,512]{1,0:T(8,128)(2,1)S(1)}, bf16[512,512]{1,0:T(8,128)(2,1)S(1)}, u32[]{:S(2)}, u32[]{:S(2)}) collective-permute-start(bf16[512,512]{1,0:T(8,128)(2,1)S(1)} %collective-permute-done.35.p2), channel_id=1, source_target_pairs={{0,1},{1,0},{2,3},{3,2},{4,5},{5,4},{6,7},{7,6},{8,9},{9,8},{10,11... | collective-permute-start | bytes 1572872 | tf_op jit(solution)/shard_map/ppermute | solution.py:584
  160.5 11.3 %collective-permute-start.39 = (bf16[1056,128]{1,0:T(8,128)(2,1)S(1)}, bf16[1056,128]{1,0:T(8,128)(2,1)S(1)}, u32[]{:S(2)}, u32[]{:S(2)}) collective-permute-start(bf16[1056,128]{1,0:T(8,128)(2,1)S(1)} %sum_near_late.1.keep), channel_id=1, source_target_pairs={{0,12},{4,8},{8,4},{12,0},{1,13},{5,9},{9,5},{13,1},{2,14},{6,10},... | collective-permute-start | bytes 811016 | tf_op jit(solution)/shard_map/ppermute | solution.py:584
  164.3 14.3 %collective-permute-start.44 = (bf16[256,512]{1,0:T(8,128)(2,1)S(1)}, bf16[256,512]{1,0:T(8,128)(2,1)S(1)}, u32[]{:S(2)}, u32[]{:S(2)}) collective-permute-start(bf16[256,512]{1,0:T(8,128)(2,1)S(1)} %sum_far_up.1.own), channel_id=1, source_target_pairs={{0,4},{4,0},{8,12},{12,8},{1,5},{5,1},{9,13},{13,9},{2,6},{6,2},{1... | collective-permute-start | bytes 786440 | tf_op jit(solution)/shard_map/ppermute | solution.py:584
  171.9 10.1 %collective-permute-start.40 = (bf16[1056,128]{1,0:T(8,128)(2,1)S(1)}, bf16[1056,128]{1,0:T(8,128)(2,1)S(1)}, u32[]{:S(2)}, u32[]{:S(2)}) collective-permute-start(bf16[1056,128]{1,0:T(8,128)(2,1)S(1)} %sum_far_late.1.own), channel_id=1, source_target_pairs={{0,4},{4,0},{8,12},{12,8},{1,5},{5,1},{9,13},{13,9},{2,6},{6,2},{1... | collective-permute-start | bytes 811016 | tf_op jit(solution)/shard_map/ppermute | solution.py:584
  178.6 5.0 %copy-start.1 = (bf16[2048,512]{1,0:T(8,128)(2,1)S(1)}, bf16[2048,512]{1,0:T(8,128)(2,1)}, u32[]{:S(2)}) copy-start(bf16[2048,512]{1,0:T(8,128)(2,1)} %param.10) | copy-start | bytes 6291460
